TPU v7x, 32 devices: a whole 2x2x4 slice. The times are simulated.
32 devices in a mesh: groups: 2 (over y), dp: 16 (over z, x, core).
Axes of the slice: x: 2, y: 2, z: 4, core: 2. Of those that a mesh axis runs over, the one named last changes fastest.
Arguments:
- queries: bfloat16 [32, 128, 8192], P(('groups', 'dp')), parts along dimension 0, may hold values from -30 to 30
- fresh_kv: bfloat16 [32, 128, 2, 512], P(('groups', 'dp')), parts along dimension 0, may hold values from -13 to 13
- kv_pool: bfloat16 [4096, 2, 8, 512], P(('groups', 'dp')), parts along dimension 0, may hold values from -6 to 6
- page_holder: int32 [32, 128], P(('groups', 'dp')), parts along dimension 0, may hold values from 0 to 15, as said below
- page_slot: int32 [32, 128], P(('groups', 'dp')), parts along dimension 0, may hold values from 0 to 127, as said below
- cached_len: int32 [32], P(('groups', 'dp')), parts along dimension 0, may hold values from 768 to 1024, as said below
- fresh_len: int32 [32], P(('groups', 'dp')), parts along dimension 0, may hold values from 64 to 128, as said below
Outputs:
- attended: bfloat16 [32, 128, 8192], P(('groups', 'dp')), parts along dimension 0
There are 2 independent parts, one for each index of `groups`. A program takes and returns all parts, laid end to end along the dimension named above; each array names one. Nothing has to cross between parts.
Inputs may be any that keep to these rules, and one draw needn't show every extreme that they name: `page_holder`: each pool device holds exactly 8 of the 128 pages of every trajectory; for one page index j no two trajectories have the same holder. `page_slot`: no two pages of the group share a (holder, slot) pair, so every slot of every pool is used. `cached_len`: some trajectory has the most. `fresh_len`: some trajectory has the most.
All inputs are finite; a program needn't handle non-finite values.
Results may differ from a plain program's by a relative error of at most 0.0031.
Values may be sent and summed in bfloat16 or wider, within the bound.
No kernel may reach another device: no remote copies, remote signals or barrier semaphores. Data moves between devices by JAX's collectives and lax.ppermute only.
A program may use at most 128 MiB of HBM per device.

v0:
```python
import jax
import jax.numpy as jnp
from jax import lax
from jax.sharding import PartitionSpec as P

H = 64
KVH = 4
HD = 128
PAGE = 8
MP = 128
C = 128


def local(queries, fresh_kv, kv_pool, page_holder, page_slot, cached_len, fresh_len):
    devices = lax.axis_size("dp")
    myself = lax.axis_index("dp")
    capacity = MP // devices
    group_size = H // KVH
    kv_width = KVH * HD
    inv_root = HD ** (-0.5)
    own_holder = page_holder[0]
    index_j = jnp.arange(MP, dtype=jnp.int32)
    same_holder = own_holder[:, None] == own_holder[None, :]
    earlier = index_j[None, :] < index_j[:, None]
    rank_seen = jnp.sum(same_holder & earlier, axis=1)
    arrival = own_holder * capacity + rank_seen
    hit_table = arrival[:, None] == index_j[None, :]
    all_holder, all_slot = (
        lax.all_gather(page_holder, "dp", axis=0, tiled=True),
        lax.all_gather(page_slot, "dp", axis=0, tiled=True),
    )
    mine_mask = all_holder == myself
    order_seen = jnp.cumsum(mine_mask.astype(jnp.int32), axis=1) - 1
    places = jnp.arange(capacity, dtype=jnp.int32)
    picked = mine_mask[:, :, None] & (order_seen[:, :, None] == places[None, None, :])
    outgoing = jnp.sum(jnp.where(picked, all_slot[:, :, None], 0), axis=1).reshape(MP)
    sending = jnp.take(kv_pool, outgoing, axis=0)
    received = lax.all_to_all(sending, "dp", split_axis=0, concat_axis=0, tiled=True)
    length = cached_len[0]
    filled = fresh_len[0]
    query_all = queries[0].reshape(C, KVH, group_size, HD)
    fresh_keys = fresh_kv[0, :, 0]
    fresh_values = fresh_kv[0, :, 1]
    row_ids = jnp.arange(C, dtype=jnp.int32)
    causal = row_ids[None, :] <= row_ids[:, None]
    position_page = jnp.sum(jnp.where(hit_table, index_j[:, None], 0), axis=0)
    token_place = (
        position_page[:, None] * PAGE + jnp.arange(PAGE, dtype=jnp.int32)[None, :]
    ).reshape(MP * PAGE)
    cache_live = token_place < length
    cache_keys = received[:, 0].reshape(MP * PAGE, kv_width)
    cache_values = received[:, 1].reshape(MP * PAGE, kv_width)
    fresh_allowed = jnp.repeat(causal, group_size, axis=0)
    outputs = []
    for kv_head in range(KVH):
        low_col = kv_head * HD
        query_rows = query_all[:, kv_head].reshape(C * group_size, HD)
        cache_scores = (
            jnp.einsum(
                "rd,nd->rn",
                query_rows,
                cache_keys[:, low_col : low_col + HD],
                preferred_element_type=jnp.float32,
            )
            * inv_root
        )
        fresh_scores = (
            jnp.einsum(
                "rd,nd->rn",
                query_rows,
                fresh_keys[:, low_col : low_col + HD],
                preferred_element_type=jnp.float32,
            )
            * inv_root
        )
        cache_scores = jnp.where(cache_live[None, :], cache_scores, -jnp.inf)
        fresh_scores = jnp.where(fresh_allowed, fresh_scores, -jnp.inf)
        top_score = jnp.maximum(
            jnp.max(cache_scores, axis=1, keepdims=True),
            jnp.max(fresh_scores, axis=1, keepdims=True),
        )
        cache_weights = jnp.exp(cache_scores - top_score)
        fresh_weights = jnp.exp(fresh_scores - top_score)
        weight_sum = jnp.sum(cache_weights, axis=1, keepdims=True) + jnp.sum(
            fresh_weights, axis=1, keepdims=True
        )
        mixed_out = jnp.dot(
            cache_weights.astype(jnp.bfloat16),
            cache_values[:, low_col : low_col + HD],
            preferred_element_type=jnp.float32,
        )
        mixed_out = mixed_out + jnp.dot(
            fresh_weights.astype(jnp.bfloat16),
            fresh_values[:, low_col : low_col + HD],
            preferred_element_type=jnp.float32,
        )
        outputs.append((mixed_out / weight_sum).reshape(C, group_size, HD))
    result = jnp.stack(outputs, axis=1)
    result = jnp.where((row_ids < filled)[:, None, None, None], result, 0.0)
    return result.reshape(1, C, H * HD).astype(jnp.bfloat16)


def solution(mesh):
    return jax.shard_map(
        local,
        mesh=mesh,
        in_specs=(
            P(("groups", "dp"), None, None),
            P(("groups", "dp"), None, None, None),
            P(("groups", "dp"), None, None, None),
            P(("groups", "dp"), None),
            P(("groups", "dp"), None),
            P(("groups", "dp")),
            P(("groups", "dp")),
        ),
        out_specs=P(("groups", "dp"), None, None),
        check_vma=False,
    )
```

profile of v0, /device:TPU:11, one launch (start us, length us, event | category | flops | bytes accessed | tf_op | source)
XLA Modules:
  0.0 149.6 jit_solution(6619789340341138718)
XLA Ops:
  0.0 15.8 %all-gather = s32[16,1,128]{2,1,0:T(1,128)S(1)} all-gather(s32[1,1,128]{2,1,0:T(1,128)} %bitcast.64), channel_id=1, replica_groups=mesh['groups'=2,'dp'=16] {'dp'}, dimensions={0}, use_global_device_ids=true | all-gather | bytes 8704 | tf_op jit(solution)/shard_map/all_gather | solution.py:29
  15.8 0.3 reduce_window_sum.11
  16.1 21.3 %all-gather.1 = s32[16,1,128]{2,1,0:T(1,128)S(1)} all-gather(s32[1,1,128]{2,1,0:T(1,128)} %bitcast.63), channel_id=1, replica_groups=mesh['groups'=2,'dp'=16] {'dp'}, dimensions={0}, use_global_device_ids=true | all-gather | bytes 8704 | tf_op jit(solution)/shard_map/all_gather | solution.py:30
  37.4 0.3 select_reduce_fusion
  37.7 0.1 reshape.175
  37.8 0.1 reshape.174
  38.0 2.0 %gather_fusion = bf16[128,2,8,512]{3,2,1,0:T(8,128)(2,1)} fusion(bf16[128,2,8,512]{3,2,1,0:T(8,128)(2,1)S(1)} %copy-done, s32[1024]{0:T(1024)S(1)} %pad_clamp_fusion), kind=kCustom, calls=%fused_computation | custom fusion | bytes 4194816 | tf_op jit(solution)/shard_map/jit(_take)/gather | solution.py:37
  40.0 3.2 %broadcast_select_fusion = bf16[128,2,8,512]{3,2,1,0:T(8,128)(2,1)} fusion(bf16[128,2,8,512]{3,2,1,0:T(8,128)(2,1)} %gather_fusion, pred[128]{0:T(512)(128)(4,1)S(1)} %compare_and_fusion), kind=kLoop, calls=%fused_computation.47 | loop fusion | flops 1048576 | bytes 4194432 | tf_op jit(solution)/shard_map/jit(_take)/select_n | solution.py:37
  43.2 6.4 %all-to-all-start = ((bf16[128,2,8,512]{3,2,1,0:T(8,128)(2,1)}), bf16[128,2,8,512]{3,2,1,0:T(8,128)(2,1)S(1)}, u32[]{:S(2)}, u32[]{:S(2)}) async-start(bf16[128,2,8,512]{3,2,1,0:T(8,128)(2,1)} %broadcast_select_fusion), calls=%async_computation | async-start | bytes 4194304 | tf_op jit(solution)/shard_map/all_to_all | solution.py:38
  50.3 0.2 convert_reduce_fusion
  50.4 0.1 select_reduce_fusion.1
  50.6 0.1 add_compare_fusion
  50.7 0.1 lt.86
  50.8 2.2 %copy.34 = bf16[16,8,64,128]{3,2,1,0:T(8,128)(2,1)S(1)} copy(bf16[16,8,64,128]{3,1,2,0:T(8,128)(2,1)} %bitcast.53) | data formatting | bytes 4194304
  53.0 0.1 broadcast_in_dim.126
  53.1 0.3 copy.26
  54.1 0.4 fusion.81
  54.5 0.7 copy_bitcast_fusion
  55.1 0.4 fusion.80
  55.5 1.9 %fusion.82 = (f32[2048]{0:T(1024)}, f32[2048,128]{0,1:T(8,128)}) fusion(pred[2048,128]{0,1:T(32,128)(4,1)S(1)} %copy.26, bf16[2048,128]{1,0:T(8,128)(2,1)S(1)} %bitcast.47, bf16[128,512]{1,0:T(8,128)(2,1)S(1)} %get-tuple-element.34), kind=kOutput, calls=%fused_computation.119 | convolution fusion | flops 67893248 | bytes 1875968 | tf_op jit(solution)/shard_map/rd,nd->rn/dot_general | solution.py:68
  57.4 1.3 fusion.84
  58.8 1.3 fusion.85
  60.1 1.4 fusion.83
  61.5 35.5 %all-to-all-done = bf16[128,2,8,512]{3,2,1,0:T(8,128)(2,1)S(1)} async-done(((bf16[128,2,8,512]{3,2,1,0:T(8,128)(2,1)}), bf16[128,2,8,512]{3,2,1,0:T(8,128)(2,1)S(1)}, u32[]{:S(2)}, u32[]{:S(2)}) %all-to-all-start) | async-done | bytes 2097184 | tf_op jit(solution)/shard_map/all_to_all | solution.py:38
  97.0 0.1 slice_bitcast_fusion
  97.2 2.7 %fusion.52 = f32[1024,2048]{1,0:T(8,128)S(1)} fusion(bf16[2048,128]{1,0:T(8,128)(2,1)} %bitcast.52, bf16[1024,512]{1,0:T(8,128)(2,1)S(1)} %get-tuple-element.15), kind=kOutput, calls=%fused_computation.70 | convolution fusion | flops 536870912 | bytes 9175040 | tf_op jit(solution)/shard_map/rd,nd->rn/dot_general | solution.py:59
  99.9 1.3 fusion.49
  101.1 1.5 %fusion = (f32[2048]{0:T(1024)S(1)}, f32[1024,2048]{1,0:T(8,128)S(1)}) fusion(pred[1024]{0:T(1024)(128)(4,1)S(1)} %lt.86, bf16[2048,128]{1,0:T(8,128)(2,1)S(1)} %bitcast.48, bf16[1024,512]{1,0:T(8,128)(2,1)S(1)} %get-tuple-element.15), kind=kOutput, calls=%fused_computation.9 | convolution fusion | flops 543160320 | bytes 9184256 | tf_op jit(solution)/shard_map/rd,nd->rn/dot_general | solution.py:59
  102.7 3.2 %copy-done.2 = f32[1024,2048]{1,0:T(8,128)} copy-done((f32[1024,2048]{1,0:T(8,128)}, f32[1024,2048]{1,0:T(8,128)S(1)}, u32[]{:S(2)}) %copy-start.2) | copy-done | bytes 8388632
  105.9 3.2 %fusion.18 = f32[2048,128]{1,0:T(8,128)} fusion(f32[1024,2048]{1,0:T(8,128)S(1)} %get-tuple-element.23, f32[2048]{0:T(1024)S(1)} %max.32, pred[1024]{0:T(1024)(128)(4,1)S(1)} %lt.86, bf16[1024,512]{1,0:T(8,128)(2,1)S(1)} %get-tuple-element.14), kind=kOutput, calls=%fused_computation.26 | convolution fusion | flops 545259520 | bytes 9708544 | tf_op jit(solution)/shard_map/dot_general | solution.py:87
  109.1 11.7 %fusion.4 = (f32[2048]{0:T(1024)}, f32[2048]{0:T(1024)S(1)}, f32[2048]{0:T(1024)S(1)}, f32[2048]{0:T(1024)S(1)}, f32[1024,2048]{1,0:T(8,128)}) fusion(f32[1024,2048]{1,0:T(8,128)} %copy-done.2, f32[2048]{0:T(1024)S(1)} %max.32, pred[1024]{0:T(1024)(128)(4,1)S(1)} %lt.86, f32[1024,2048]{1,0:T(8,128)S(1)} %fusion.52, f32[1024,2048]{1,0:T(8,128)S(1)} %fusion.49, ...), kind=kOutput, calls=%fused_computation.13 | convolution fusion | flops 564125696 | bytes 34382848 | tf_op jit(solution)/shard_map/rd,nd->rn/dot_general | solution.py:59
  120.9 2.2 %fusion.14 = f32[2048,128]{1,0:T(8,128)S(1)} fusion(f32[1024,2048]{1,0:T(8,128)S(1)} %fusion.52, f32[2048]{0:T(1024)S(1)} %max.34, pred[1024]{0:T(1024)(128)(4,1)S(1)} %lt.86, bf16[1024,512]{1,0:T(8,128)(2,1)S(1)} %copy-done.13), kind=kOutput, calls=%fused_computation.24 | convolution fusion | flops 545259520 | bytes 9708544 | tf_op jit(solution)/shard_map/dot_general | solution.py:87
  123.2 1.1 copy-done.3
  124.3 2.3 %fusion.16 = f32[2048,128]{1,0:T(8,128)S(1)} fusion(f32[1024,2048]{1,0:T(8,128)S(1)} %copy-done.3, f32[2048]{0:T(1024)S(1)} %max.33, pred[1024]{0:T(1024)(128)(4,1)S(1)} %lt.86, bf16[1024,512]{1,0:T(8,128)(2,1)S(1)} %copy-done.13), kind=kOutput, calls=%fused_computation.25 | convolution fusion | flops 545259520 | bytes 9708544 | tf_op jit(solution)/shard_map/dot_general | solution.py:87
  126.5 8.1 %fusion.6 = (f32[2048]{0:T(1024)S(1)}, f32[2048]{0:T(1024)S(1)}, f32[2048]{0:T(1024)S(1)}) fusion(f32[1024,2048]{1,0:T(8,128)} %get-tuple-element.26, f32[2048]{0:T(1024)S(1)} %max.33, pred[1024]{0:T(1024)(128)(4,1)S(1)} %lt.86, f32[2048]{0:T(1024)S(1)} %max.34, f32[1024,2048]{1,0:T(8,128)S(1)} %fusion.52, f32[2048]{0:T(1024)S(1)} %max.35, ...), kind=kLoop, calls=%fused_computation.15 | loop fusion | flops 25159680 | bytes 25216000 | tf_op jit(solution)/shard_map/reduce_sum | solution.py:84
  134.8 2.2 %fusion.12 = f32[2048,128]{1,0:T(8,128)S(1)} fusion(f32[1024,2048]{1,0:T(8,128)S(1)} %fusion.49, f32[2048]{0:T(1024)S(1)} %max.35, pred[1024]{0:T(1024)(128)(4,1)S(1)} %lt.86, bf16[1024,512]{1,0:T(8,128)(2,1)S(1)} %copy-done.13), kind=kOutput, calls=%fused_computation.23 | convolution fusion | flops 545259520 | bytes 9708544 | tf_op jit(solution)/shard_map/dot_general | solution.py:87
  137.0 0.2 fusion.32
  137.2 0.2 fusion.34
  137.4 0.2 fusion.36
  137.5 0.2 fusion.38
  137.8 0.5 fusion.30
  138.3 0.5 fusion.28
  138.8 0.5 fusion.26
  139.3 0.5 fusion.24
  139.8 0.3 pad_maximum_fusion
  140.1 2.0 %copy.31 = bf16[128,4,16,128]{3,2,1,0:T(8,128)(2,1)} copy(bf16[128,4,16,128]{3,2,0,1:T(8,128)(2,1)S(1)} %pad_maximum_fusion) | data formatting | bytes 4194304 | tf_op jit(solution)/shard_map/stack | solution.py:98
  142.1 4.2 %stack.6 = bf16[1,128,8192]{2,1,0:T(8,128)(2,1)} reshape(bf16[128,4,16,128]{3,2,1,0:T(8,128)(2,1)} %copy.31) | data formatting | bytes 4194304 | tf_op jit(solution)/shard_map/stack | solution.py:98
  146.3 3.4 %select_convert_fusion = bf16[1,128,8192]{2,1,0:T(8,128)(2,1)} fusion(bf16[1,128,8192]{2,1,0:T(8,128)(2,1)} %stack.6, pred[128]{0:T(512)(128)(4,1)S(1)} %iota_compare_fusion.4), kind=kLoop, calls=%fused_computation.22 | loop fusion | flops 1048576 | bytes 4194432 | tf_op jit(solution)/shard_map/convert_element_type | solution.py:100
  (53 shorter events, 0.2 us)
Async XLA Ops:
  0.0 38.0 %copy-start = (bf16[128,2,8,512]{3,2,1,0:T(8,128)(2,1)S(1)}, bf16[128,2,8,512]{3,2,1,0:T(8,128)(2,1)}, u32[]{:S(2)}) copy-start(bf16[128,2,8,512]{3,2,1,0:T(8,128)(2,1)} %param.9) | copy-start | bytes 6291460
  0.0 50.2 %copy-start.17 = (s32[1,128]{1,0:T(1,128)S(1)}, s32[1,128]{1,0:T(1,128)}, u32[]{:S(2)}) copy-start(s32[1,128]{1,0:T(1,128)} %param.10) | copy-start | bytes 1540
  38.0 16.1 %copy-start.11 = (bf16[1,128,2,512]{3,2,1,0:T(2,128)(2,1)S(1)}, bf16[1,128,2,512]{3,2,1,0:T(2,128)(2,1)}, u32[]{:S(2)}) copy-start(bf16[1,128,2,512]{3,2,1,0:T(2,128)(2,1)} %param.8) | copy-start | bytes 786436
  43.2 53.9 %all-to-all-start = ((bf16[128,2,8,512]{3,2,1,0:T(8,128)(2,1)}), bf16[128,2,8,512]{3,2,1,0:T(8,128)(2,1)S(1)}, u32[]{:S(2)}, u32[]{:S(2)}) async-start(bf16[128,2,8,512]{3,2,1,0:T(8,128)(2,1)} %broadcast_select_fusion), calls=%async_computation | async-start | bytes 4194304 | tf_op jit(solution)/shard_map/all_to_all | solution.py:38
  55.5 4.6 %copy-start.4 = (bf16[128,1,16,128]{3,2,1,0:T(8,128)(2,1)}, bf16[128,1,16,128]{3,2,1,0:T(8,128)(2,1)S(1)}, u32[]{:S(2)}) copy-start(bf16[128,1,16,128]{3,2,1,0:T(8,128)(2,1)S(1)} %get-tuple-element.16) | copy-start | bytes 1572868
  55.5 4.6 %copy-start.9 = (bf16[128,1,16,128]{3,2,1,0:T(8,128)(2,1)}, bf16[128,1,16,128]{3,2,1,0:T(8,128)(2,1)S(1)}, u32[]{:S(2)}) copy-start(bf16[128,1,16,128]{3,2,1,0:T(8,128)(2,1)S(1)} %get-tuple-element.18) | copy-start | bytes 1572868
  97.2 5.5 %copy-start.12 = (bf16[1024,512]{1,0:T(8,128)(2,1)}, bf16[1024,512]{1,0:T(8,128)(2,1)S(1)}, u32[]{:S(2)}) copy-start(bf16[1024,512]{1,0:T(8,128)(2,1)S(1)} %get-tuple-element.14) | copy-start | bytes 3145732
  101.1 1.6 %copy-start.15 = (f32[2048]{0:T(1024)S(1)}, f32[2048]{0:T(1024)}, u32[]{:S(2)}) copy-start(f32[2048]{0:T(1024)} %get-tuple-element.24) | copy-start | bytes 24580
  102.7 3.2 %copy-start.2 = (f32[1024,2048]{1,0:T(8,128)}, f32[1024,2048]{1,0:T(8,128)S(1)}, u32[]{:S(2)}) copy-start(f32[1024,2048]{1,0:T(8,128)S(1)} %get-tuple-element.23) | copy-start | bytes 25165828
  105.9 3.2 %copy-start.10 = (bf16[128,1,16,128]{3,2,1,0:T(8,128)(2,1)S(1)}, bf16[128,1,16,128]{3,2,1,0:T(8,128)(2,1)}, u32[]{:S(2)}) copy-start(bf16[128,1,16,128]{3,2,1,0:T(8,128)(2,1)} %copy-done.9) | copy-start | bytes 1572868
  109.1 11.8 %copy-start.13 = (bf16[1024,512]{1,0:T(8,128)(2,1)S(1)}, bf16[1024,512]{1,0:T(8,128)(2,1)}, u32[]{:S(2)}) copy-start(bf16[1024,512]{1,0:T(8,128)(2,1)} %copy-done.12) | copy-start | bytes 3145732
  120.9 3.4 %copy-start.3 = (f32[1024,2048]{1,0:T(8,128)S(1)}, f32[1024,2048]{1,0:T(8,128)}, u32[]{:S(2)}) copy-start(f32[1024,2048]{1,0:T(8,128)} %get-tuple-element.26) | copy-start | bytes 25165828
  134.7 2.3 %copy-start.8 = (f32[2048,128]{0,1:T(8,128)S(1)}, f32[2048,128]{0,1:T(8,128)}, u32[]{:S(2)}) copy-start(f32[2048,128]{0,1:T(8,128)} %get-tuple-element.25) | copy-start | bytes 3145732
  134.7 2.5 %copy-start.7 = (f32[2048,128]{0,1:T(8,128)S(1)}, f32[2048,128]{0,1:T(8,128)}, u32[]{:S(2)}) copy-start(f32[2048,128]{0,1:T(8,128)} %get-tuple-element.30) | copy-start | bytes 3145732
  134.7 2.6 %copy-start.6 = (f32[2048,128]{0,1:T(8,128)S(1)}, f32[2048,128]{0,1:T(8,128)}, u32[]{:S(2)}) copy-start(f32[2048,128]{0,1:T(8,128)} %get-tuple-element.32) | copy-start | bytes 3145732
  134.7 2.8 %copy-start.5 = (f32[2048,128]{0,1:T(8,128)S(1)}, f32[2048,128]{0,1:T(8,128)}, u32[]{:S(2)}) copy-start(f32[2048,128]{0,1:T(8,128)} %get-tuple-element.28) | copy-start | bytes 3145732
  134.7 3.0 %copy-start.16 = (f32[2048]{0:T(1024)S(1)}, f32[2048]{0:T(1024)}, u32[]{:S(2)}) copy-start(f32[2048]{0:T(1024)} %get-tuple-element.5) | copy-start | bytes 24580
  134.7 3.0 %copy-start.14 = (bf16[128,512]{1,0:T(8,128)(2,1)S(1)}, bf16[128,512]{1,0:T(8,128)(2,1)}, u32[]{:S(2)}) copy-start(bf16[128,512]{1,0:T(8,128)(2,1)} %get-tuple-element.33) | copy-start | bytes 393220
  134.7 3.0 %copy-start.18 = (f32[2048,128]{1,0:T(8,128)S(1)}, f32[2048,128]{1,0:T(8,128)}, u32[]{:S(2)}) copy-start(f32[2048,128]{1,0:T(8,128)} %fusion.18) | copy-start | bytes 3145732
  139.8 9.8 %copy-start.1 = (bf16[128,2,8,512]{3,2,1,0:T(8,128)(2,1)S(1)}, bf16[128,2,8,512]{3,2,1,0:T(8,128)(2,1)}, u32[]{:S(2)}) copy-start(bf16[128,2,8,512]{3,2,1,0:T(8,128)(2,1)} %param.9) | copy-start | bytes 6291460
where the time goes:
time: 150 us
  blocking collectives  37.1 us (25%)
  waiting for transfers between devices  35.5 us (24%)
  matrix products  35.2 us (23%)
  local copies, waits for them, and re-layouts  16.9 us (11%)
  other arithmetic  16.7 us (11%)
  starting transfers between devices  6.42 us (4%)
  between operations  1.75 us (1%)
    all_to_all x1, waiting for transfers between devices, local(): lax.all_to_all(sending, 'dp', split_axis=0, concat_axis=0, tiled=True)  35.5 us
    all_gather x1, blocking collectives, local(): lax.all_gather(page_slot, 'dp', axis=0, tiled=True)  21.3 us
    dot_general x4, matrix products, local(): jnp.einsum('rd,nd->rn', query_rows, cache_keys[:, low_col:low_col + HD],...  17.2 us
    all_gather x1, blocking collectives, local(): lax.all_gather(page_holder, 'dp', axis=0, tiled=True)  15.8 us
    dot_general x4, matrix products, local(): jnp.dot(cache_weights.astype(jnp.bfloat16), cache_values[:, low_col:low_c...  9.98 us
    reduce_sum x1, other arithmetic, local(): jnp.sum(cache_weights, axis=1, keepdims=True)  8.13 us
    unnamed x39, local copies, waits for them, and re-layouts  6.55 us
    all_to_all x1, starting transfers between devices, local(): lax.all_to_all(sending, 'dp', split_axis=0, concat_axis=0, tiled=True)  6.42 us
  transfers between devices with their start and end apart: 1, of which 1 were waited for; matrix products, arithmetic and copies ran while one was open for 7% of the time, Pallas kernels for 0%

commit v1 on v0

v1 whole, which is shorter than its diff:
```python
import functools

import jax
import jax.numpy as jnp
from jax import lax
from jax.experimental import pallas as pl
from jax.experimental.pallas import tpu as pltpu
from jax.sharding import PartitionSpec as P

H = 64
KVH = 4
HD = 128
PAGE = 8
MP = 128
C = 128
GROUP = H // KVH
LOG2E = 1.4426950408889634
NEG = -1e30


def gather_kernel(outgoing_ref, pool_ref, *out_refs):
    devices, capacity = out_refs[0].shape[0], out_refs[0].shape[2]

    def step(t, carry):
        for r in range(capacity):
            page = pool_ref[outgoing_ref[t * capacity + r]]
            for h in range(KVH):
                out_refs[h][t, :, r] = page[:, :, h * HD : (h + 1) * HD]
        return carry

    lax.fori_loop(0, devices, step, 0)


def gather_pages(kv_pool, outgoing, devices):
    capacity = MP // devices
    piece = jax.ShapeDtypeStruct((devices, 2, capacity, PAGE, HD), kv_pool.dtype)
    return pl.pallas_call(
        gather_kernel,
        out_shape=(piece,) * KVH,
        in_specs=[
            pl.BlockSpec(memory_space=pltpu.SMEM),
            pl.BlockSpec(memory_space=pltpu.VMEM),
        ],
        out_specs=(pl.BlockSpec(memory_space=pltpu.VMEM),) * KVH,
        compiler_params=pltpu.CompilerParams(vmem_limit_bytes=24 * 2**20),
        cost_estimate=pl.CostEstimate(
            flops=0, bytes_accessed=2 * kv_pool.size * 2, transcendentals=0
        ),
        name="gather_pages",
    )(outgoing, kv_pool)


def attend_kernel(
    filled_ref, bias_ref, q_ref, k_ref, v_ref, fk_ref, fv_ref, *rest, heads
):
    o_ref = rest[-1]
    scale = HD**-0.5 * LOG2E
    rows = heads * C
    k = k_ref[...].reshape(MP * PAGE, HD)
    v = v_ref[...].reshape(MP * PAGE, HD)
    fk = fk_ref[...]
    fv = fv_ref[...]
    bias = bias_ref[...]
    nt = (((1,), (1,)), ((), ()))
    token = lax.rem(lax.broadcasted_iota(jnp.int32, (rows, C), 0), C)
    causal = lax.broadcasted_iota(jnp.int32, (rows, C), 1) <= token
    live = token[:, :HD] < filled_ref[0]
    for g in range(0, GROUP, heads):
        q = jnp.concatenate(
            [q_ref[:, (g + i) * HD : (g + i + 1) * HD] for i in range(heads)], axis=0
        )
        s1 = lax.dot_general(q, k, nt, preferred_element_type=jnp.float32) + bias
        s2 = lax.dot_general(q, fk, nt, preferred_element_type=jnp.float32)
        s2 = jnp.where(causal, s2, NEG)
        top = jnp.maximum(
            jnp.max(s1, axis=1, keepdims=True), jnp.max(s2, axis=1, keepdims=True)
        )
        p1 = jnp.exp2((s1 - top) * scale)
        p2 = jnp.exp2((s2 - top) * scale)
        total = jnp.sum(p1, axis=1, keepdims=True) + jnp.sum(p2, axis=1, keepdims=True)
        o = jnp.dot(p1.astype(jnp.bfloat16), v, preferred_element_type=jnp.float32)
        o += jnp.dot(p2.astype(jnp.bfloat16), fv, preferred_element_type=jnp.float32)
        o = jnp.where(live, o * (1.0 / total), 0.0).astype(o_ref.dtype)
        for i in range(heads):
            o_ref[:, (g + i) * HD : (g + i + 1) * HD] = o[i * C : (i + 1) * C]


def attend(h, filled, bias, queries, pages, fresh_k, fresh_v, out):
    width = GROUP * HD
    devices = pages.shape[0]
    tokens = MP * PAGE // devices
    pages = pages.reshape(devices, 2, tokens, HD)
    operands = [filled, bias, queries, pages, pages, fresh_k, fresh_v]
    in_specs = [
        pl.BlockSpec(memory_space=pltpu.SMEM),
        pl.BlockSpec((1, MP * PAGE), lambda i: (0, 0)),
        pl.BlockSpec((C, width), lambda i: (0, h)),
        pl.BlockSpec((devices, None, tokens, HD), lambda i: (0, 0, 0, 0)),
        pl.BlockSpec((devices, None, tokens, HD), lambda i: (0, 1, 0, 0)),
        pl.BlockSpec((C, HD), lambda i: (0, h)),
        pl.BlockSpec((C, HD), lambda i: (0, h)),
    ]
    aliases = {}
    if out is not None:
        operands.append(out)
        in_specs.append(pl.BlockSpec(memory_space=pl.ANY))
        aliases = {len(operands) - 1: 0}
    return pl.pallas_call(
        functools.partial(attend_kernel, heads=2),
        grid=(1,),
        out_shape=jax.ShapeDtypeStruct((C, H * HD), jnp.bfloat16),
        in_specs=in_specs,
        out_specs=pl.BlockSpec((C, width), lambda i: (0, h)),
        input_output_aliases=aliases,
        compiler_params=pltpu.CompilerParams(vmem_limit_bytes=32 * 2**20),
        cost_estimate=pl.CostEstimate(
            flops=4 * C * width * (MP * PAGE + C),
            bytes_accessed=4 * C * width * 2,
            transcendentals=C * GROUP * (MP * PAGE + C),
        ),
        name=f"attend_{h}",
    )(*operands)


def local(queries, fresh_kv, kv_pool, page_holder, page_slot, cached_len, fresh_len):
    devices = lax.axis_size("dp")
    capacity = MP // devices
    holder, slot = page_holder[0], page_slot[0]
    page = jnp.arange(MP, dtype=jnp.int32)
    same = holder[:, None] == holder[None, :]
    rank = jnp.sum((same & (page[None, :] < page[:, None])).astype(jnp.int32), axis=1)
    hits = (holder * capacity + rank)[:, None] == page[None, :]
    asked = jnp.sum(jnp.where(hits, slot[:, None], 0), axis=0).reshape(devices, capacity)
    outgoing = lax.all_to_all(asked, "dp", split_axis=0, concat_axis=0, tiled=True)
    pieces = gather_pages(kv_pool, outgoing.reshape(MP), devices)
    received = [
        lax.all_to_all(piece, "dp", split_axis=0, concat_axis=0, tiled=True)
        for piece in pieces
    ]
    arrived = jnp.sum(jnp.where(hits, page[:, None], 0), axis=0)
    place = arrived[:, None] * PAGE + jnp.arange(PAGE, dtype=jnp.int32)[None, :]
    bias = jnp.where(place < cached_len[0], 0.0, NEG).astype(jnp.float32)
    bias = bias.reshape(1, MP * PAGE)
    fresh_k, fresh_v = fresh_kv[0, :, 0], fresh_kv[0, :, 1]
    out = None
    for h in range(KVH):
        out = attend(
            h, fresh_len, bias, queries[0], received[h], fresh_k, fresh_v, out
        )
    return out[None]


def solution(mesh):
    return jax.shard_map(
        local,
        mesh=mesh,
        in_specs=(
            P(("groups", "dp"), None, None),
            P(("groups", "dp"), None, None, None),
            P(("groups", "dp"), None, None, None),
            P(("groups", "dp"), None),
            P(("groups", "dp"), None),
            P(("groups", "dp")),
            P(("groups", "dp")),
        ),
        out_specs=P(("groups", "dp"), None, None),
        check_vma=False,
    )
```

time: 150 us -> 103 us (0.69)
  the two profiles are of different devices: /device:TPU:11 before, /device:TPU:0 now
where the time goes in v1:
time: 103 us
  blocking collectives  49.1 us (48%)
  Pallas kernels  24.5 us (24%)
  waiting for transfers between devices  13.2 us (13%)
  starting transfers between devices  8.62 us (8%)
  other arithmetic  3.08 us (3%)
  local copies, waits for them, and re-layouts  2.79 us (3%)
  between operations  1.42 us (1%)
    all_to_all x2, blocking collectives, local(): lax.all_to_all(piece, 'dp', split_axis=0, concat_axis=0, tiled=True)  35.5 us
    pallas_call x4, Pallas kernels, attend(): pl.pallas_call(functools.partial(attend_kernel, heads=2), grid=(1,), out_...  23.6 us
    all_to_all x1, blocking collectives, local(): lax.all_to_all(asked, 'dp', split_axis=0, concat_axis=0, tiled=True)  13.6 us
    all_to_all x2, waiting for transfers between devices, local(): lax.all_to_all(piece, 'dp', split_axis=0, concat_axis=0, tiled=True)  13.2 us
    all_to_all x2, starting transfers between devices, local(): lax.all_to_all(piece, 'dp', split_axis=0, concat_axis=0, tiled=True)  8.62 us
  transfers between devices with their start and end apart: 2, of which 1 were waited for; matrix products, arithmetic and copies ran while one was open for 1% of the time, Pallas kernels for 17%

profile of v1, /device:TPU:0, one launch (start us, length us, event | category | flops | bytes accessed | tf_op | source)
XLA Modules:
  0.0 102.7 jit_solution(8360038195933470767)
XLA Ops:
  0.0 0.9 convert_reduce_fusion
  0.9 0.7 multiply_add_fusion
  1.6 0.8 select_reduce_fusion
  2.3 0.1 all_to_all.18
  2.4 13.6 %all_to_all.29 = s32[16,1,8]{2,1,0:T(1,128)S(1)} all-to-all(s32[16,1,8]{2,1,0:T(1,128)S(1)} %bitcast.24), channel_id=1, replica_groups=mesh['groups'=2,'dp'=16] {'dp'}, dimensions={0} | all-to-all | bytes 1024 | tf_op jit(solution)/shard_map/all_to_all | solution.py:134
  16.0 0.5 broadcast.43
  16.5 0.7 reduce.3
  17.2 0.1 reshape.68.outgoing_ref
  17.3 0.0 copy-start.1
  17.3 1.6 %copy-done.1 = bf16[128,2,8,512]{3,2,1,0:T(8,128)(2,1)S(1)} copy-done((bf16[128,2,8,512]{3,2,1,0:T(8,128)(2,1)S(1)}, bf16[128,2,8,512]{3,2,1,0:T(8,128)(2,1)}, u32[]{:S(2)}) %copy-start.1) | copy-done | bytes 2097176
  18.9 1.0 gather_pages.1
  19.8 0.0 copy-start.2
  19.8 0.0 copy-start.3
  19.9 0.0 copy-start.4
  19.9 17.2 %all_to_all.30 = bf16[16,2,8,8,128]{4,3,2,1,0:T(8,128)(2,1)S(1)} all-to-all(bf16[16,2,8,8,128]{4,3,2,1,0:T(8,128)(2,1)S(1)} %get-tuple-element.10), channel_id=1, replica_groups=mesh['groups'=2,'dp'=16] {'dp'}, dimensions={0} | all-to-all | bytes 1048576 | tf_op jit(solution)/shard_map/all_to_all | solution.py:137
  37.1 0.0 copy-done.2
  37.1 18.3 %all_to_all.31 = bf16[16,2,8,8,128]{4,3,2,1,0:T(8,128)(2,1)S(1)} all-to-all(bf16[16,2,8,8,128]{4,3,2,1,0:T(8,128)(2,1)S(1)} %get-tuple-element.11), channel_id=1, replica_groups=mesh['groups'=2,'dp'=16] {'dp'}, dimensions={0} | all-to-all | bytes 1048576 | tf_op jit(solution)/shard_map/all_to_all | solution.py:137
  55.4 0.0 copy-done.3
  55.4 0.0 copy-start
  55.4 4.4 %all-to-all-start.4 = ((bf16[16,2,8,8,128]{4,3,2,1,0:T(8,128)(2,1)}), bf16[16,2,8,8,128]{4,3,2,1,0:T(8,128)(2,1)}, u32[]{:S(2)}, u32[]{:S(2)}) async-start(bf16[16,2,8,8,128]{4,3,2,1,0:T(8,128)(2,1)} %copy-done.3), calls=%async_computation.4 | async-start | bytes 1048576 | tf_op jit(solution)/shard_map/all_to_all | solution.py:137
  61.1 13.2 %all-to-all-done.4 = bf16[16,2,8,8,128]{4,3,2,1,0:T(8,128)(2,1)} async-done(((bf16[16,2,8,8,128]{4,3,2,1,0:T(8,128)(2,1)}), bf16[16,2,8,8,128]{4,3,2,1,0:T(8,128)(2,1)}, u32[]{:S(2)}, u32[]{:S(2)}) %all-to-all-start.4) | async-done | bytes 524320 | tf_op jit(solution)/shard_map/all_to_all | solution.py:137
  74.2 4.2 %all-to-all-start.1 = ((bf16[16,2,8,8,128]{4,3,2,1,0:T(8,128)(2,1)}), bf16[16,2,8,8,128]{4,3,2,1,0:T(8,128)(2,1)}, u32[]{:S(2)}, u32[]{:S(2)}) async-start(bf16[16,2,8,8,128]{4,3,2,1,0:T(8,128)(2,1)} %copy-done.2), calls=%async_computation.1 | async-start | bytes 1048576 | tf_op jit(solution)/shard_map/all_to_all | solution.py:137
  78.5 0.1 fusion.1
  78.6 0.1 select_n.23.bias_ref
  78.7 0.0 copy-done.4
  78.7 0.4 fusion.2
  79.1 0.0 copy-done
  79.1 6.4 %attend_0.1.rest_0_ = bf16[128,8192]{1,0:T(8,128)(2,1)} custom-call(s32[1]{0:T(128)S(6)} %copy.29.filled_ref, f32[1,1024]{1,0:T(1,128)S(1)} %select_n.23.bias_ref, bf16[128,8192]{1,0:T(8,128)(2,1)S(1)} %bitcast.16, bf16[16,2,64,128]{3,2,1,0:T(8,128)(2,1)} %bitcast.10.k_ref.v_ref, bf16[16,2,64,128]{3,2,1,0:T(8,128)(2,1)} %bitcast.10.k_ref.v_ref, ...), custom_call_target="tpu_custom_call" | custom-call | flops 1207959552 | bytes 2097152 | tf_op jit(solution)/shard_map/attend_0/pallas_call | solution.py:108
  85.4 5.3 %attend_1.1.rest_0_ = bf16[128,8192]{1,0:T(8,128)(2,1)} custom-call(s32[1]{0:T(128)S(6)} %copy.29.filled_ref, f32[1,1024]{1,0:T(1,128)S(1)} %select_n.23.bias_ref, bf16[128,8192]{1,0:T(8,128)(2,1)S(1)} %bitcast.17, bf16[16,2,64,128]{3,2,1,0:T(8,128)(2,1)S(1)} %bitcast.22, bf16[16,2,64,128]{3,2,1,0:T(8,128)(2,1)S(1)} %bitcast.23, ...), custom_call_target="tpu_custom_call", output_to_operand_aliasing={{}: (7, {})} | custom-call | flops 1207959552 | bytes 2097152 | tf_op jit(solution)/shard_map/attend_1/pallas_call | solution.py:108
  90.8 5.5 %attend_2.1.rest_0_ = bf16[128,8192]{1,0:T(8,128)(2,1)} custom-call(s32[1]{0:T(128)S(6)} %copy.29.filled_ref, f32[1,1024]{1,0:T(1,128)S(1)} %select_n.23.bias_ref, bf16[128,8192]{1,0:T(8,128)(2,1)S(1)} %bitcast.18, bf16[16,2,64,128]{3,2,1,0:T(8,128)(2,1)S(1)} %bitcast.20, bf16[16,2,64,128]{3,2,1,0:T(8,128)(2,1)S(1)} %bitcast.21, ...), custom_call_target="tpu_custom_call", output_to_operand_aliasing={{}: (7, {})} | custom-call | flops 1207959552 | bytes 2097152 | tf_op jit(solution)/shard_map/attend_2/pallas_call | solution.py:108
  96.3 0.0 all-to-all-done.1
  96.3 6.3 %attend_3.1 = bf16[128,8192]{1,0:T(8,128)(2,1)} custom-call(s32[1]{0:T(128)S(6)} %copy.29.filled_ref, f32[1,1024]{1,0:T(1,128)S(1)} %select_n.23.bias_ref, bf16[128,8192]{1,0:T(8,128)(2,1)S(1)} %bitcast.19, bf16[16,2,64,128]{3,2,1,0:T(8,128)(2,1)} %bitcast.5.k_ref.v_ref, ...), custom_call_target="tpu_custom_call", output_to_operand_aliasing={{}: (7, {})} | custom-call | flops 1207959552 | bytes 2097152 | tf_op jit(solution)/shard_map/attend_3/pallas_call | solution.py:108
  (2 shorter events, 0.0 us)
Async XLA Ops:
  17.3 1.6 %copy-start.1 = (bf16[128,2,8,512]{3,2,1,0:T(8,128)(2,1)S(1)}, bf16[128,2,8,512]{3,2,1,0:T(8,128)(2,1)}, u32[]{:S(2)}) copy-start(bf16[128,2,8,512]{3,2,1,0:T(8,128)(2,1)} %pool_ref.1) | copy-start | bytes 6291460
  19.8 17.2 %copy-start.2 = (bf16[16,2,8,8,128]{4,3,2,1,0:T(8,128)(2,1)}, bf16[16,2,8,8,128]{4,3,2,1,0:T(8,128)(2,1)S(1)}, u32[]{:S(2)}) copy-start(bf16[16,2,8,8,128]{4,3,2,1,0:T(8,128)(2,1)S(1)} %get-tuple-element.9) | copy-start | bytes 1572868
  19.8 35.5 %copy-start.3 = (bf16[16,2,8,8,128]{4,3,2,1,0:T(8,128)(2,1)}, bf16[16,2,8,8,128]{4,3,2,1,0:T(8,128)(2,1)S(1)}, u32[]{:S(2)}) copy-start(bf16[16,2,8,8,128]{4,3,2,1,0:T(8,128)(2,1)S(1)} %get-tuple-element.12) | copy-start | bytes 1572868
  19.9 58.8 %copy-start.4 = (bf16[1,128,2,512]{3,2,1,0:T(2,128)(2,1)S(1)}, bf16[1,128,2,512]{3,2,1,0:T(2,128)(2,1)}, u32[]{:S(2)}) copy-start(bf16[1,128,2,512]{3,2,1,0:T(2,128)(2,1)} %param.8) | copy-start | bytes 786436
  55.4 23.7 %copy-start = (bf16[1,128,8192]{2,1,0:T(8,128)(2,1)S(1)}, bf16[1,128,8192]{2,1,0:T(8,128)(2,1)}, u32[]{:S(2)}) copy-start(bf16[1,128,8192]{2,1,0:T(8,128)(2,1)} %param.7) | copy-start | bytes 6291460
  55.4 18.9 %all-to-all-start.4 = ((bf16[16,2,8,8,128]{4,3,2,1,0:T(8,128)(2,1)}), bf16[16,2,8,8,128]{4,3,2,1,0:T(8,128)(2,1)}, u32[]{:S(2)}, u32[]{:S(2)}) async-start(bf16[16,2,8,8,128]{4,3,2,1,0:T(8,128)(2,1)} %copy-done.3), calls=%async_computation.4 | async-start | bytes 1048576 | tf_op jit(solution)/shard_map/all_to_all | solution.py:137
  74.2 22.1 %all-to-all-start.1 = ((bf16[16,2,8,8,128]{4,3,2,1,0:T(8,128)(2,1)}), bf16[16,2,8,8,128]{4,3,2,1,0:T(8,128)(2,1)}, u32[]{:S(2)}, u32[]{:S(2)}) async-start(bf16[16,2,8,8,128]{4,3,2,1,0:T(8,128)(2,1)} %copy-done.2), calls=%async_computation.1 | async-start | bytes 1048576 | tf_op jit(solution)/shard_map/all_to_all | solution.py:137

commit v2 on v1

v2 whole, which is shorter than its diff:
```python
import functools

import jax
import jax.numpy as jnp
from jax import lax
from jax.experimental import pallas as pl
from jax.experimental.pallas import tpu as pltpu
from jax.sharding import PartitionSpec as P

H = 64
KVH = 4
HD = 128
PAGE = 8
MP = 128
C = 128
GROUP = H // KVH
LOG2E = 1.4426950408889634
NEG = -1e30
CHUNKS = ((0, 3), (3, 1))
MOST_PERMUTES = 8


def ask_kernel(me_ref, holder_ref, slot_ref, asked_ref):
    chips = asked_ref.shape[0]
    capacity = MP // (2 * chips)
    core = me_ref[0] & 1
    square = (MP, MP)
    row = lax.broadcasted_iota(jnp.int32, square, 0)
    lane = lax.broadcasted_iota(jnp.int32, square, 1)
    holder = jnp.broadcast_to(holder_ref[...], square)
    same = (holder.T == holder) & (row < lane)
    rank = jnp.sum(same.astype(jnp.int32), axis=0, keepdims=True)
    low = (holder_ref[...] & 1 ^ core) * capacity + rank
    packed = jnp.broadcast_to(low * MP + slot_ref[...], square).T
    slots = jnp.where(packed // MP == lane, packed % MP, 0)
    chip = lax.broadcasted_iota(jnp.int32, (chips, MP), 0)
    of_chip = jnp.broadcast_to(holder_ref[...] >> 1, (chips, MP)) == chip
    asked = jnp.dot(
        of_chip.astype(jnp.float32).astype(jnp.bfloat16),
        slots.astype(jnp.float32).astype(jnp.bfloat16),
        preferred_element_type=jnp.float32,
    )
    asked_ref[...] = asked.astype(jnp.int32).reshape(chips, 1, MP)


def ask(me, page_holder, page_slot, chips):
    return pl.pallas_call(
        ask_kernel,
        out_shape=jax.ShapeDtypeStruct((chips, 1, MP), jnp.int32),
        in_specs=[
            pl.BlockSpec(memory_space=pltpu.SMEM),
            pl.BlockSpec(memory_space=pltpu.VMEM),
            pl.BlockSpec(memory_space=pltpu.VMEM),
        ],
        out_specs=pl.BlockSpec(memory_space=pltpu.VMEM),
        name="ask",
    )(me, page_holder, page_slot)


def live_kernel(order_ref, length_ref, holder_ref, live_ref, *, capacity):
    square = (MP, MP)
    row = lax.broadcasted_iota(jnp.int32, square, 0)
    lane = lax.broadcasted_iota(jnp.int32, square, 1)
    holder = jnp.broadcast_to(holder_ref[...], square)
    same = (holder.T == holder) & (row < lane)
    rank = jnp.sum(same.astype(jnp.int32), axis=0, keepdims=True)
    place = (holder_ref[...] ^ order_ref[0]) * capacity + rank
    hits = jnp.broadcast_to(place, square) == row
    page = jnp.sum(jnp.where(hits, lane, 0), axis=1, keepdims=True)
    page = jnp.broadcast_to(page, square)
    shape = (MP, PAGE, HD)
    token = page[:, None, :] * PAGE + lax.broadcasted_iota(jnp.int32, shape, 1)
    live = jnp.where(token < length_ref[0], 1.0, 0.0)
    live_ref[...] = live.reshape(MP * PAGE, HD).astype(live_ref.dtype)


def live_tokens(order, cached_len, page_holder, capacity):
    return pl.pallas_call(
        functools.partial(live_kernel, capacity=capacity),
        out_shape=jax.ShapeDtypeStruct((MP * PAGE, HD), jnp.bfloat16),
        in_specs=[
            pl.BlockSpec(memory_space=pltpu.SMEM),
            pl.BlockSpec(memory_space=pltpu.SMEM),
            pl.BlockSpec(memory_space=pltpu.VMEM),
        ],
        out_specs=pl.BlockSpec(memory_space=pltpu.VMEM),
        name="live_tokens",
    )(order, cached_len, page_holder)


def gather_kernel(mine_ref, wanted_ref, own_ref, mate_ref, *out_refs, flip):
    whole = len(out_refs) == len(CHUNKS)
    chips, capacity = wanted_ref.shape[0], out_refs[0].shape[-3] // 2

    def copy(x, asker):
        for b, pool_ref in enumerate((own_ref, mate_ref)):
            for r in range(capacity):
                n = b * capacity + r
                page = pool_ref[wanted_ref[asker, 0, n]]
                for c, (first, count) in enumerate(CHUNKS):
                    out_ref = out_refs[c] if whole else out_refs[c * chips + x]
                    for h in range(count):
                        cols = slice((first + h) * HD, (first + h + 1) * HD)
                        if whole:
                            out_ref[x, h, :, n] = page[:, :, cols]
                        else:
                            out_ref[h, :, n] = page[:, :, cols]

    if whole:
        pl.loop(0, chips)(lambda x: copy(x, x))
    else:
        for x in range(chips):
            copy(x, mine_ref[0] ^ x)


def gather_pages(mine, wanted, own, mate, flip):
    chips = wanted.shape[0]
    places = MP // chips
    shapes = []
    for first, count in CHUNKS:
        shape = (count, 2, places, PAGE, HD)
        shapes += [shape] * chips if flip else [(chips,) + shape]
    pool = pl.BlockSpec(memory_space=pltpu.VMEM)
    return pl.pallas_call(
        functools.partial(gather_kernel, flip=flip),
        out_shape=[jax.ShapeDtypeStruct(shape, own.dtype) for shape in shapes],
        in_specs=[
            pl.BlockSpec(memory_space=pltpu.SMEM),
            pl.BlockSpec(memory_space=pltpu.SMEM),
            pool,
            pool,
        ],
        out_specs=[pl.BlockSpec(memory_space=pltpu.VMEM)] * len(shapes),
        compiler_params=pltpu.CompilerParams(vmem_limit_bytes=32 * 2**20),
        cost_estimate=pl.CostEstimate(
            flops=0, bytes_accessed=4 * own.size * 2, transcendentals=0
        ),
        name="gather_pages",
    )(mine, wanted, own, mate)


def attend_kernel(filled_ref, live_ref, q_ref, fk_ref, fv_ref, *rest, parts, heads):
    piece_refs = rest[:parts]
    o_ref, k_ref, v_ref = rest[-3:]
    scale = HD**-0.5 * LOG2E
    rows = heads * C
    tokens = piece_refs[0].shape[-2]
    cached = parts * tokens
    fk = fk_ref[...]
    for p in range(parts):
        at = slice(p * tokens, (p + 1) * tokens)
        live = live_ref[at]
        k_ref[at] = jnp.where(live > 0, piece_refs[p][0], fk[:1])
        v_ref[at, :HD] = jnp.where(live > 0, piece_refs[p][1], jnp.zeros_like(live))
        v_ref[at, HD:] = live
    k_ref[cached:] = fk
    v_ref[cached:, :HD] = fv_ref[...]
    v_ref[cached:, HD:] = jnp.ones_like(fk)
    nt = (((1,), (1,)), ((), ()))
    token = lax.rem(lax.broadcasted_iota(jnp.int32, (rows, C), 0), C)
    causal = lax.broadcasted_iota(jnp.int32, (rows, C), 1) <= token
    filled = token < filled_ref[0]
    for g in range(0, q_ref.shape[1] // HD, heads):
        q = jnp.concatenate(
            [q_ref[:, (g + i) * HD : (g + i + 1) * HD] for i in range(heads)], axis=0
        )
        s = lax.dot_general(q, k_ref[...], nt, preferred_element_type=jnp.float32)
        s1, s2 = s[:, :cached], jnp.where(causal, s[:, cached:], NEG)
        top = jnp.maximum(
            jnp.max(s1, axis=1, keepdims=True), jnp.max(s2, axis=1, keepdims=True)
        )
        p1 = jnp.exp2((s1 - top) * scale).astype(jnp.bfloat16)
        p2 = jnp.exp2((s2 - top) * scale).astype(jnp.bfloat16)
        o = jnp.dot(
            jnp.concatenate([p1, p2], axis=1),
            v_ref[...],
            preferred_element_type=jnp.float32,
        )
        o = jnp.where(filled, o[:, :HD] / o[:, HD:], 0.0).astype(o_ref.dtype)
        for i in range(heads):
            o_ref[:, (g + i) * HD : (g + i + 1) * HD] = o[i * C : (i + 1) * C]


def attend(first, filled, live, queries, fresh_k, fresh_v, pieces, out):
    width = GROUP * HD
    operands = [filled, live, queries, fresh_k, fresh_v]
    in_specs = [
        pl.BlockSpec(memory_space=pltpu.SMEM),
        pl.BlockSpec((MP * PAGE, HD), lambda h: (0, 0)),
        pl.BlockSpec((C, width), lambda h: (0, h + first)),
        pl.BlockSpec((C, HD), lambda h: (0, h + first)),
        pl.BlockSpec((C, HD), lambda h: (0, h + first)),
    ]
    parts = 0
    for piece in pieces:
        sources = piece.shape[0] if piece.ndim == 5 else 1
        for i in range(sources):
            operands.append(piece)
            if piece.ndim == 5:
                in_specs.append(
                    pl.BlockSpec(
                        (None, None) + piece.shape[2:],
                        lambda h, i=i: (i, h, 0, 0, 0),
                    )
                )
            else:
                in_specs.append(
                    pl.BlockSpec((None,) + piece.shape[1:], lambda h: (h, 0, 0, 0))
                )
        parts += sources
    count = pieces[0].shape[-4]
    aliases = {}
    if out is not None:
        operands.append(out)
        in_specs.append(pl.BlockSpec(memory_space=pl.ANY))
        aliases = {len(operands) - 1: 0}
    keys = MP * PAGE + C
    return pl.pallas_call(
        functools.partial(attend_kernel, parts=parts, heads=4),
        grid=(count,),
        out_shape=jax.ShapeDtypeStruct((C, H * HD), jnp.bfloat16),
        in_specs=in_specs,
        out_specs=pl.BlockSpec((C, width), lambda h: (0, h + first)),
        scratch_shapes=[
            pltpu.VMEM((keys, HD), jnp.bfloat16),
            pltpu.VMEM((keys, 2 * HD), jnp.bfloat16),
        ],
        input_output_aliases=aliases,
        compiler_params=pltpu.CompilerParams(vmem_limit_bytes=40 * 2**20),
        cost_estimate=pl.CostEstimate(
            flops=4 * count * C * width * keys,
            bytes_accessed=4 * count * C * width * 2,
            transcendentals=count * C * GROUP * keys,
        ),
        name=f"attend_{first}",
    )(*operands)


def local(queries, fresh_kv, kv_pool, page_holder, page_slot, cached_len, fresh_len):
    devices = lax.axis_size("dp")
    chips = devices // 2
    me = lax.axis_index("dp")
    flip = chips <= MOST_PERMUTES
    same_core = [[2 * i + core for i in range(chips)] for core in range(2)]
    mate_pool = lax.ppermute(kv_pool, "dp", [(i, i ^ 1) for i in range(devices)])
    asked = ask(me.reshape(1), page_holder, page_slot, chips)
    exchange = functools.partial(
        lax.all_to_all,
        axis_name="dp",
        split_axis=0,
        concat_axis=0,
        axis_index_groups=same_core,
        tiled=True,
    )
    wanted = exchange(asked)
    mine = (me // 2).reshape(1)
    gathered = gather_pages(mine, wanted, kv_pool, mate_pool, flip)
    order = (me if flip else me & 1).reshape(1)
    live = live_tokens(order, cached_len, page_holder, MP // devices)
    fresh_k, fresh_v = fresh_kv[0, :, 0], fresh_kv[0, :, 1]
    out = None
    for c, (first, count) in enumerate(CHUNKS):
        if flip:
            pieces = list(gathered[c * chips : (c + 1) * chips])
            for x in reversed(range(1, chips)):
                pairs = [(i, i ^ (2 * x)) for i in range(devices)]
                pieces[x] = lax.ppermute(pieces[x], "dp", pairs)
        else:
            pieces = [exchange(gathered[c])]
        tokens = pieces[0].shape[-3] * PAGE
        pieces = [p.reshape(p.shape[:-3] + (tokens, HD)) for p in pieces]
        out = attend(first, fresh_len, live, queries[0], fresh_k, fresh_v, pieces, out)
    return out[None]


def solution(mesh):
    return jax.shard_map(
        local,
        mesh=mesh,
        in_specs=(
            P(("groups", "dp"), None, None),
            P(("groups", "dp"), None, None, None),
            P(("groups", "dp"), None, None, None),
            P(("groups", "dp"), None),
            P(("groups", "dp"), None),
            P(("groups", "dp")),
            P(("groups", "dp")),
        ),
        out_specs=P(("groups", "dp"), None, None),
        check_vma=False,
    )
```

time: 103 us -> 89.5 us (0.87)
  the two profiles are of different devices: /device:TPU:0 before, /device:TPU:8 now
where the time goes in v2:
time: 89.5 us; the launch traced here: 89.2 us
  starting transfers between devices  30.7 us (34%)
  waiting for transfers between devices  28.7 us (32%)
  Pallas kernels  19.9 us (22%)
  local copies, waits for them, and re-layouts  8.61 us (10%)
  between operations  1.35 us (2%)
    ppermute x14, starting transfers between devices, local(): pieces[x] = lax.ppermute(pieces[x], 'dp', pairs)  24.4 us
    ppermute x14, waiting for transfers between devices, local(): pieces[x] = lax.ppermute(pieces[x], 'dp', pairs)  23.7 us
    pallas_call x2, Pallas kernels, attend(): pl.pallas_call(functools.partial(attend_kernel, parts=parts, heads=4), gr...  14.9 us
    unnamed x20, local copies, waits for them, and re-layouts  6.37 us
    all_to_all x1, starting transfers between devices, local(): wanted = exchange(asked)  6.25 us
    all_to_all x1, waiting for transfers between devices, local(): wanted = exchange(asked)  4.91 us
  transfers between devices with their start and end apart: 16, of which 6 were waited for; matrix products, arithmetic and copies ran while one was open for 3% of the time, Pallas kernels for 16%

profile of v2, /device:TPU:8, one launch (start us, length us, event | category | flops | bytes accessed | tf_op | source)
XLA Modules:
  0.0 89.2 jit_solution(926685278197131188)
XLA Ops:
  0.0 0.0 collective-permute-start
  0.0 1.6 %ask.1 = s32[8,1,128]{2,1,0:T(1,128)} custom-call(s32[1]{0:T(128)} %bitcast.order_ref.me_ref, s32[1,128]{1,0:T(1,128)} %holder_ref.3, s32[1,128]{1,0:T(1,128)} %slot_ref.1), custom_call_target="tpu_custom_call" | custom-call | tf_op jit(solution)/shard_map/ask/pallas_call | solution.py:47
  1.6 6.3 %all-to-all-start = ((s32[8,1,128]{2,1,0:T(1,128)}), s32[8,1,128]{2,1,0:T(1,128)S(1)}, u32[]{:S(2)}, u32[]{:S(2)}) async-start(s32[8,1,128]{2,1,0:T(1,128)} %ask.1), calls=%async_computation | async-start | bytes 8192 | tf_op jit(solution)/shard_map/all_to_all | solution.py:255
  7.9 4.9 %all-to-all-done.wanted_ref = s32[8,1,128]{2,1,0:T(1,128)S(1)} async-done(((s32[8,1,128]{2,1,0:T(1,128)}), s32[8,1,128]{2,1,0:T(1,128)S(1)}, u32[]{:S(2)}, u32[]{:S(2)}) %all-to-all-start) | async-done | bytes 4128 | tf_op jit(solution)/shard_map/all_to_all | solution.py:255
  12.8 0.0 collective-permute-done.mate_ref
  12.8 1.6 %copy-done = bf16[128,2,8,512]{3,2,1,0:T(8,128)(2,1)S(1)} copy-done((bf16[128,2,8,512]{3,2,1,0:T(8,128)(2,1)S(1)}, bf16[128,2,8,512]{3,2,1,0:T(8,128)(2,1)}, u32[]{:S(2)}) %copy-start) | copy-done | bytes 2097176
  14.4 1.7 %gather_pages.1 = (bf16[3,2,16,8,128]{4,3,2,1,0:T(8,128)(2,1)S(1)}, bf16[3,2,16,8,128]{4,3,2,1,0:T(8,128)(2,1)}, bf16[3,2,16,8,128]{4,3,2,1,0:T(8,128)(2,1)}, bf...) custom-call(s32[1]{0:T(128)} %bitcast.4.mine_ref, ...), custom_call_target="tpu_custom_call" | custom-call | bytes 8388608 | tf_op jit(solution)/shard_map/gather_pages/pallas_call | solution.py:124
  16.1 0.7 copy-done.3
  16.7 0.7 copy-done.4
  17.4 0.6 copy-done.5
  18.0 0.6 copy-done.6
  18.6 0.6 copy-done.7
  19.3 0.6 copy-done.8
  19.9 0.6 collective-permute-start.1
  20.5 1.4 %collective-permute-start.2 = (bf16[1,2,16,8,128]{4,3,2,1,0:T(8,128)(2,1)}, bf16[1,2,16,8,128]{4,3,2,1,0:T(8,128)(2,1)S(1)}, u32[]{:S(2)}, u32[]{:S(2)}) collective-permute-start(bf16[1,2,16,8,128]{4,3,2,1,0:T(8,128)(2,1)} %get-tuple-element.23), channel_id=1, source_target_pairs={{0,4},{1,5},{2,6},{3,7},{4,0},{5,1},{6,2},{7,3},{8,12},{9,13},{10,... | collective-permute-start | bytes 196616 | tf_op jit(solution)/shard_map/ppermute | solution.py:267
  21.9 1.5 %collective-permute-start.8 = (bf16[3,2,16,8,128]{4,3,2,1,0:T(8,128)(2,1)}, bf16[3,2,16,8,128]{4,3,2,1,0:T(8,128)(2,1)S(1)}, u32[]{:S(2)}, u32[]{:S(2)}) collective-permute-start(bf16[3,2,16,8,128]{4,3,2,1,0:T(8,128)(2,1)} %get-tuple-element.30), channel_id=1, source_target_pairs={{0,2},{1,3},{2,0},{3,1},{4,6},{5,7},{6,4},{7,5},{8,10},{9,11},{10,... | collective-permute-start | bytes 589832 | tf_op jit(solution)/shard_map/ppermute | solution.py:267
  23.4 0.5 collective-permute-start.9
  23.9 1.2 %fusion = (bf16[1,128,1,512]{3,2,1,0:T(2,128)(2,1)}, bf16[1,128,1,512]{3,2,1,0:T(2,128)(2,1)}) fusion(bf16[1,128,2,512]{3,2,1,0:T(2,128)(2,1)S(1)} %copy-done.9), kind=kLoop, calls=%fused_computation.2 | loop fusion | bytes 524288 | tf_op jit(solution)/shard_map/slice | solution.py:260
  26.4 1.7 %live_tokens.1.live_ref = bf16[1024,128]{1,0:T(8,128)(2,1)} custom-call(s32[1]{0:T(128)} %bitcast.order_ref.me_ref, s32[1]{0:T(128)S(6)} %copy.16.length_ref, s32[1,128]{1,0:T(1,128)} %holder_ref.3), custom_call_target="tpu_custom_call" | custom-call | tf_op jit(solution)/shard_map/live_tokens/pallas_call | solution.py:78
  28.1 1.5 %collective-permute-start.10 = (bf16[3,2,16,8,128]{4,3,2,1,0:T(8,128)(2,1)}, bf16[3,2,16,8,128]{4,3,2,1,0:T(8,128)(2,1)S(1)}, u32[]{:S(2)}, u32[]{:S(2)}) collective-permute-start(bf16[3,2,16,8,128]{4,3,2,1,0:T(8,128)(2,1)} %copy-done.4), channel_id=1, source_target_pairs={{0,6},{1,7},{2,4},{3,5},{4,2},{5,3},{6,0},{7,1},{8,14},{9,15},{10,... | collective-permute-start | bytes 589832 | tf_op jit(solution)/shard_map/ppermute | solution.py:267
  29.6 0.0 collective-permute-done.1
  29.6 0.6 collective-permute-start.11
  30.2 0.0 collective-permute-done.2
  30.2 3.3 %collective-permute-start.12 = (bf16[3,2,16,8,128]{4,3,2,1,0:T(8,128)(2,1)S(1)}, bf16[3,2,16,8,128]{4,3,2,1,0:T(8,128)(2,1)S(1)}, u32[]{:S(2)}, u32[]{:S(2)}) collective-permute-start(bf16[3,2,16,8,128]{4,3,2,1,0:T(8,128)(2,1)S(1)} %get-tuple-element.34), channel_id=1, source_target_pairs={{0,10},{1,11},{2,8},{3,9},{4,14},{5,15},{6,12},{7,13},{8,2},{9,3},... | collective-permute-start | bytes 589832 | tf_op jit(solution)/shard_map/ppermute | solution.py:267
  33.4 0.0 collective-permute-done.8
  33.4 0.0 collective-permute-start.13
  33.5 0.0 collective-permute-done.9
  33.5 2.0 %collective-permute-start.14 = (bf16[3,2,16,8,128]{4,3,2,1,0:T(8,128)(2,1)S(1)}, bf16[3,2,16,8,128]{4,3,2,1,0:T(8,128)(2,1)S(1)}, u32[]{:S(2)}, u32[]{:S(2)}) collective-permute-start(bf16[3,2,16,8,128]{4,3,2,1,0:T(8,128)(2,1)S(1)} %get-tuple-element.36), channel_id=1, source_target_pairs={{0,14},{1,15},{2,12},{3,13},{4,10},{5,11},{6,8},{7,9},{8,6},{9,7},... | collective-permute-start | bytes 589832 | tf_op jit(solution)/shard_map/ppermute | solution.py:267
  35.5 1.1 %copy_bitcast_fusion = (bf16[128,512]{1,0:T(8,128)(2,1)S(1)}, bf16[128,512]{1,0:T(8,128)(2,1)S(1)}) fusion(bf16[1,128,1,512]{3,2,1,0:T(2,128)(2,1)} %get-tuple-element.37, bf16[1,128,1,512]{3,2,1,0:T(2,128)(2,1)} %get-tuple-element.38), kind=kLoop, calls=%fused_computation | loop fusion | bytes 524288 | tf_op jit(solution)/shard_map/squeeze | solution.py:260
  36.5 0.6 collective-permute-done.10
  37.1 2.7 %collective-permute-start.3 = (bf16[1,2,16,8,128]{4,3,2,1,0:T(8,128)(2,1)}, bf16[1,2,16,8,128]{4,3,2,1,0:T(8,128)(2,1)S(1)}, u32[]{:S(2)}, u32[]{:S(2)}) collective-permute-start(bf16[1,2,16,8,128]{4,3,2,1,0:T(8,128)(2,1)} %copy-done.8), channel_id=1, source_target_pairs={{0,6},{1,7},{2,4},{3,5},{4,2},{5,3},{6,0},{7,1},{8,14},{9,15},{10,... | collective-permute-start | bytes 196616 | tf_op jit(solution)/shard_map/ppermute | solution.py:267
  39.9 12.6 %collective-permute-done.11 = bf16[3,2,16,8,128]{4,3,2,1,0:T(8,128)(2,1)S(1)} collective-permute-done((bf16[3,2,16,8,128]{4,3,2,1,0:T(8,128)(2,1)}, bf16[3,2,16,8,128]{4,3,2,1,0:T(8,128)(2,1)S(1)}, u32[]{:S(2)}, u32[]{:S(2)}) %collective-permute-start.11) | collective-permute-done | bytes 196640 | tf_op jit(solution)/shard_map/ppermute | solution.py:267
  52.5 3.3 %collective-permute-start.4 = (bf16[1,2,16,8,128]{4,3,2,1,0:T(8,128)(2,1)}, bf16[1,2,16,8,128]{4,3,2,1,0:T(8,128)(2,1)S(1)}, u32[]{:S(2)}, u32[]{:S(2)}) collective-permute-start(bf16[1,2,16,8,128]{4,3,2,1,0:T(8,128)(2,1)} %copy-done.7), channel_id=1, source_target_pairs={{0,8},{1,9},{2,10},{3,11},{4,12},{5,13},{6,14},{7,15},{8,0},{9,1},... | collective-permute-start | bytes 196616 | tf_op jit(solution)/shard_map/ppermute | solution.py:267
  55.8 2.8 %collective-permute-done.12 = bf16[3,2,16,8,128]{4,3,2,1,0:T(8,128)(2,1)S(1)} collective-permute-done((bf16[3,2,16,8,128]{4,3,2,1,0:T(8,128)(2,1)S(1)}, bf16[3,2,16,8,128]{4,3,2,1,0:T(8,128)(2,1)S(1)}, u32[]{:S(2)}, u32[]{:S(2)}) %collective-permute-start.12) | collective-permute-done | bytes 196640 | tf_op jit(solution)/shard_map/ppermute | solution.py:267
  58.5 4.4 %collective-permute-start.5 = (bf16[1,2,16,8,128]{4,3,2,1,0:T(8,128)(2,1)}, bf16[1,2,16,8,128]{4,3,2,1,0:T(8,128)(2,1)S(1)}, u32[]{:S(2)}, u32[]{:S(2)}) collective-permute-start(bf16[1,2,16,8,128]{4,3,2,1,0:T(8,128)(2,1)} %copy-done.6), channel_id=1, source_target_pairs={{0,10},{1,11},{2,8},{3,9},{4,14},{5,15},{6,12},{7,13},{8,2},{9,3},... | collective-permute-start | bytes 196616 | tf_op jit(solution)/shard_map/ppermute | solution.py:267
  63.0 2.5 %collective-permute-done.13 = bf16[3,2,16,8,128]{4,3,2,1,0:T(8,128)(2,1)S(1)} collective-permute-done((bf16[3,2,16,8,128]{4,3,2,1,0:T(8,128)(2,1)S(1)}, bf16[3,2,16,8,128]{4,3,2,1,0:T(8,128)(2,1)S(1)}, u32[]{:S(2)}, u32[]{:S(2)}) %collective-permute-start.13) | collective-permute-done | bytes 196640 | tf_op jit(solution)/shard_map/ppermute | solution.py:267
  65.5 1.3 %collective-permute-start.6 = (bf16[1,2,16,8,128]{4,3,2,1,0:T(8,128)(2,1)}, bf16[1,2,16,8,128]{4,3,2,1,0:T(8,128)(2,1)S(1)}, u32[]{:S(2)}, u32[]{:S(2)}) collective-permute-start(bf16[1,2,16,8,128]{4,3,2,1,0:T(8,128)(2,1)} %copy-done.5), channel_id=1, source_target_pairs={{0,12},{1,13},{2,14},{3,15},{4,8},{5,9},{6,10},{7,11},{8,4},{9,5},... | collective-permute-start | bytes 196616 | tf_op jit(solution)/shard_map/ppermute | solution.py:267
  66.8 5.2 %collective-permute-done.14 = bf16[3,2,16,8,128]{4,3,2,1,0:T(8,128)(2,1)S(1)} collective-permute-done((bf16[3,2,16,8,128]{4,3,2,1,0:T(8,128)(2,1)S(1)}, bf16[3,2,16,8,128]{4,3,2,1,0:T(8,128)(2,1)S(1)}, u32[]{:S(2)}, u32[]{:S(2)}) %collective-permute-start.14) | collective-permute-done | bytes 196640 | tf_op jit(solution)/shard_map/ppermute | solution.py:267
  72.0 1.3 %collective-permute-start.7 = (bf16[1,2,16,8,128]{4,3,2,1,0:T(8,128)(2,1)S(1)}, bf16[1,2,16,8,128]{4,3,2,1,0:T(8,128)(2,1)S(1)}, u32[]{:S(2)}, u32[]{:S(2)}) collective-permute-start(bf16[1,2,16,8,128]{4,3,2,1,0:T(8,128)(2,1)S(1)} %get-tuple-element.28), channel_id=1, source_target_pairs={{0,14},{1,15},{2,12},{3,13},{4,10},{5,11},{6,8},{7,9},{8,6},{9,7},... | collective-permute-start | bytes 196616 | tf_op jit(solution)/shard_map/ppermute | solution.py:267
  73.3 0.0 copy-done.1
  73.3 0.9 %copy-done.2 = bf16[1024,128]{1,0:T(8,128)(2,1)S(1)} copy-done((bf16[1024,128]{1,0:T(8,128)(2,1)S(1)}, bf16[1024,128]{1,0:T(8,128)(2,1)}, u32[]{:S(2)}) %copy-start.2) | copy-done | bytes 262168
  74.3 10.8 %attend_0.1.rest_8_ = bf16[128,8192]{1,0:T(8,128)(2,1)} custom-call(s32[1]{0:T(128)S(6)} %copy.17.filled_ref, bf16[1024,128]{1,0:T(8,128)(2,1)S(1)} %copy-done.2, bf16[128,8192]{1,0:T(8,128)(2,1)S(1)} %bitcast.24, bf16[128,512]{1,0:T(8,128)(2,1)S(1)} %get-tuple-element.40.fk_ref, bf16[128,512]{1,0:T(8,128)(2,1)S(1)} %get-tuple-element.39.fv_ref, ...), custom_call_target="tpu_custom_call" | custom-call | flops 3623878656 | bytes 6291456 | tf_op jit(solution)/shard_map/attend_0/pallas_call | solution.py:218
  85.0 0.0 collective-permute-done.3
  85.1 0.0 collective-permute-done.4
  85.1 0.0 collective-permute-done.5
  85.1 0.0 collective-permute-done.6
  85.1 0.0 collective-permute-done.7
  85.1 4.1 %attend_3.1 = bf16[128,8192]{1,0:T(8,128)(2,1)} custom-call(s32[1]{0:T(128)S(6)} %copy.17.filled_ref, bf16[1024,128]{1,0:T(8,128)(2,1)S(1)} %copy-done.2, bf16[128,8192]{1,0:T(8,128)(2,1)S(1)} %bitcast.25, bf16[128,512]{1,0:T(8,128)(2,1)S(1)} %get-tuple-element.40.fk_ref, ...), custom_call_target="tpu_custom_call", output_to_operand_aliasing={{}: (13, {})} | custom-call | flops 1207959552 | bytes 2097152 | tf_op jit(solution)/shard_map/attend_3/pallas_call | solution.py:218
  (11 shorter events, 0.0 us)
Async XLA Ops:
  0.0 12.8 %collective-permute-start = (bf16[128,2,8,512]{3,2,1,0:T(8,128)(2,1)}, bf16[128,2,8,512]{3,2,1,0:T(8,128)(2,1)S(1)}, u32[]{:S(2)}, u32[]{:S(2)}) collective-permute-start(bf16[128,2,8,512]{3,2,1,0:T(8,128)(2,1)} %own_ref.1), channel_id=1, source_target_pairs={{0,1},{1,0},{2,3},{3,2},{4,5},{5,4},{6,7},{7,6},{8,9},{9,8},{10,11... | collective-permute-start | bytes 6291464 | tf_op jit(solution)/shard_map/ppermute | solution.py:245
  1.6 11.2 %all-to-all-start = ((s32[8,1,128]{2,1,0:T(1,128)}), s32[8,1,128]{2,1,0:T(1,128)S(1)}, u32[]{:S(2)}, u32[]{:S(2)}) async-start(s32[8,1,128]{2,1,0:T(1,128)} %ask.1), calls=%async_computation | async-start | bytes 8192 | tf_op jit(solution)/shard_map/all_to_all | solution.py:255
  12.8 1.6 %copy-start = (bf16[128,2,8,512]{3,2,1,0:T(8,128)(2,1)S(1)}, bf16[128,2,8,512]{3,2,1,0:T(8,128)(2,1)}, u32[]{:S(2)}) copy-start(bf16[128,2,8,512]{3,2,1,0:T(8,128)(2,1)} %own_ref.1) | copy-start | bytes 6291460
  14.4 9.6 %copy-start.9 = (bf16[1,128,2,512]{3,2,1,0:T(2,128)(2,1)S(1)}, bf16[1,128,2,512]{3,2,1,0:T(2,128)(2,1)}, u32[]{:S(2)}) copy-start(bf16[1,128,2,512]{3,2,1,0:T(2,128)(2,1)} %param.8) | copy-start | bytes 786436
  16.1 0.7 copy-start.3
  16.7 0.7 copy-start.4
  17.4 0.6 copy-start.5
  18.0 0.6 copy-start.6
  18.6 0.6 copy-start.7
  19.3 0.6 copy-start.8
  19.9 53.4 %copy-start.1 = (bf16[1,128,8192]{2,1,0:T(8,128)(2,1)S(1)}, bf16[1,128,8192]{2,1,0:T(8,128)(2,1)}, u32[]{:S(2)}) copy-start(bf16[1,128,8192]{2,1,0:T(8,128)(2,1)} %param.7) | copy-start | bytes 6291460
  19.9 9.7 %collective-permute-start.1 = (bf16[1,2,16,8,128]{4,3,2,1,0:T(8,128)(2,1)}, bf16[1,2,16,8,128]{4,3,2,1,0:T(8,128)(2,1)S(1)}, u32[]{:S(2)}, u32[]{:S(2)}) collective-permute-start(bf16[1,2,16,8,128]{4,3,2,1,0:T(8,128)(2,1)} %get-tuple-element.22), channel_id=1, source_target_pairs={{0,2},{1,3},{2,0},{3,1},{4,6},{5,7},{6,4},{7,5},{8,10},{9,11},{10,... | collective-permute-start | bytes 196616 | tf_op jit(solution)/shard_map/ppermute | solution.py:267
  20.5 9.7 %collective-permute-start.2 = (bf16[1,2,16,8,128]{4,3,2,1,0:T(8,128)(2,1)}, bf16[1,2,16,8,128]{4,3,2,1,0:T(8,128)(2,1)S(1)}, u32[]{:S(2)}, u32[]{:S(2)}) collective-permute-start(bf16[1,2,16,8,128]{4,3,2,1,0:T(8,128)(2,1)} %get-tuple-element.23), channel_id=1, source_target_pairs={{0,4},{1,5},{2,6},{3,7},{4,0},{5,1},{6,2},{7,3},{8,12},{9,13},{10,... | collective-permute-start | bytes 196616 | tf_op jit(solution)/shard_map/ppermute | solution.py:267
  21.9 11.5 %collective-permute-start.8 = (bf16[3,2,16,8,128]{4,3,2,1,0:T(8,128)(2,1)}, bf16[3,2,16,8,128]{4,3,2,1,0:T(8,128)(2,1)S(1)}, u32[]{:S(2)}, u32[]{:S(2)}) collective-permute-start(bf16[3,2,16,8,128]{4,3,2,1,0:T(8,128)(2,1)} %get-tuple-element.30), channel_id=1, source_target_pairs={{0,2},{1,3},{2,0},{3,1},{4,6},{5,7},{6,4},{7,5},{8,10},{9,11},{10,... | collective-permute-start | bytes 589832 | tf_op jit(solution)/shard_map/ppermute | solution.py:267
  23.4 10.1 %collective-permute-start.9 = (bf16[3,2,16,8,128]{4,3,2,1,0:T(8,128)(2,1)}, bf16[3,2,16,8,128]{4,3,2,1,0:T(8,128)(2,1)S(1)}, u32[]{:S(2)}, u32[]{:S(2)}) collective-permute-start(bf16[3,2,16,8,128]{4,3,2,1,0:T(8,128)(2,1)} %get-tuple-element.31), channel_id=1, source_target_pairs={{0,4},{1,5},{2,6},{3,7},{4,0},{5,1},{6,2},{7,3},{8,12},{9,13},{10,... | collective-permute-start | bytes 589832 | tf_op jit(solution)/shard_map/ppermute | solution.py:267
  28.1 9.0 %collective-permute-start.10 = (bf16[3,2,16,8,128]{4,3,2,1,0:T(8,128)(2,1)}, bf16[3,2,16,8,128]{4,3,2,1,0:T(8,128)(2,1)S(1)}, u32[]{:S(2)}, u32[]{:S(2)}) collective-permute-start(bf16[3,2,16,8,128]{4,3,2,1,0:T(8,128)(2,1)} %copy-done.4), channel_id=1, source_target_pairs={{0,6},{1,7},{2,4},{3,5},{4,2},{5,3},{6,0},{7,1},{8,14},{9,15},{10,... | collective-permute-start | bytes 589832 | tf_op jit(solution)/shard_map/ppermute | solution.py:267
  29.6 22.9 %collective-permute-start.11 = (bf16[3,2,16,8,128]{4,3,2,1,0:T(8,128)(2,1)}, bf16[3,2,16,8,128]{4,3,2,1,0:T(8,128)(2,1)S(1)}, u32[]{:S(2)}, u32[]{:S(2)}) collective-permute-start(bf16[3,2,16,8,128]{4,3,2,1,0:T(8,128)(2,1)} %copy-done.3), channel_id=1, source_target_pairs={{0,8},{1,9},{2,10},{3,11},{4,12},{5,13},{6,14},{7,15},{8,0},{9,1},... | collective-permute-start | bytes 589832 | tf_op jit(solution)/shard_map/ppermute | solution.py:267
  30.2 28.4 %collective-permute-start.12 = (bf16[3,2,16,8,128]{4,3,2,1,0:T(8,128)(2,1)S(1)}, bf16[3,2,16,8,128]{4,3,2,1,0:T(8,128)(2,1)S(1)}, u32[]{:S(2)}, u32[]{:S(2)}) collective-permute-start(bf16[3,2,16,8,128]{4,3,2,1,0:T(8,128)(2,1)S(1)} %get-tuple-element.34), channel_id=1, source_target_pairs={{0,10},{1,11},{2,8},{3,9},{4,14},{5,15},{6,12},{7,13},{8,2},{9,3},... | collective-permute-start | bytes 589832 | tf_op jit(solution)/shard_map/ppermute | solution.py:267
  33.4 32.0 %collective-permute-start.13 = (bf16[3,2,16,8,128]{4,3,2,1,0:T(8,128)(2,1)S(1)}, bf16[3,2,16,8,128]{4,3,2,1,0:T(8,128)(2,1)S(1)}, u32[]{:S(2)}, u32[]{:S(2)}) collective-permute-start(bf16[3,2,16,8,128]{4,3,2,1,0:T(8,128)(2,1)S(1)} %get-tuple-element.35), channel_id=1, source_target_pairs={{0,12},{1,13},{2,14},{3,15},{4,8},{5,9},{6,10},{7,11},{8,4},{9,5},... | collective-permute-start | bytes 589832 | tf_op jit(solution)/shard_map/ppermute | solution.py:267
  33.5 38.5 %collective-permute-start.14 = (bf16[3,2,16,8,128]{4,3,2,1,0:T(8,128)(2,1)S(1)}, bf16[3,2,16,8,128]{4,3,2,1,0:T(8,128)(2,1)S(1)}, u32[]{:S(2)}, u32[]{:S(2)}) collective-permute-start(bf16[3,2,16,8,128]{4,3,2,1,0:T(8,128)(2,1)S(1)} %get-tuple-element.36), channel_id=1, source_target_pairs={{0,14},{1,15},{2,12},{3,13},{4,10},{5,11},{6,8},{7,9},{8,6},{9,7},... | collective-permute-start | bytes 589832 | tf_op jit(solution)/shard_map/ppermute | solution.py:267
  37.1 47.9 %collective-permute-start.3 = (bf16[1,2,16,8,128]{4,3,2,1,0:T(8,128)(2,1)}, bf16[1,2,16,8,128]{4,3,2,1,0:T(8,128)(2,1)S(1)}, u32[]{:S(2)}, u32[]{:S(2)}) collective-permute-start(bf16[1,2,16,8,128]{4,3,2,1,0:T(8,128)(2,1)} %copy-done.8), channel_id=1, source_target_pairs={{0,6},{1,7},{2,4},{3,5},{4,2},{5,3},{6,0},{7,1},{8,14},{9,15},{10,... | collective-permute-start | bytes 196616 | tf_op jit(solution)/shard_map/ppermute | solution.py:267
  52.5 32.6 %collective-permute-start.4 = (bf16[1,2,16,8,128]{4,3,2,1,0:T(8,128)(2,1)}, bf16[1,2,16,8,128]{4,3,2,1,0:T(8,128)(2,1)S(1)}, u32[]{:S(2)}, u32[]{:S(2)}) collective-permute-start(bf16[1,2,16,8,128]{4,3,2,1,0:T(8,128)(2,1)} %copy-done.7), channel_id=1, source_target_pairs={{0,8},{1,9},{2,10},{3,11},{4,12},{5,13},{6,14},{7,15},{8,0},{9,1},... | collective-permute-start | bytes 196616 | tf_op jit(solution)/shard_map/ppermute | solution.py:267
  58.5 26.5 %collective-permute-start.5 = (bf16[1,2,16,8,128]{4,3,2,1,0:T(8,128)(2,1)}, bf16[1,2,16,8,128]{4,3,2,1,0:T(8,128)(2,1)S(1)}, u32[]{:S(2)}, u32[]{:S(2)}) collective-permute-start(bf16[1,2,16,8,128]{4,3,2,1,0:T(8,128)(2,1)} %copy-done.6), channel_id=1, source_target_pairs={{0,10},{1,11},{2,8},{3,9},{4,14},{5,15},{6,12},{7,13},{8,2},{9,3},... | collective-permute-start | bytes 196616 | tf_op jit(solution)/shard_map/ppermute | solution.py:267
  65.5 19.6 %collective-permute-start.6 = (bf16[1,2,16,8,128]{4,3,2,1,0:T(8,128)(2,1)}, bf16[1,2,16,8,128]{4,3,2,1,0:T(8,128)(2,1)S(1)}, u32[]{:S(2)}, u32[]{:S(2)}) collective-permute-start(bf16[1,2,16,8,128]{4,3,2,1,0:T(8,128)(2,1)} %copy-done.5), channel_id=1, source_target_pairs={{0,12},{1,13},{2,14},{3,15},{4,8},{5,9},{6,10},{7,11},{8,4},{9,5},... | collective-permute-start | bytes 196616 | tf_op jit(solution)/shard_map/ppermute | solution.py:267
  72.0 13.1 %collective-permute-start.7 = (bf16[1,2,16,8,128]{4,3,2,1,0:T(8,128)(2,1)S(1)}, bf16[1,2,16,8,128]{4,3,2,1,0:T(8,128)(2,1)S(1)}, u32[]{:S(2)}, u32[]{:S(2)}) collective-permute-start(bf16[1,2,16,8,128]{4,3,2,1,0:T(8,128)(2,1)S(1)} %get-tuple-element.28), channel_id=1, source_target_pairs={{0,14},{1,15},{2,12},{3,13},{4,10},{5,11},{6,8},{7,9},{8,6},{9,7},... | collective-permute-start | bytes 196616 | tf_op jit(solution)/shard_map/ppermute | solution.py:267
  73.3 1.0 %copy-start.2 = (bf16[1024,128]{1,0:T(8,128)(2,1)S(1)}, bf16[1024,128]{1,0:T(8,128)(2,1)}, u32[]{:S(2)}) copy-start(bf16[1024,128]{1,0:T(8,128)(2,1)} %live_tokens.1.live_ref) | copy-start | bytes 786436

commit v3 on v2

v3 whole, which is shorter than its diff:
```python
import functools

import jax
import jax.numpy as jnp
from jax import lax
from jax.experimental import pallas as pl
from jax.experimental.pallas import tpu as pltpu
from jax.sharding import PartitionSpec as P

H = 64
KVH = 4
HD = 128
PAGE = 8
MP = 128
C = 128
GROUP = H // KVH
LOG2E = 1.4426950408889634
NEG = -1e30
CHUNKS = ((0, 2), (2, 2))
MOST_PERMUTES = 8


def ask_kernel(me_ref, holder_ref, slot_ref, asked_ref):
    chips = asked_ref.shape[0]
    capacity = MP // (2 * chips)
    core = me_ref[0] & 1
    square = (MP, MP)
    row = lax.broadcasted_iota(jnp.int32, square, 0)
    lane = lax.broadcasted_iota(jnp.int32, square, 1)
    holder = jnp.broadcast_to(holder_ref[...], square)
    same = (holder.T == holder) & (row < lane)
    rank = jnp.sum(same.astype(jnp.int32), axis=0, keepdims=True)
    low = (holder_ref[...] & 1 ^ core) * capacity + rank
    packed = jnp.broadcast_to(low * MP + slot_ref[...], square).T
    slots = jnp.where(packed // MP == lane, packed % MP, 0)
    chip = lax.broadcasted_iota(jnp.int32, (chips, MP), 0)
    of_chip = jnp.broadcast_to(holder_ref[...] >> 1, (chips, MP)) == chip
    asked = jnp.dot(
        of_chip.astype(jnp.float32).astype(jnp.bfloat16),
        slots.astype(jnp.float32).astype(jnp.bfloat16),
        preferred_element_type=jnp.float32,
    )
    asked_ref[...] = asked.astype(jnp.int32).reshape(chips, 1, MP)


def ask(me, page_holder, page_slot, chips):
    return pl.pallas_call(
        ask_kernel,
        out_shape=jax.ShapeDtypeStruct((chips, 1, MP), jnp.int32),
        in_specs=[
            pl.BlockSpec(memory_space=pltpu.SMEM),
            pl.BlockSpec(memory_space=pltpu.VMEM),
            pl.BlockSpec(memory_space=pltpu.VMEM),
        ],
        out_specs=pl.BlockSpec(memory_space=pltpu.VMEM),
        name="ask",
    )(me, page_holder, page_slot)


def live_kernel(order_ref, length_ref, holder_ref, live_ref, *, capacity):
    square = (MP, MP)
    row = lax.broadcasted_iota(jnp.int32, square, 0)
    lane = lax.broadcasted_iota(jnp.int32, square, 1)
    holder = jnp.broadcast_to(holder_ref[...], square)
    same = (holder.T == holder) & (row < lane)
    rank = jnp.sum(same.astype(jnp.int32), axis=0, keepdims=True)
    place = (holder_ref[...] ^ order_ref[0]) * capacity + rank
    hits = jnp.broadcast_to(place, square) == row
    page = jnp.sum(jnp.where(hits, lane, 0), axis=1, keepdims=True)
    page = jnp.broadcast_to(page, square)
    shape = (MP, PAGE, HD)
    token = page[:, None, :] * PAGE + lax.broadcasted_iota(jnp.int32, shape, 1)
    live = jnp.where(token < length_ref[0], 1.0, 0.0)
    live_ref[...] = live.reshape(MP * PAGE, HD).astype(live_ref.dtype)


def live_tokens(order, cached_len, page_holder, capacity):
    return pl.pallas_call(
        functools.partial(live_kernel, capacity=capacity),
        out_shape=pltpu.VMEM((MP * PAGE, HD), jnp.bfloat16),
        in_specs=[
            pl.BlockSpec(memory_space=pltpu.SMEM),
            pl.BlockSpec(memory_space=pltpu.SMEM),
            pl.BlockSpec(memory_space=pltpu.VMEM),
        ],
        out_specs=pl.BlockSpec(memory_space=pltpu.VMEM),
        name="live_tokens",
    )(order, cached_len, page_holder)


def gather_kernel(mine_ref, wanted_ref, own_ref, mate_ref, *rest, pieces):
    out_refs = rest[: len(pieces)]
    held_refs = rest[len(pieces) : -2]
    load_sem, store_sem = rest[-2:]
    chips = wanted_ref.shape[0]
    capacity = out_refs[0].shape[-3] // 2
    whole = pieces[0][0] is None
    places = range(chips)[::-1]

    def parts_of(x):
        return [i for i, piece in enumerate(pieces) if whole or piece[0] == x]

    def place_of(i, x, asker, n):
        held_ref = held_refs[i].at[asker] if whole else held_refs[i]
        return held_ref.at[:, n]

    def columns(i):
        _, first, count = pieces[i]
        return pl.ds(first * HD, count * HD)

    def loads(x, asker):
        for n in range(capacity):
            for i in parts_of(x):
                yield pltpu.make_async_copy(
                    own_ref.at[wanted_ref[asker, 0, n], :, :, columns(i)],
                    place_of(i, x, asker, n),
                    load_sem.at[0 if whole else x],
                )

    def copy(x, asker):
        for n in range(capacity, 2 * capacity):
            page_ref = mate_ref.at[wanted_ref[asker, 0, n]]
            for i in parts_of(x):
                place_of(i, x, asker, n)[...] = page_ref[:, :, columns(i)]

    def store(i):
        return pltpu.make_async_copy(held_refs[i], out_refs[i], store_sem.at[i])

    if whole:

        @pl.loop(0, chips)
        def _(x):
            for load in loads(None, x):
                load.start()
            copy(None, x)
            for load in loads(None, x):
                load.wait()

        for i in range(len(pieces)):
            store(i).start()
    else:
        for x in places:
            for load in loads(x, mine_ref[0] ^ x):
                load.start()
        for x in places:
            copy(x, mine_ref[0] ^ x)
            for i in parts_of(x):
                half = held_refs[i].at[:, pl.ds(0, capacity)]
                pltpu.make_async_copy(half, half, load_sem.at[x]).wait()
            for i in parts_of(x):
                store(i).start()
    for i in range(len(pieces)):
        store(i).wait()


def gather_pages(mine, wanted, own, mate, pieces):
    chips = wanted.shape[0]
    shapes = []
    for x, _, count in pieces:
        shape = (2, MP // chips, PAGE, count * HD)
        shapes.append((chips,) + shape if x is None else shape)
    return pl.pallas_call(
        functools.partial(gather_kernel, pieces=tuple(pieces)),
        out_shape=[pltpu.HBM(shape, own.dtype) for shape in shapes],
        in_specs=[
            pl.BlockSpec(memory_space=pltpu.SMEM),
            pl.BlockSpec(memory_space=pltpu.SMEM),
            pl.BlockSpec(memory_space=pltpu.HBM),
            pl.BlockSpec(memory_space=pltpu.VMEM),
        ],
        out_specs=[pl.BlockSpec(memory_space=pltpu.HBM)] * len(pieces),
        scratch_shapes=[pltpu.VMEM(shape, own.dtype) for shape in shapes]
        + [
            pltpu.SemaphoreType.DMA((chips,)),
            pltpu.SemaphoreType.DMA((len(shapes),)),
        ],
        compiler_params=pltpu.CompilerParams(vmem_limit_bytes=24 * 2**20),
        cost_estimate=pl.CostEstimate(
            flops=0, bytes_accessed=2 * own.size * 2, transcendentals=0
        ),
        name="gather_pages",
    )(mine, wanted, own, mate)


def hold_back(pieces, after):
    anywhere = pl.BlockSpec(memory_space=pl.ANY)
    return pl.pallas_call(
        lambda *refs: None,
        out_shape=[pltpu.HBM(p.shape, p.dtype) for p in pieces],
        in_specs=[pl.BlockSpec(memory_space=pltpu.HBM)] * len(pieces)
        + [anywhere] * len(after),
        out_specs=[pl.BlockSpec(memory_space=pltpu.HBM)] * len(pieces),
        input_output_aliases={i: i for i in range(len(pieces))},
        name="hold_back",
    )(*pieces, *after)


def attend_kernel(filled_ref, live_ref, q_ref, fk_ref, fv_ref, *rest, parts, heads, fresh, earlier):
    piece_refs = rest[:parts]
    k_ref, v_ref = rest[-2:]
    rest = rest[parts:-2]
    if earlier:
        old_ref, stats_ref = rest[:2]
        o_ref = rest[-1]
    elif len(rest) == 2 and rest[0].dtype == jnp.float32:
        o_ref, stats_ref = rest
    else:
        o_ref = rest[-1]
    last = o_ref.dtype != jnp.float32
    scale = HD**-0.5 * LOG2E
    rows = heads * C
    tokens = piece_refs[0].shape[-2]
    cached = parts * tokens
    fk = fk_ref[...]
    for p in range(parts):
        at = slice(p * tokens, (p + 1) * tokens)
        live = live_ref[at]
        k_ref[at] = jnp.where(live > 0, piece_refs[p][0], fk[:1])
        v_ref[at, :HD] = jnp.where(live > 0, piece_refs[p][1], jnp.zeros_like(live))
        v_ref[at, HD:] = live
    if fresh:
        k_ref[cached:] = fk
        v_ref[cached:, :HD] = fv_ref[...]
        v_ref[cached:, HD:] = jnp.ones_like(fk)
    nt = (((1,), (1,)), ((), ()))
    token = lax.rem(lax.broadcasted_iota(jnp.int32, (rows, C), 0), C)
    lane = lax.broadcasted_iota(jnp.int32, (C, HD), 1)
    causal = lax.broadcasted_iota(jnp.int32, (rows, C), 1) <= token
    filled = token < filled_ref[0]
    if earlier:
        old_stats = stats_ref[...]
    elif not last:
        stats = jnp.zeros((C, HD), jnp.float32)
    for g in range(0, GROUP, heads):
        many = range(g, g + heads)
        cols = [slice(i * HD, (i + 1) * HD) for i in many]
        q = jnp.concatenate([q_ref[:, c] for c in cols], axis=0)
        s = lax.dot_general(q, k_ref[...], nt, preferred_element_type=jnp.float32)
        s1 = s[:, :cached]
        top = jnp.max(s1, axis=1, keepdims=True)
        if fresh:
            s2 = jnp.where(causal, s[:, cached:], NEG)
            top = jnp.maximum(top, jnp.max(s2, axis=1, keepdims=True))
        if earlier:
            old_top = jnp.concatenate([old_stats[:, i : i + 1] for i in many], axis=0)
            old_sum = jnp.concatenate(
                [old_stats[:, GROUP + i : GROUP + i + 1] for i in many], axis=0
            )
            top = jnp.maximum(top, old_top)
        p = jnp.exp2((s1 - top) * scale).astype(jnp.bfloat16)
        if fresh:
            p2 = jnp.exp2((s2 - top) * scale).astype(jnp.bfloat16)
            p = jnp.concatenate([p, p2], axis=1)
        o = jnp.dot(p, v_ref[...], preferred_element_type=jnp.float32)
        o, total = o[:, :HD], o[:, HD:]
        if earlier:
            share = jnp.exp2((old_top - top) * scale)
            old = jnp.concatenate([old_ref[:, c] for c in cols], axis=0)
            o = o + share * old
            total = total + share * old_sum
        if last:
            o = jnp.where(filled, o / total, 0.0).astype(o_ref.dtype)
        for k, i in enumerate(many):
            at = slice(k * C, (k + 1) * C)
            o_ref[:, cols[k]] = o[at]
            if not last:
                stats = jnp.where(lane == i, top[at], stats)
                stats = jnp.where(lane == GROUP + i, total[at], stats)
    if not last:
        stats_ref[...] = stats


def attend(first, count, filled, live, queries, fresh_k, fresh_v, pieces, rows, out=None, earlier=None, fresh=True, last=True):
    width = GROUP * HD
    tokens = sum(
        p.shape[-2] * (p.shape[0] if p.ndim == 4 else 1) for p, start in pieces
    )
    wide = pl.BlockSpec((C, width), lambda h: (0, h + first))
    narrow = pl.BlockSpec((C, HD), lambda h: (0, h + first))
    operands = [filled, live, queries, fresh_k, fresh_v]
    in_specs = [
        pl.BlockSpec(memory_space=pltpu.SMEM),
        pl.BlockSpec((tokens, HD), lambda h: (rows, 0)),
        wide,
        narrow,
        narrow,
    ]
    parts = 0
    for piece, start in pieces:
        low = first - start
        for i in range(piece.shape[0] if piece.ndim == 4 else 1):
            operands.append(piece)
            lead = (i,) if piece.ndim == 4 else ()
            block = (None,) * len(lead) + piece.shape[-3:-1] + (HD,)
            in_specs.append(
                pl.BlockSpec(block, lambda h, l=lead, d=low: l + (0, 0, h + d))
            )
            parts += 1
    if earlier is not None:
        operands += earlier
        in_specs += [wide, narrow]
    aliases = {}
    if out is not None:
        operands.append(out)
        in_specs.append(pl.BlockSpec(memory_space=pl.ANY))
        aliases = {len(operands) - 1: 0}
    if last:
        out_shape = jax.ShapeDtypeStruct((C, H * HD), jnp.bfloat16)
        out_specs = wide
    else:
        out_shape = [
            jax.ShapeDtypeStruct((C, H * HD), jnp.float32),
            jax.ShapeDtypeStruct((C, KVH * HD), jnp.float32),
        ]
        out_specs = [wide, narrow]
    keys = tokens + (C if fresh else 0)
    return pl.pallas_call(
        functools.partial(
            attend_kernel,
            parts=parts,
            heads=4,
            fresh=fresh,
            earlier=earlier is not None,
        ),
        grid=(count,),
        out_shape=out_shape,
        in_specs=in_specs,
        out_specs=out_specs,
        scratch_shapes=[
            pltpu.VMEM((keys, HD), jnp.bfloat16),
            pltpu.VMEM((keys, 2 * HD), jnp.bfloat16),
        ],
        input_output_aliases=aliases,
        compiler_params=pltpu.CompilerParams(vmem_limit_bytes=32 * 2**20),
        cost_estimate=pl.CostEstimate(
            flops=4 * count * C * width * keys,
            bytes_accessed=4 * count * C * width * 2,
            transcendentals=count * C * GROUP * keys,
        ),
        name=f"attend_{first}_{rows}",
    )(*operands)


def local(queries, fresh_kv, kv_pool, page_holder, page_slot, cached_len, fresh_len):
    devices = lax.axis_size("dp")
    chips = devices // 2
    me = lax.axis_index("dp")
    flip = chips <= MOST_PERMUTES
    same_core = [[2 * i + core for i in range(chips)] for core in range(2)]
    mate_pool = lax.ppermute(kv_pool, "dp", [(i, i ^ 1) for i in range(devices)])
    asked = ask(me.reshape(1), page_holder, page_slot, chips)
    exchange = functools.partial(
        lax.all_to_all,
        axis_name="dp",
        split_axis=0,
        concat_axis=0,
        axis_index_groups=same_core,
        tiled=True,
    )
    wanted = exchange(asked)
    own_pool = pltpu.with_memory_space_constraint(kv_pool, pltpu.HBM)
    mate_pool = pltpu.with_memory_space_constraint(mate_pool, pltpu.VMEM)
    mine = (me >> 1).reshape(1)
    gather = functools.partial(gather_pages, mine, wanted, own_pool, mate_pool)
    order = (me if flip else me & 1).reshape(1)
    live = live_tokens(order, cached_len, page_holder, MP // devices)
    fresh_k, fresh_v = fresh_kv[0, :, 0], fresh_kv[0, :, 1]

    def attend_some(first, count, pieces, *args, **kwargs):
        pieces = [
            (p.reshape(p.shape[:-3] + (-1, p.shape[-1])), start) for p, start in pieces
        ]
        return attend(
            first, count, fresh_len, live, queries[0], fresh_k, fresh_v, pieces, *args, **kwargs
        )

    out = None
    if not flip:
        sent = gather([(None, first, count) for first, count in CHUNKS])
        for (first, count), piece in zip(CHUNKS, sent):
            out = attend_some(first, count, [(exchange(piece), first)], 0, out)
        return out[None]

    def swap(piece, x):
        return lax.ppermute(piece, "dp", [(i, i ^ 2 * x) for i in range(devices)])

    near, far = range(chips // 2), range(chips // 2, chips)
    sent = gather(
        [(x, 0, KVH) for x in near]
        + [(x, first, count) for first, count in CHUNKS for x in far]
    )
    close = [(sent[x] if x == 0 else swap(sent[x], x), 0) for x in near]
    earlier = attend_some(0, KVH, close, 0, last=False)
    arrived = []
    for c, (first, count) in enumerate(CHUNKS):
        batch = sent[len(near) + c * len(far) : len(near) + (c + 1) * len(far)]
        if c > 0:
            batch = hold_back(batch, arrived[:2])
        arrived = [swap(piece, x) for piece, x in zip(batch, far)]
        pieces = [(piece, first) for piece in arrived]
        out = attend_some(
            first, count, pieces, 1, out, earlier=earlier, fresh=False
        )
    return out[None]


def solution(mesh):
    return jax.shard_map(
        local,
        mesh=mesh,
        in_specs=(
            P(("groups", "dp"), None, None),
            P(("groups", "dp"), None, None, None),
            P(("groups", "dp"), None, None, None),
            P(("groups", "dp"), None),
            P(("groups", "dp"), None),
            P(("groups", "dp")),
            P(("groups", "dp")),
        ),
        out_specs=P(("groups", "dp"), None, None),
        check_vma=False,
    )
```

time: 89.5 us -> 76.5 us (0.85)
  the two profiles are of different devices: /device:TPU:8 before, /device:TPU:0 now
where the time goes in v3:
time: 76.5 us; the launch traced here: 76.2 us
  Pallas kernels  31.4 us (41%)
  starting transfers between devices  25 us (33%)
  waiting for transfers between devices  16.1 us (21%)
  local copies, waits for them, and re-layouts  2.25 us (3%)
  between operations  1.4 us (2%)
    pallas_call x3, Pallas kernels, attend(): pl.pallas_call(functools.partial(attend_kernel, parts=parts, heads=4, fre...  25.8 us
    ppermute x11, starting transfers between devices, swap(): return lax.ppermute(piece, 'dp', [(i, i ^ 2 * x) for i in range(devices)])  17.8 us
    ppermute x11, waiting for transfers between devices, swap(): return lax.ppermute(piece, 'dp', [(i, i ^ 2 * x) for i in range(devices)])  9.75 us
    all_to_all x1, starting transfers between devices, local(): wanted = exchange(asked)  6.8 us
    all_to_all x1, waiting for transfers between devices, local(): wanted = exchange(asked)  6.39 us
    pallas_call x1, Pallas kernels, gather_pages(): pl.pallas_call(functools.partial(gather_kernel, pieces=tuple(pieces)), ou...  3.02 us
    pallas_call x1, Pallas kernels, ask(): pl.pallas_call(ask_kernel, out_shape=jax.ShapeDtypeStruct((chips, 1, MP),...  1.62 us
  transfers between devices with their start and end apart: 13, of which 3 were waited for; matrix products, arithmetic and copies ran while one was open for 3% of the time, Pallas kernels for 27%

profile of v3, /device:TPU:0, one launch (start us, length us, event | category | flops | bytes accessed | tf_op | source)
XLA Modules:
  0.0 76.2 jit_solution(16906095681489440110)
XLA Ops:
  0.0 0.5 collective-permute-start
  0.5 1.6 %ask.1 = s32[8,1,128]{2,1,0:T(1,128)} custom-call(s32[1]{0:T(128)} %bitcast.order_ref.me_ref, s32[1,128]{1,0:T(1,128)} %holder_ref.3, s32[1,128]{1,0:T(1,128)} %slot_ref.1), custom_call_target="tpu_custom_call" | custom-call | tf_op jit(solution)/shard_map/ask/pallas_call | solution.py:47
  2.1 6.8 %all-to-all-start = ((s32[8,1,128]{2,1,0:T(1,128)}), s32[8,1,128]{2,1,0:T(1,128)S(1)}, u32[]{:S(2)}, u32[]{:S(2)}) async-start(s32[8,1,128]{2,1,0:T(1,128)} %ask.1), calls=%async_computation | async-start | bytes 8192 | tf_op jit(solution)/shard_map/all_to_all | solution.py:360
  8.9 6.4 %all-to-all-done.wanted_ref = s32[8,1,128]{2,1,0:T(1,128)S(1)} async-done(((s32[8,1,128]{2,1,0:T(1,128)}), s32[8,1,128]{2,1,0:T(1,128)S(1)}, u32[]{:S(2)}, u32[]{:S(2)}) %all-to-all-start) | async-done | bytes 4128 | tf_op jit(solution)/shard_map/all_to_all | solution.py:360
  15.3 0.0 collective-permute-done.mate_ref
  15.3 0.0 copy-start.6
  15.3 3.0 %gather_pages.1 = (bf16[2,16,8,512]{3,2,1,0:T(8,128)(2,1)}, bf16[2,16,8,512]{3,2,1,0:T(8,128)(2,1)}, bf16[2,16,8,512]{3,2,1,0:T(8,128)(2,1)}, bf16[2,16,8,512]{3...) custom-call(s32[1]{0:T(128)} %bitcast.4.mine_ref, ...), custom_call_target="tpu_custom_call" | custom-call | bytes 4194304 | tf_op jit(solution)/shard_map/gather_pages/pallas_call | solution.py:162
  18.3 0.0 copy-start
  18.3 0.0 copy-start.5
  18.3 0.6 collective-permute-start.1
  18.9 0.6 collective-permute-start.7
  19.5 0.6 collective-permute-start.8
  20.1 2.3 %collective-permute-start.9 = (bf16[2,16,8,512]{3,2,1,0:T(8,128)(2,1)}, bf16[2,16,8,512]{3,2,1,0:T(8,128)(2,1)}, u32[]{:S(2)}, u32[]{:S(2)}) collective-permute-start(bf16[2,16,8,512]{3,2,1,0:T(8,128)(2,1)} %get-tuple-element.36), channel_id=1, source_target_pairs={{0,6},{1,7},{2,4},{3,5},{4,2},{5,3},{6,0},{7,1},{8,14},{9,15},{10,... | collective-permute-start | bytes 786440 | tf_op jit(solution)/shard_map/ppermute | solution.py:385
  22.4 0.0 copy-done.6
  22.4 1.2 %fusion = (bf16[1,128,1,512]{3,2,1,0:T(2,128)(2,1)}, bf16[1,128,1,512]{3,2,1,0:T(2,128)(2,1)}) fusion(bf16[1,128,2,512]{3,2,1,0:T(2,128)(2,1)S(1)} %copy-done.6), kind=kLoop, calls=%fused_computation.2 | loop fusion | bytes 524288 | tf_op jit(solution)/shard_map/slice | solution.py:367
  24.9 1.0 %live_tokens.1.live_ref = bf16[1024,128]{1,0:T(8,128)(2,1)S(1)} custom-call(s32[1]{0:T(128)} %bitcast.order_ref.me_ref, s32[1]{0:T(128)S(6)} %copy.24.length_ref, s32[1,128]{1,0:T(1,128)} %holder_ref.3), custom_call_target="tpu_custom_call" | custom-call | tf_op jit(solution)/shard_map/live_tokens/pallas_call | solution.py:78
  25.9 2.4 %collective-permute-start.2 = (bf16[2,16,8,256]{3,2,1,0:T(8,128)(2,1)}, bf16[2,16,8,256]{3,2,1,0:T(8,128)(2,1)S(1)}, u32[]{:S(2)}, u32[]{:S(2)}) collective-permute-start(bf16[2,16,8,256]{3,2,1,0:T(8,128)(2,1)} %get-tuple-element.28), channel_id=1, source_target_pairs={{0,10},{1,11},{2,8},{3,9},{4,14},{5,15},{6,12},{7,13},{8,2},{9,3},... | collective-permute-start | bytes 393224 | tf_op jit(solution)/shard_map/ppermute | solution.py:385
  28.3 0.0 collective-permute-done.1.refs_4_
  28.3 0.0 copy-start.1
  28.3 0.6 collective-permute-start.10
  28.9 1.1 %copy_bitcast_fusion = (bf16[128,512]{1,0:T(8,128)(2,1)S(1)}, bf16[128,512]{1,0:T(8,128)(2,1)S(1)}) fusion(bf16[1,128,1,512]{3,2,1,0:T(2,128)(2,1)} %get-tuple-element.41, bf16[1,128,1,512]{3,2,1,0:T(2,128)(2,1)} %get-tuple-element.42), kind=kLoop, calls=%fused_computation | loop fusion | bytes 524288 | tf_op jit(solution)/shard_map/squeeze | solution.py:367
  30.0 6.8 %collective-permute-done.2.refs_5_ = bf16[2,16,8,256]{3,2,1,0:T(8,128)(2,1)S(1)} collective-permute-done((bf16[2,16,8,256]{3,2,1,0:T(8,128)(2,1)}, bf16[2,16,8,256]{3,2,1,0:T(8,128)(2,1)S(1)}, u32[]{:S(2)}, u32[]{:S(2)}) %collective-permute-start.2) | collective-permute-done | bytes 131104 | tf_op jit(solution)/shard_map/ppermute | solution.py:385
  36.8 0.0 copy-start.3
  36.8 3.0 %collective-permute-start.11 = (bf16[2,16,8,256]{3,2,1,0:T(8,128)(2,1)}, bf16[2,16,8,256]{3,2,1,0:T(8,128)(2,1)S(1)}, u32[]{:S(2)}, u32[]{:S(2)}) collective-permute-start(bf16[2,16,8,256]{3,2,1,0:T(8,128)(2,1)} %get-tuple-element.40), channel_id=1, source_target_pairs={{0,14},{1,15},{2,12},{3,13},{4,10},{5,11},{6,8},{7,9},{8,6},{9,7},... | collective-permute-start | bytes 393224 | tf_op jit(solution)/shard_map/ppermute | solution.py:385
  39.7 0.0 copy-done.1
  39.8 0.0 copy-done.3
  39.8 3.0 %collective-permute-done.10 = bf16[2,16,8,256]{3,2,1,0:T(8,128)(2,1)S(1)} collective-permute-done((bf16[2,16,8,256]{3,2,1,0:T(8,128)(2,1)}, bf16[2,16,8,256]{3,2,1,0:T(8,128)(2,1)S(1)}, u32[]{:S(2)}, u32[]{:S(2)}) %collective-permute-start.10) | collective-permute-done | bytes 131104 | tf_op jit(solution)/shard_map/ppermute | solution.py:385
  42.7 0.1 collective-permute-start.3
  42.8 0.0 collective-permute-done.7
  42.8 3.1 %collective-permute-start.4 = (bf16[2,16,8,256]{3,2,1,0:T(8,128)(2,1)}, bf16[2,16,8,256]{3,2,1,0:T(8,128)(2,1)S(1)}, u32[]{:S(2)}, u32[]{:S(2)}) collective-permute-start(bf16[2,16,8,256]{3,2,1,0:T(8,128)(2,1)} %get-tuple-element.30), channel_id=1, source_target_pairs={{0,10},{1,11},{2,8},{3,9},{4,14},{5,15},{6,12},{7,13},{8,2},{9,3},... | collective-permute-start | bytes 393224 | tf_op jit(solution)/shard_map/ppermute | solution.py:385
  45.9 0.0 collective-permute-done.8
  45.9 0.1 collective-permute-start.5
  46.1 0.0 collective-permute-done.9
  46.1 4.3 %collective-permute-start.6 = (bf16[2,16,8,256]{3,2,1,0:T(8,128)(2,1)}, bf16[2,16,8,256]{3,2,1,0:T(8,128)(2,1)S(1)}, u32[]{:S(2)}, u32[]{:S(2)}) collective-permute-start(bf16[2,16,8,256]{3,2,1,0:T(8,128)(2,1)} %get-tuple-element.32), channel_id=1, source_target_pairs={{0,14},{1,15},{2,12},{3,13},{4,10},{5,11},{6,8},{7,9},{8,6},{9,7},... | collective-permute-start | bytes 393224 | tf_op jit(solution)/shard_map/ppermute | solution.py:385
  50.4 0.0 copy-done
  50.4 0.0 copy-done.5
  50.4 0.0 copy-start.2
  50.4 0.0 copy-start.4
  50.4 10.6 %attend_0_0.1 = (f32[128,8192]{1,0:T(8,128)S(1)}, f32[128,512]{1,0:T(8,128)S(1)}) custom-call(s32[1]{0:T(128)S(6)} %copy.25.filled_ref, bf16[1024,128]{1,0:T(8,128)(2,1)S(1)} %live_tokens.1.live_ref, bf16[128,8192]{1,0:T(8,128)(2,1)S(1)} %bitcast.20, bf16[128,512]{1,0:T(8,128)(2,1)S(1)} %get-tuple-element.44.fk_ref, ...), custom_call_target="tpu_custom_call" | custom-call | flops 2684354560 | bytes 8388608 | tf_op jit(solution)/shard_map/attend_0_0/pallas_call | solution.py:317
  61.0 0.0 collective-permute-done.11
  61.1 0.0 copy-done.2
  61.1 0.0 copy-done.4
  61.1 7.6 %attend_0_1.1.rest_6_ = bf16[128,8192]{1,0:T(8,128)(2,1)} custom-call(s32[1]{0:T(128)S(6)} %copy.25.filled_ref, bf16[1024,128]{1,0:T(8,128)(2,1)S(1)} %live_tokens.1.live_ref, bf16[128,8192]{1,0:T(8,128)(2,1)S(1)} %bitcast.21, bf16[128,512]{1,0:T(8,128)(2,1)S(1)} %get-tuple-element.44.fk_ref, bf16[128,512]{1,0:T(8,128)(2,1)S(1)} %get-tuple-element.43.fv_ref, ...), custom_call_target="tpu_custom_call" | custom-call | flops 1073741824 | bytes 4194304 | tf_op jit(solution)/shard_map/attend_0_1/pallas_call | solution.py:317
  68.6 0.0 collective-permute-done.3
  68.6 0.0 collective-permute-done.4
  68.6 0.0 collective-permute-done.5
  68.6 0.0 collective-permute-done.6
  68.6 7.6 %attend_2_1.1 = bf16[128,8192]{1,0:T(8,128)(2,1)} custom-call(s32[1]{0:T(128)S(6)} %copy.25.filled_ref, bf16[1024,128]{1,0:T(8,128)(2,1)S(1)} %live_tokens.1.live_ref, bf16[128,8192]{1,0:T(8,128)(2,1)S(1)} %bitcast.22, bf16[128,512]{1,0:T(8,128)(2,1)S(1)} %get-tuple-element.44.fk_ref, ...), custom_call_target="tpu_custom_call", output_to_operand_aliasing={{}: (11, {})} | custom-call | flops 1073741824 | bytes 4194304 | tf_op jit(solution)/shard_map/attend_2_1/pallas_call | solution.py:317
  (1 shorter events, 0.0 us)
Async XLA Ops:
  0.0 15.3 %collective-permute-start = (bf16[128,2,8,512]{3,2,1,0:T(8,128)(2,1)}, bf16[128,2,8,512]{3,2,1,0:T(8,128)(2,1)S(1)}, u32[]{:S(2)}, u32[]{:S(2)}) collective-permute-start(bf16[128,2,8,512]{3,2,1,0:T(8,128)(2,1)} %own_ref.1), channel_id=1, source_target_pairs={{0,1},{1,0},{2,3},{3,2},{4,5},{5,4},{6,7},{7,6},{8,9},{9,8},{10,11... | collective-permute-start | bytes 6291464 | tf_op jit(solution)/shard_map/ppermute | solution.py:350
  2.1 13.2 %all-to-all-start = ((s32[8,1,128]{2,1,0:T(1,128)}), s32[8,1,128]{2,1,0:T(1,128)S(1)}, u32[]{:S(2)}, u32[]{:S(2)}) async-start(s32[8,1,128]{2,1,0:T(1,128)} %ask.1), calls=%async_computation | async-start | bytes 8192 | tf_op jit(solution)/shard_map/all_to_all | solution.py:360
  15.3 7.2 %copy-start.6 = (bf16[1,128,2,512]{3,2,1,0:T(2,128)(2,1)S(1)}, bf16[1,128,2,512]{3,2,1,0:T(2,128)(2,1)}, u32[]{:S(2)}) copy-start(bf16[1,128,2,512]{3,2,1,0:T(2,128)(2,1)} %param.8) | copy-start | bytes 786436
  18.3 32.1 %copy-start = (bf16[1,128,8192]{2,1,0:T(8,128)(2,1)S(1)}, bf16[1,128,8192]{2,1,0:T(8,128)(2,1)}, u32[]{:S(2)}) copy-start(bf16[1,128,8192]{2,1,0:T(8,128)(2,1)} %param.7) | copy-start | bytes 6291460
  18.3 32.1 %copy-start.5 = (bf16[2,16,8,512]{3,2,1,0:T(8,128)(2,1)S(1)}, bf16[2,16,8,512]{3,2,1,0:T(8,128)(2,1)}, u32[]{:S(2)}) copy-start(bf16[2,16,8,512]{3,2,1,0:T(8,128)(2,1)} %get-tuple-element.33) | copy-start | bytes 786436
  18.3 10.0 %collective-permute-start.1 = (bf16[2,16,8,256]{3,2,1,0:T(8,128)(2,1)}, bf16[2,16,8,256]{3,2,1,0:T(8,128)(2,1)S(1)}, u32[]{:S(2)}, u32[]{:S(2)}) collective-permute-start(bf16[2,16,8,256]{3,2,1,0:T(8,128)(2,1)} %get-tuple-element.27), channel_id=1, source_target_pairs={{0,8},{1,9},{2,10},{3,11},{4,12},{5,13},{6,14},{7,15},{8,0},{9,1},... | collective-permute-start | bytes 393224 | tf_op jit(solution)/shard_map/ppermute | solution.py:385
  18.9 23.9 %collective-permute-start.7 = (bf16[2,16,8,512]{3,2,1,0:T(8,128)(2,1)}, bf16[2,16,8,512]{3,2,1,0:T(8,128)(2,1)}, u32[]{:S(2)}, u32[]{:S(2)}) collective-permute-start(bf16[2,16,8,512]{3,2,1,0:T(8,128)(2,1)} %get-tuple-element.34), channel_id=1, source_target_pairs={{0,2},{1,3},{2,0},{3,1},{4,6},{5,7},{6,4},{7,5},{8,10},{9,11},{10,... | collective-permute-start | bytes 786440 | tf_op jit(solution)/shard_map/ppermute | solution.py:385
  19.5 26.4 %collective-permute-start.8 = (bf16[2,16,8,512]{3,2,1,0:T(8,128)(2,1)}, bf16[2,16,8,512]{3,2,1,0:T(8,128)(2,1)}, u32[]{:S(2)}, u32[]{:S(2)}) collective-permute-start(bf16[2,16,8,512]{3,2,1,0:T(8,128)(2,1)} %get-tuple-element.35), channel_id=1, source_target_pairs={{0,4},{1,5},{2,6},{3,7},{4,0},{5,1},{6,2},{7,3},{8,12},{9,13},{10,... | collective-permute-start | bytes 786440 | tf_op jit(solution)/shard_map/ppermute | solution.py:385
  20.1 26.0 %collective-permute-start.9 = (bf16[2,16,8,512]{3,2,1,0:T(8,128)(2,1)}, bf16[2,16,8,512]{3,2,1,0:T(8,128)(2,1)}, u32[]{:S(2)}, u32[]{:S(2)}) collective-permute-start(bf16[2,16,8,512]{3,2,1,0:T(8,128)(2,1)} %get-tuple-element.36), channel_id=1, source_target_pairs={{0,6},{1,7},{2,4},{3,5},{4,2},{5,3},{6,0},{7,1},{8,14},{9,15},{10,... | collective-permute-start | bytes 786440 | tf_op jit(solution)/shard_map/ppermute | solution.py:385
  25.9 10.9 %collective-permute-start.2 = (bf16[2,16,8,256]{3,2,1,0:T(8,128)(2,1)}, bf16[2,16,8,256]{3,2,1,0:T(8,128)(2,1)S(1)}, u32[]{:S(2)}, u32[]{:S(2)}) collective-permute-start(bf16[2,16,8,256]{3,2,1,0:T(8,128)(2,1)} %get-tuple-element.28), channel_id=1, source_target_pairs={{0,10},{1,11},{2,8},{3,9},{4,14},{5,15},{6,12},{7,13},{8,2},{9,3},... | collective-permute-start | bytes 393224 | tf_op jit(solution)/shard_map/ppermute | solution.py:385
  28.3 11.4 %copy-start.1 = (bf16[2,16,8,256]{3,2,1,0:T(8,128)(2,1)}, bf16[2,16,8,256]{3,2,1,0:T(8,128)(2,1)S(1)}, u32[]{:S(2)}) copy-start(bf16[2,16,8,256]{3,2,1,0:T(8,128)(2,1)S(1)} %collective-permute-done.1.refs_4_) | copy-start | bytes 393220
  28.3 14.4 %collective-permute-start.10 = (bf16[2,16,8,256]{3,2,1,0:T(8,128)(2,1)}, bf16[2,16,8,256]{3,2,1,0:T(8,128)(2,1)S(1)}, u32[]{:S(2)}, u32[]{:S(2)}) collective-permute-start(bf16[2,16,8,256]{3,2,1,0:T(8,128)(2,1)} %get-tuple-element.39), channel_id=1, source_target_pairs={{0,12},{1,13},{2,14},{3,15},{4,8},{5,9},{6,10},{7,11},{8,4},{9,5},... | collective-permute-start | bytes 393224 | tf_op jit(solution)/shard_map/ppermute | solution.py:385
  36.8 3.0 %copy-start.3 = (bf16[2,16,8,256]{3,2,1,0:T(8,128)(2,1)}, bf16[2,16,8,256]{3,2,1,0:T(8,128)(2,1)S(1)}, u32[]{:S(2)}) copy-start(bf16[2,16,8,256]{3,2,1,0:T(8,128)(2,1)S(1)} %collective-permute-done.2.refs_5_) | copy-start | bytes 393220
  36.8 24.3 %collective-permute-start.11 = (bf16[2,16,8,256]{3,2,1,0:T(8,128)(2,1)}, bf16[2,16,8,256]{3,2,1,0:T(8,128)(2,1)S(1)}, u32[]{:S(2)}, u32[]{:S(2)}) collective-permute-start(bf16[2,16,8,256]{3,2,1,0:T(8,128)(2,1)} %get-tuple-element.40), channel_id=1, source_target_pairs={{0,14},{1,15},{2,12},{3,13},{4,10},{5,11},{6,8},{7,9},{8,6},{9,7},... | collective-permute-start | bytes 393224 | tf_op jit(solution)/shard_map/ppermute | solution.py:385
  42.7 25.9 %collective-permute-start.3 = (bf16[2,16,8,256]{3,2,1,0:T(8,128)(2,1)}, bf16[2,16,8,256]{3,2,1,0:T(8,128)(2,1)S(1)}, u32[]{:S(2)}, u32[]{:S(2)}) collective-permute-start(bf16[2,16,8,256]{3,2,1,0:T(8,128)(2,1)} %get-tuple-element.29), channel_id=1, source_target_pairs={{0,8},{1,9},{2,10},{3,11},{4,12},{5,13},{6,14},{7,15},{8,0},{9,1},... | collective-permute-start | bytes 393224 | tf_op jit(solution)/shard_map/ppermute | solution.py:385
  42.8 25.8 %collective-permute-start.4 = (bf16[2,16,8,256]{3,2,1,0:T(8,128)(2,1)}, bf16[2,16,8,256]{3,2,1,0:T(8,128)(2,1)S(1)}, u32[]{:S(2)}, u32[]{:S(2)}) collective-permute-start(bf16[2,16,8,256]{3,2,1,0:T(8,128)(2,1)} %get-tuple-element.30), channel_id=1, source_target_pairs={{0,10},{1,11},{2,8},{3,9},{4,14},{5,15},{6,12},{7,13},{8,2},{9,3},... | collective-permute-start | bytes 393224 | tf_op jit(solution)/shard_map/ppermute | solution.py:385
  45.9 22.7 %collective-permute-start.5 = (bf16[2,16,8,256]{3,2,1,0:T(8,128)(2,1)}, bf16[2,16,8,256]{3,2,1,0:T(8,128)(2,1)S(1)}, u32[]{:S(2)}, u32[]{:S(2)}) collective-permute-start(bf16[2,16,8,256]{3,2,1,0:T(8,128)(2,1)} %get-tuple-element.31), channel_id=1, source_target_pairs={{0,12},{1,13},{2,14},{3,15},{4,8},{5,9},{6,10},{7,11},{8,4},{9,5},... | collective-permute-start | bytes 393224 | tf_op jit(solution)/shard_map/ppermute | solution.py:385
  46.1 22.6 %collective-permute-start.6 = (bf16[2,16,8,256]{3,2,1,0:T(8,128)(2,1)}, bf16[2,16,8,256]{3,2,1,0:T(8,128)(2,1)S(1)}, u32[]{:S(2)}, u32[]{:S(2)}) collective-permute-start(bf16[2,16,8,256]{3,2,1,0:T(8,128)(2,1)} %get-tuple-element.32), channel_id=1, source_target_pairs={{0,14},{1,15},{2,12},{3,13},{4,10},{5,11},{6,8},{7,9},{8,6},{9,7},... | collective-permute-start | bytes 393224 | tf_op jit(solution)/shard_map/ppermute | solution.py:385
  50.4 10.7 %copy-start.2 = (bf16[2,16,8,256]{3,2,1,0:T(8,128)(2,1)S(1)}, bf16[2,16,8,256]{3,2,1,0:T(8,128)(2,1)}, u32[]{:S(2)}) copy-start(bf16[2,16,8,256]{3,2,1,0:T(8,128)(2,1)} %copy-done.1) | copy-start | bytes 393220
  50.4 10.7 %copy-start.4 = (bf16[2,16,8,256]{3,2,1,0:T(8,128)(2,1)S(1)}, bf16[2,16,8,256]{3,2,1,0:T(8,128)(2,1)}, u32[]{:S(2)}) copy-start(bf16[2,16,8,256]{3,2,1,0:T(8,128)(2,1)} %copy-done.3) | copy-start | bytes 393220

commit v4 on v3

--- a/solution.py
+++ b/solution.py
@@ -16,6 +16,7 @@
 GROUP = H // KVH
 LOG2E = 1.4426950408889634
 NEG = -1e30
+HEADS = 4
 CHUNKS = ((0, 2), (2, 2))
 MOST_PERMUTES = 8
 
@@ -195,79 +196,111 @@
     )(*pieces, *after)
 
 
-def attend_kernel(filled_ref, live_ref, q_ref, fk_ref, fv_ref, *rest, parts, heads, fresh, earlier):
-    piece_refs = rest[:parts]
+def attend_kernel(*refs, first, count, starts, rows, fresh, earlier, last):
+    filled_ref, live_ref, q_ref, fk_ref, fv_ref = refs[:5]
+    piece_refs = refs[5 : 5 + len(starts)]
+    rest = refs[5 + len(starts) :]
+    if earlier:
+        old_ref, old_top_ref, old_sum_ref = rest[:3]
     k_ref, v_ref = rest[-2:]
-    rest = rest[parts:-2]
-    if earlier:
-        old_ref, stats_ref = rest[:2]
-        o_ref = rest[-1]
-    elif len(rest) == 2 and rest[0].dtype == jnp.float32:
-        o_ref, stats_ref = rest
+    if last:
+        out_ref, held_ref, sem = rest[-5:-2]
     else:
-        o_ref = rest[-1]
-    last = o_ref.dtype != jnp.float32
+        o_ref, top_ref, sum_ref = rest[-5:-2]
     scale = HD**-0.5 * LOG2E
-    rows = heads * C
-    tokens = piece_refs[0].shape[-2]
-    cached = parts * tokens
-    fk = fk_ref[...]
-    for p in range(parts):
-        at = slice(p * tokens, (p + 1) * tokens)
-        live = live_ref[at]
-        k_ref[at] = jnp.where(live > 0, piece_refs[p][0], fk[:1])
-        v_ref[at, :HD] = jnp.where(live > 0, piece_refs[p][1], jnp.zeros_like(live))
-        v_ref[at, HD:] = live
-    if fresh:
-        k_ref[cached:] = fk
-        v_ref[cached:, :HD] = fv_ref[...]
-        v_ref[cached:, HD:] = jnp.ones_like(fk)
+    heads = HEADS
+    parts = []
+    for piece_ref, start in zip(piece_refs, starts):
+        if len(piece_ref.shape) == 4:
+            parts += [(piece_ref.at[i], start) for i in range(piece_ref.shape[0])]
+        else:
+            parts.append((piece_ref, start))
+    tokens = parts[0][0].shape[-2]
+    cached = len(parts) * tokens
     nt = (((1,), (1,)), ((), ()))
-    token = lax.rem(lax.broadcasted_iota(jnp.int32, (rows, C), 0), C)
-    lane = lax.broadcasted_iota(jnp.int32, (C, HD), 1)
-    causal = lax.broadcasted_iota(jnp.int32, (rows, C), 1) <= token
+    shape = (heads * C, C)
+    token = lax.rem(lax.broadcasted_iota(jnp.int32, shape, 0), C)
+    causal = lax.broadcasted_iota(jnp.int32, shape, 1) <= token
     filled = token < filled_ref[0]
-    if earlier:
-        old_stats = stats_ref[...]
-    elif not last:
-        stats = jnp.zeros((C, HD), jnp.float32)
-    for g in range(0, GROUP, heads):
-        many = range(g, g + heads)
-        cols = [slice(i * HD, (i + 1) * HD) for i in many]
-        q = jnp.concatenate([q_ref[:, c] for c in cols], axis=0)
-        s = lax.dot_general(q, k_ref[...], nt, preferred_element_type=jnp.float32)
-        s1 = s[:, :cached]
-        top = jnp.max(s1, axis=1, keepdims=True)
+
+    def span(start, size):
+        return pl.ds(pl.multiple_of(start * HD, HD), size * HD)
+
+    def store(h, g):
+        return pltpu.make_async_copy(
+            held_ref.at[:, span(h * GROUP + g, heads)],
+            out_ref.at[:, span((first + h) * GROUP + g, heads)],
+            sem.at[h * (GROUP // heads) + g // heads],
+        )
+
+    def one_head(h):
+        head = first + h
+        base = head * GROUP
+        fk = fk_ref[:, span(head, 1)]
+        for p, (piece_ref, start) in enumerate(parts):
+            at = slice(p * tokens, (p + 1) * tokens)
+            live = live_ref[rows * cached + p * tokens : rows * cached + (p + 1) * tokens]
+            col = span(head - start, 1)
+            k_ref[at] = jnp.where(live > 0, piece_ref[0, :, col], fk[:1])
+            v_ref[at, :HD] = jnp.where(live > 0, piece_ref[1, :, col], jnp.zeros_like(live))
+            v_ref[at, HD:] = live
         if fresh:
-            s2 = jnp.where(causal, s[:, cached:], NEG)
-            top = jnp.maximum(top, jnp.max(s2, axis=1, keepdims=True))
-        if earlier:
-            old_top = jnp.concatenate([old_stats[:, i : i + 1] for i in many], axis=0)
-            old_sum = jnp.concatenate(
-                [old_stats[:, GROUP + i : GROUP + i + 1] for i in many], axis=0
-            )
-            top = jnp.maximum(top, old_top)
-        p = jnp.exp2((s1 - top) * scale).astype(jnp.bfloat16)
-        if fresh:
-            p2 = jnp.exp2((s2 - top) * scale).astype(jnp.bfloat16)
-            p = jnp.concatenate([p, p2], axis=1)
-        o = jnp.dot(p, v_ref[...], preferred_element_type=jnp.float32)
-        o, total = o[:, :HD], o[:, HD:]
-        if earlier:
-            share = jnp.exp2((old_top - top) * scale)
-            old = jnp.concatenate([old_ref[:, c] for c in cols], axis=0)
-            o = o + share * old
-            total = total + share * old_sum
-        if last:
-            o = jnp.where(filled, o / total, 0.0).astype(o_ref.dtype)
-        for k, i in enumerate(many):
-            at = slice(k * C, (k + 1) * C)
-            o_ref[:, cols[k]] = o[at]
-            if not last:
-                stats = jnp.where(lane == i, top[at], stats)
-                stats = jnp.where(lane == GROUP + i, total[at], stats)
-    if not last:
-        stats_ref[...] = stats
+            k_ref[cached:] = fk
+            v_ref[cached:, :HD] = fv_ref[:, span(head, 1)]
+            v_ref[cached:, HD:] = jnp.ones_like(fk)
+
+        def scores(g):
+            q = [q_ref[:, span(base + i, 1)] for i in range(g, g + heads)]
+            q = jnp.concatenate(q, axis=0)
+            return lax.dot_general(q, k_ref[...], nt, preferred_element_type=jnp.float32)
+
+        def old(ref, many):
+            return jnp.concatenate([ref[:, span(h * GROUP + i, 1)] for i in many], axis=0)
+
+        ahead = scores(0)
+        for g in range(0, GROUP, heads):
+            many = range(g, g + heads)
+            s = ahead
+            if g + heads < GROUP:
+                ahead = scores(g + heads)
+            blocks = [s[:, i : i + HD] for i in range(0, s.shape[1], HD)]
+            if fresh:
+                blocks[-1] = jnp.where(causal, blocks[-1], NEG)
+            top = functools.reduce(jnp.maximum, blocks)
+            top = jnp.broadcast_to(jnp.max(top, axis=1, keepdims=True), top.shape)
+            if earlier:
+                old_top = old(old_top_ref, many)
+                top = jnp.maximum(top, old_top)
+            p = [jnp.exp2((b - top) * scale).astype(jnp.bfloat16) for b in blocks]
+            p = jnp.concatenate(p, axis=1)
+            o = jnp.dot(p, v_ref[...], preferred_element_type=jnp.float32)
+            o, total = o[:, :HD], o[:, HD:]
+            if earlier:
+                share = jnp.exp2((old_top - top) * scale)
+                o = o + share * old(old_ref, many)
+                total = total + share * old(old_sum_ref, many)
+            if last:
+                o = jnp.where(filled, o / total, 0.0).astype(held_ref.dtype)
+            for k, i in enumerate(many):
+                at = slice(k * C, (k + 1) * C)
+                if last:
+                    held_ref[:, span(h * GROUP + i, 1)] = o[at]
+                else:
+                    col = span(h * GROUP + i, 1)
+                    o_ref[:, col] = o[at]
+                    top_ref[:, col] = top[at]
+                    sum_ref[:, col] = total[at]
+            if last:
+                store(h, g).start()
+
+    if count == 1:
+        one_head(0)
+    else:
+        pl.loop(0, count)(one_head)
+    if last:
+        for h in range(count):
+            for g in range(0, GROUP, heads):
+                store(h, g).wait()
 
 
 def attend(first, count, filled, live, queries, fresh_k, fresh_v, pieces, rows, out=None, earlier=None, fresh=True, last=True):
@@ -275,63 +308,50 @@
     tokens = sum(
         p.shape[-2] * (p.shape[0] if p.ndim == 4 else 1) for p, start in pieces
     )
-    wide = pl.BlockSpec((C, width), lambda h: (0, h + first))
-    narrow = pl.BlockSpec((C, HD), lambda h: (0, h + first))
-    operands = [filled, live, queries, fresh_k, fresh_v]
-    in_specs = [
-        pl.BlockSpec(memory_space=pltpu.SMEM),
-        pl.BlockSpec((tokens, HD), lambda h: (rows, 0)),
-        wide,
-        narrow,
-        narrow,
-    ]
-    parts = 0
-    for piece, start in pieces:
-        low = first - start
-        for i in range(piece.shape[0] if piece.ndim == 4 else 1):
-            operands.append(piece)
-            lead = (i,) if piece.ndim == 4 else ()
-            block = (None,) * len(lead) + piece.shape[-3:-1] + (HD,)
-            in_specs.append(
-                pl.BlockSpec(block, lambda h, l=lead, d=low: l + (0, 0, h + d))
-            )
-            parts += 1
+    operands = [filled, live, queries, fresh_k, fresh_v] + [p for p, start in pieces]
     if earlier is not None:
         operands += earlier
-        in_specs += [wide, narrow]
+    inside = pl.BlockSpec(memory_space=pltpu.VMEM)
+    in_specs = [pl.BlockSpec(memory_space=pltpu.SMEM)] + [inside] * (len(operands) - 1)
     aliases = {}
     if out is not None:
         operands.append(out)
         in_specs.append(pl.BlockSpec(memory_space=pl.ANY))
         aliases = {len(operands) - 1: 0}
+    keys = tokens + (C if fresh else 0)
+    scratch_shapes = [
+        pltpu.VMEM((keys, HD), jnp.bfloat16),
+        pltpu.VMEM((keys, 2 * HD), jnp.bfloat16),
+    ]
     if last:
-        out_shape = jax.ShapeDtypeStruct((C, H * HD), jnp.bfloat16)
-        out_specs = wide
+        out_shape = pltpu.HBM((C, H * HD), jnp.bfloat16)
+        out_specs = pl.BlockSpec(memory_space=pltpu.HBM)
+        scratch_shapes = [
+            pltpu.VMEM((C, count * width), jnp.bfloat16),
+            pltpu.SemaphoreType.DMA((count * GROUP // HEADS,)),
+        ] + scratch_shapes
     else:
         out_shape = [
-            jax.ShapeDtypeStruct((C, H * HD), jnp.float32),
-            jax.ShapeDtypeStruct((C, KVH * HD), jnp.float32),
-        ]
-        out_specs = [wide, narrow]
-    keys = tokens + (C if fresh else 0)
+            jax.ShapeDtypeStruct((C, count * width), jnp.float32)
+        ] * 3
+        out_specs = [inside] * 3
     return pl.pallas_call(
         functools.partial(
             attend_kernel,
-            parts=parts,
-            heads=4,
+            first=first,
+            count=count,
+            starts=tuple(start for p, start in pieces),
+            rows=rows,
             fresh=fresh,
             earlier=earlier is not None,
+            last=last,
         ),
-        grid=(count,),
         out_shape=out_shape,
         in_specs=in_specs,
         out_specs=out_specs,
-        scratch_shapes=[
-            pltpu.VMEM((keys, HD), jnp.bfloat16),
-            pltpu.VMEM((keys, 2 * HD), jnp.bfloat16),
-        ],
+        scratch_shapes=scratch_shapes,
         input_output_aliases=aliases,
-        compiler_params=pltpu.CompilerParams(vmem_limit_bytes=32 * 2**20),
+        compiler_params=pltpu.CompilerParams(vmem_limit_bytes=16 * 2**20),
         cost_estimate=pl.CostEstimate(
             flops=4 * count * C * width * keys,
             bytes_accessed=4 * count * C * width * 2,
@@ -390,7 +410,6 @@
         + [(x, first, count) for first, count in CHUNKS for x in far]
     )
     close = [(sent[x] if x == 0 else swap(sent[x], x), 0) for x in near]
-    earlier = attend_some(0, KVH, close, 0, last=False)
     arrived = []
     for c, (first, count) in enumerate(CHUNKS):
         batch = sent[len(near) + c * len(far) : len(near) + (c + 1) * len(far)]
@@ -398,9 +417,13 @@
             batch = hold_back(batch, arrived[:2])
         arrived = [swap(piece, x) for piece, x in zip(batch, far)]
         pieces = [(piece, first) for piece in arrived]
-        out = attend_some(
-            first, count, pieces, 1, out, earlier=earlier, fresh=False
-        )
+        if c < len(CHUNKS) - 1:
+            out = attend_some(first, count, close + pieces, 0, out)
+        else:
+            earlier = attend_some(first, count, close, 0, last=False)
+            out = attend_some(
+                first, count, pieces, 1, out, earlier=earlier, fresh=False
+            )
     return out[None]
 
 

time: 76.5 us -> 72.6 us (0.949)
  Pallas kernels: 31.4 us -> 25.2 us
  waiting for transfers between devices: 16.1 us -> 19.3 us
  starting transfers between devices: 25 us -> 22.3 us
  local copies, waits for them, and re-layouts: 2.25 us -> 4.04 us
    pallas_call x3, Pallas kernels: 25.8 us -> 19.5 us  [attend(): pl.pallas_call(functools.partial(attend_kernel, first=first, count=count,...]
    ppermute x11, waiting for transfers between devices: 9.75 us -> 12.9 us  [swap(): return lax.ppermute(piece, 'dp', [(i, i ^ 2 * x) for i in range(devices)])]
    ppermute x11, starting transfers between devices: 17.8 us -> 15 us  [swap(): return lax.ppermute(piece, 'dp', [(i, i ^ 2 * x) for i in range(devices)])]
    unnamed x14, local copies, waits for them, and re-layouts: 0.03 us -> 1.82 us
  transfers between devices with their start and end apart: 13 -> 13, of which waited for: 3 -> 5; matrix products, arithmetic and copies ran while one was open for 3% -> 3% of each run, Pallas kernels for 27% -> 24%
where the time goes in v4:
time: 72.6 us; the launch traced here: 72.3 us
  Pallas kernels  25.2 us (35%)
  starting transfers between devices  22.3 us (31%)
  waiting for transfers between devices  19.3 us (27%)
  local copies, waits for them, and re-layouts  4.04 us (6%)
  between operations  1.43 us (2%)
    pallas_call x3, Pallas kernels, attend(): pl.pallas_call(functools.partial(attend_kernel, first=first, count=count,...  19.5 us
    ppermute x11, starting transfers between devices, swap(): return lax.ppermute(piece, 'dp', [(i, i ^ 2 * x) for i in range(devices)])  15 us
    ppermute x11, waiting for transfers between devices, swap(): return lax.ppermute(piece, 'dp', [(i, i ^ 2 * x) for i in range(devices)])  12.9 us
    all_to_all x1, starting transfers between devices, local(): wanted = exchange(asked)  6.8 us
    all_to_all x1, waiting for transfers between devices, local(): wanted = exchange(asked)  6.39 us
    pallas_call x1, Pallas kernels, gather_pages(): pl.pallas_call(functools.partial(gather_kernel, pieces=tuple(pieces)), ou...  3.01 us
    unnamed x14, local copies, waits for them, and re-layouts  1.82 us
    pallas_call x1, Pallas kernels, ask(): pl.pallas_call(ask_kernel, out_shape=jax.ShapeDtypeStruct((chips, 1, MP),...  1.62 us
  transfers between devices with their start and end apart: 13, of which 5 were waited for; matrix products, arithmetic and copies ran while one was open for 3% of the time, Pallas kernels for 24%

profile of v4, /device:TPU:0, one launch (start us, length us, event | category | flops | bytes accessed | tf_op | source)
XLA Modules:
  0.0 72.3 jit_solution(12586854725144438674)
XLA Ops:
  0.0 0.5 collective-permute-start
  0.5 1.6 %ask.1 = s32[8,1,128]{2,1,0:T(1,128)} custom-call(s32[1]{0:T(128)} %bitcast.order_ref.me_ref, s32[1,128]{1,0:T(1,128)} %holder_ref.3, s32[1,128]{1,0:T(1,128)} %slot_ref.1), custom_call_target="tpu_custom_call" | custom-call | tf_op jit(solution)/shard_map/ask/pallas_call | solution.py:48
  2.1 6.8 %all-to-all-start = ((s32[8,1,128]{2,1,0:T(1,128)}), s32[8,1,128]{2,1,0:T(1,128)S(1)}, u32[]{:S(2)}, u32[]{:S(2)}) async-start(s32[8,1,128]{2,1,0:T(1,128)} %ask.1), calls=%async_computation | async-start | bytes 8192 | tf_op jit(solution)/shard_map/all_to_all | solution.py:380
  8.9 6.4 %all-to-all-done.wanted_ref = s32[8,1,128]{2,1,0:T(1,128)S(1)} async-done(((s32[8,1,128]{2,1,0:T(1,128)}), s32[8,1,128]{2,1,0:T(1,128)S(1)}, u32[]{:S(2)}, u32[]{:S(2)}) %all-to-all-start) | async-done | bytes 4128 | tf_op jit(solution)/shard_map/all_to_all | solution.py:380
  15.3 0.0 collective-permute-done.mate_ref
  15.3 0.0 copy-start.6
  15.3 3.0 %gather_pages.1 = (bf16[2,16,8,512]{3,2,1,0:T(8,128)(2,1)}, bf16[2,16,8,512]{3,2,1,0:T(8,128)(2,1)}, bf16[2,16,8,512]{3,2,1,0:T(8,128)(2,1)}, bf16[2,16,8,512]{3...) custom-call(s32[1]{0:T(128)} %bitcast.4.mine_ref, ...), custom_call_target="tpu_custom_call" | custom-call | bytes 4194304 | tf_op jit(solution)/shard_map/gather_pages/pallas_call | solution.py:163
  18.3 0.0 copy-start
  18.3 0.0 copy-start.5
  18.3 0.6 collective-permute-start.1
  18.9 2.4 %collective-permute-start.2 = (bf16[2,16,8,256]{3,2,1,0:T(8,128)(2,1)}, bf16[2,16,8,256]{3,2,1,0:T(8,128)(2,1)S(1)}, u32[]{:S(2)}, u32[]{:S(2)}) collective-permute-start(bf16[2,16,8,256]{3,2,1,0:T(8,128)(2,1)} %get-tuple-element.29), channel_id=1, source_target_pairs={{0,10},{1,11},{2,8},{3,9},{4,14},{5,15},{6,12},{7,13},{8,2},{9,3},... | collective-permute-start | bytes 393224 | tf_op jit(solution)/shard_map/ppermute | solution.py:405
  21.3 1.5 %collective-permute-start.7 = (bf16[2,16,8,512]{3,2,1,0:T(8,128)(2,1)}, bf16[2,16,8,512]{3,2,1,0:T(8,128)(2,1)S(1)}, u32[]{:S(2)}, u32[]{:S(2)}) collective-permute-start(bf16[2,16,8,512]{3,2,1,0:T(8,128)(2,1)} %get-tuple-element.35), channel_id=1, source_target_pairs={{0,2},{1,3},{2,0},{3,1},{4,6},{5,7},{6,4},{7,5},{8,10},{9,11},{10,... | collective-permute-start | bytes 786440 | tf_op jit(solution)/shard_map/ppermute | solution.py:405
  22.8 0.5 collective-permute-start.8
  23.3 1.5 %collective-permute-start.9 = (bf16[2,16,8,512]{3,2,1,0:T(8,128)(2,1)}, bf16[2,16,8,512]{3,2,1,0:T(8,128)(2,1)}, u32[]{:S(2)}, u32[]{:S(2)}) collective-permute-start(bf16[2,16,8,512]{3,2,1,0:T(8,128)(2,1)} %get-tuple-element.37), channel_id=1, source_target_pairs={{0,6},{1,7},{2,4},{3,5},{4,2},{5,3},{6,0},{7,1},{8,14},{9,15},{10,... | collective-permute-start | bytes 786440 | tf_op jit(solution)/shard_map/ppermute | solution.py:405
  24.8 0.0 copy-done.6
  24.8 1.2 %fusion = (bf16[1,128,1,512]{3,2,1,0:T(2,128)(2,1)}, bf16[1,128,1,512]{3,2,1,0:T(2,128)(2,1)}) fusion(bf16[1,128,2,512]{3,2,1,0:T(2,128)(2,1)S(1)} %copy-done.6), kind=kLoop, calls=%fused_computation.2 | loop fusion | bytes 524288 | tf_op jit(solution)/shard_map/slice | solution.py:387
  27.2 1.0 %live_tokens.1.refs_1_ = bf16[1024,128]{1,0:T(8,128)(2,1)S(1)} custom-call(s32[1]{0:T(128)} %bitcast.order_ref.me_ref, s32[1]{0:T(128)S(6)} %copy.24.length_ref, s32[1,128]{1,0:T(1,128)} %holder_ref.3), custom_call_target="tpu_custom_call" | custom-call | tf_op jit(solution)/shard_map/live_tokens/pallas_call | solution.py:79
  28.2 1.5 %collective-permute-done.1.refs_4_ = bf16[2,16,8,256]{3,2,1,0:T(8,128)(2,1)S(1)} collective-permute-done((bf16[2,16,8,256]{3,2,1,0:T(8,128)(2,1)}, bf16[2,16,8,256]{3,2,1,0:T(8,128)(2,1)S(1)}, u32[]{:S(2)}, u32[]{:S(2)}) %collective-permute-start.1) | collective-permute-done | bytes 131104 | tf_op jit(solution)/shard_map/ppermute | solution.py:405
  29.8 0.0 copy-start.1
  29.8 1.5 %collective-permute-start.10 = (bf16[2,16,8,256]{3,2,1,0:T(8,128)(2,1)}, bf16[2,16,8,256]{3,2,1,0:T(8,128)(2,1)S(1)}, u32[]{:S(2)}, u32[]{:S(2)}) collective-permute-start(bf16[2,16,8,256]{3,2,1,0:T(8,128)(2,1)} %get-tuple-element.41), channel_id=1, source_target_pairs={{0,12},{1,13},{2,14},{3,15},{4,8},{5,9},{6,10},{7,11},{8,4},{9,5},... | collective-permute-start | bytes 393224 | tf_op jit(solution)/shard_map/ppermute | solution.py:405
  31.3 1.2 %collective-permute-done.2.refs_5_ = bf16[2,16,8,256]{3,2,1,0:T(8,128)(2,1)S(1)} collective-permute-done((bf16[2,16,8,256]{3,2,1,0:T(8,128)(2,1)}, bf16[2,16,8,256]{3,2,1,0:T(8,128)(2,1)S(1)}, u32[]{:S(2)}, u32[]{:S(2)}) %collective-permute-start.2) | collective-permute-done | bytes 131104 | tf_op jit(solution)/shard_map/ppermute | solution.py:405
  32.5 0.0 copy-start.3
  32.5 1.5 %collective-permute-start.11 = (bf16[2,16,8,256]{3,2,1,0:T(8,128)(2,1)}, bf16[2,16,8,256]{3,2,1,0:T(8,128)(2,1)}, u32[]{:S(2)}, u32[]{:S(2)}) collective-permute-start(bf16[2,16,8,256]{3,2,1,0:T(8,128)(2,1)} %get-tuple-element.42), channel_id=1, source_target_pairs={{0,14},{1,15},{2,12},{3,13},{4,10},{5,11},{6,8},{7,9},{8,6},{9,7},... | collective-permute-start | bytes 393224 | tf_op jit(solution)/shard_map/ppermute | solution.py:405
  34.0 1.1 %copy_bitcast_fusion = (bf16[128,512]{1,0:T(8,128)(2,1)S(1)}, bf16[128,512]{1,0:T(8,128)(2,1)S(1)}) fusion(bf16[1,128,1,512]{3,2,1,0:T(2,128)(2,1)} %get-tuple-element.43, bf16[1,128,1,512]{3,2,1,0:T(2,128)(2,1)} %get-tuple-element.44), kind=kLoop, calls=%fused_computation | loop fusion | bytes 524288 | tf_op jit(solution)/shard_map/squeeze | solution.py:387
  35.1 0.0 copy-done.1
  35.1 0.0 copy-done.3
  35.1 8.0 %collective-permute-done.10 = bf16[2,16,8,256]{3,2,1,0:T(8,128)(2,1)S(1)} collective-permute-done((bf16[2,16,8,256]{3,2,1,0:T(8,128)(2,1)}, bf16[2,16,8,256]{3,2,1,0:T(8,128)(2,1)S(1)}, u32[]{:S(2)}, u32[]{:S(2)}) %collective-permute-start.10) | collective-permute-done | bytes 131104 | tf_op jit(solution)/shard_map/ppermute | solution.py:405
  43.1 0.0 collective-permute-start.3
  43.1 2.2 %collective-permute-done.11 = bf16[2,16,8,256]{3,2,1,0:T(8,128)(2,1)} collective-permute-done((bf16[2,16,8,256]{3,2,1,0:T(8,128)(2,1)}, bf16[2,16,8,256]{3,2,1,0:T(8,128)(2,1)}, u32[]{:S(2)}, u32[]{:S(2)}) %collective-permute-start.11) | collective-permute-done | bytes 131104 | tf_op jit(solution)/shard_map/ppermute | solution.py:405
  45.3 0.5 collective-permute-start.4
  45.8 0.0 collective-permute-done.7
  45.8 1.8 %collective-permute-start.5 = (bf16[2,16,8,256]{3,2,1,0:T(8,128)(2,1)}, bf16[2,16,8,256]{3,2,1,0:T(8,128)(2,1)S(1)}, u32[]{:S(2)}, u32[]{:S(2)}) collective-permute-start(bf16[2,16,8,256]{3,2,1,0:T(8,128)(2,1)} %get-tuple-element.32), channel_id=1, source_target_pairs={{0,12},{1,13},{2,14},{3,15},{4,8},{5,9},{6,10},{7,11},{8,4},{9,5},... | collective-permute-start | bytes 393224 | tf_op jit(solution)/shard_map/ppermute | solution.py:405
  47.5 0.0 collective-permute-done.8
  47.5 3.3 %collective-permute-start.6 = (bf16[2,16,8,256]{3,2,1,0:T(8,128)(2,1)}, bf16[2,16,8,256]{3,2,1,0:T(8,128)(2,1)S(1)}, u32[]{:S(2)}, u32[]{:S(2)}) collective-permute-start(bf16[2,16,8,256]{3,2,1,0:T(8,128)(2,1)} %get-tuple-element.33), channel_id=1, source_target_pairs={{0,14},{1,15},{2,12},{3,13},{4,10},{5,11},{6,8},{7,9},{8,6},{9,7},... | collective-permute-start | bytes 393224 | tf_op jit(solution)/shard_map/ppermute | solution.py:405
  50.8 0.0 collective-permute-done.9
  50.8 0.0 copy-done
  50.8 0.0 copy-done.5
  50.8 0.0 copy-start.2
  50.9 0.9 %copy-done.2 = bf16[2,16,8,256]{3,2,1,0:T(8,128)(2,1)S(1)} copy-done((bf16[2,16,8,256]{3,2,1,0:T(8,128)(2,1)S(1)}, bf16[2,16,8,256]{3,2,1,0:T(8,128)(2,1)}, u32[]{:S(2)}) %copy-start.2) | copy-done | bytes 131096
  51.8 0.0 copy-start.4
  51.8 0.9 %copy-done.4 = bf16[2,16,8,256]{3,2,1,0:T(8,128)(2,1)S(1)} copy-done((bf16[2,16,8,256]{3,2,1,0:T(8,128)(2,1)S(1)}, bf16[2,16,8,256]{3,2,1,0:T(8,128)(2,1)}, u32[]{:S(2)}) %copy-start.4) | copy-done | bytes 131096
  52.7 9.1 %attend_0_0.1.refs_12_ = bf16[128,8192]{1,0:T(8,128)(2,1)} custom-call(s32[1]{0:T(128)S(6)} %copy.25.refs_0_, bf16[1024,128]{1,0:T(8,128)(2,1)S(1)} %live_tokens.1.refs_1_, bf16[128,8192]{1,0:T(8,128)(2,1)S(1)} %bitcast.20, bf16[128,512]{1,0:T(8,128)(2,1)S(1)} %get-tuple-element.46.refs_3_, bf16[128,512]{1,0:T(8,128)(2,1)S(1)} %get-tuple-element.45.refs_4_, ...), custom_call_target="tpu_custom_call" | custom-call | flops 2415919104 | bytes 4194304 | tf_op jit(solution)/shard_map/attend_0_0/pallas_call | solution.py:338
  61.8 5.8 %attend_2_0.1 = (f32[128,4096]{1,0:T(8,128)S(1)}, f32[128,4096]{1,0:T(8,128)S(1)}, f32[128,4096]{1,0:T(8,128)S(1)}) custom-call(s32[1]{0:T(128)S(6)} %copy.25.refs_0_, bf16[1024,128]{1,0:T(8,128)(2,1)S(1)} %live_tokens.1.refs_1_, bf16[128,8192]{1,0:T(8,128)(2,1)S(1)} %bitcast.21, bf16[128,512]{1,0:T(8,128)(2,1)S(1)} %get-tuple-element.46.refs_3_, ...), custom_call_target="tpu_custom_call" | custom-call | flops 1342177280 | bytes 4194304 | tf_op jit(solution)/shard_map/attend_2_0/pallas_call | solution.py:338
  67.6 0.0 collective-permute-done.3
  67.6 0.0 collective-permute-done.4
  67.6 0.0 collective-permute-done.5
  67.6 0.0 collective-permute-done.6
  67.6 4.6 %attend_2_1.1 = bf16[128,8192]{1,0:T(8,128)(2,1)} custom-call(s32[1]{0:T(128)S(6)} %copy.25.refs_0_, bf16[1024,128]{1,0:T(8,128)(2,1)S(1)} %live_tokens.1.refs_1_, bf16[128,8192]{1,0:T(8,128)(2,1)S(1)} %bitcast.22, bf16[128,512]{1,0:T(8,128)(2,1)S(1)} %get-tuple-element.46.refs_3_, ...), custom_call_target="tpu_custom_call", output_to_operand_aliasing={{}: (12, {})} | custom-call | flops 1073741824 | bytes 4194304 | tf_op jit(solution)/shard_map/attend_2_1/pallas_call | solution.py:338
  (1 shorter events, 0.0 us)
Async XLA Ops:
  0.0 15.3 %collective-permute-start = (bf16[128,2,8,512]{3,2,1,0:T(8,128)(2,1)}, bf16[128,2,8,512]{3,2,1,0:T(8,128)(2,1)S(1)}, u32[]{:S(2)}, u32[]{:S(2)}) collective-permute-start(bf16[128,2,8,512]{3,2,1,0:T(8,128)(2,1)} %own_ref.1), channel_id=1, source_target_pairs={{0,1},{1,0},{2,3},{3,2},{4,5},{5,4},{6,7},{7,6},{8,9},{9,8},{10,11... | collective-permute-start | bytes 6291464 | tf_op jit(solution)/shard_map/ppermute | solution.py:370
  2.1 13.2 %all-to-all-start = ((s32[8,1,128]{2,1,0:T(1,128)}), s32[8,1,128]{2,1,0:T(1,128)S(1)}, u32[]{:S(2)}, u32[]{:S(2)}) async-start(s32[8,1,128]{2,1,0:T(1,128)} %ask.1), calls=%async_computation | async-start | bytes 8192 | tf_op jit(solution)/shard_map/all_to_all | solution.py:380
  15.3 9.5 %copy-start.6 = (bf16[1,128,2,512]{3,2,1,0:T(2,128)(2,1)S(1)}, bf16[1,128,2,512]{3,2,1,0:T(2,128)(2,1)}, u32[]{:S(2)}) copy-start(bf16[1,128,2,512]{3,2,1,0:T(2,128)(2,1)} %param.8) | copy-start | bytes 786436
  18.3 32.5 %copy-start = (bf16[1,128,8192]{2,1,0:T(8,128)(2,1)S(1)}, bf16[1,128,8192]{2,1,0:T(8,128)(2,1)}, u32[]{:S(2)}) copy-start(bf16[1,128,8192]{2,1,0:T(8,128)(2,1)} %param.7) | copy-start | bytes 6291460
  18.3 32.5 %copy-start.5 = (bf16[2,16,8,512]{3,2,1,0:T(8,128)(2,1)S(1)}, bf16[2,16,8,512]{3,2,1,0:T(8,128)(2,1)}, u32[]{:S(2)}) copy-start(bf16[2,16,8,512]{3,2,1,0:T(8,128)(2,1)} %get-tuple-element.34) | copy-start | bytes 786436
  18.3 11.4 %collective-permute-start.1 = (bf16[2,16,8,256]{3,2,1,0:T(8,128)(2,1)}, bf16[2,16,8,256]{3,2,1,0:T(8,128)(2,1)S(1)}, u32[]{:S(2)}, u32[]{:S(2)}) collective-permute-start(bf16[2,16,8,256]{3,2,1,0:T(8,128)(2,1)} %get-tuple-element.28), channel_id=1, source_target_pairs={{0,8},{1,9},{2,10},{3,11},{4,12},{5,13},{6,14},{7,15},{8,0},{9,1},... | collective-permute-start | bytes 393224 | tf_op jit(solution)/shard_map/ppermute | solution.py:405
  18.9 13.6 %collective-permute-start.2 = (bf16[2,16,8,256]{3,2,1,0:T(8,128)(2,1)}, bf16[2,16,8,256]{3,2,1,0:T(8,128)(2,1)S(1)}, u32[]{:S(2)}, u32[]{:S(2)}) collective-permute-start(bf16[2,16,8,256]{3,2,1,0:T(8,128)(2,1)} %get-tuple-element.29), channel_id=1, source_target_pairs={{0,10},{1,11},{2,8},{3,9},{4,14},{5,15},{6,12},{7,13},{8,2},{9,3},... | collective-permute-start | bytes 393224 | tf_op jit(solution)/shard_map/ppermute | solution.py:405
  21.3 24.5 %collective-permute-start.7 = (bf16[2,16,8,512]{3,2,1,0:T(8,128)(2,1)}, bf16[2,16,8,512]{3,2,1,0:T(8,128)(2,1)S(1)}, u32[]{:S(2)}, u32[]{:S(2)}) collective-permute-start(bf16[2,16,8,512]{3,2,1,0:T(8,128)(2,1)} %get-tuple-element.35), channel_id=1, source_target_pairs={{0,2},{1,3},{2,0},{3,1},{4,6},{5,7},{6,4},{7,5},{8,10},{9,11},{10,... | collective-permute-start | bytes 786440 | tf_op jit(solution)/shard_map/ppermute | solution.py:405
  22.8 24.8 %collective-permute-start.8 = (bf16[2,16,8,512]{3,2,1,0:T(8,128)(2,1)}, bf16[2,16,8,512]{3,2,1,0:T(8,128)(2,1)}, u32[]{:S(2)}, u32[]{:S(2)}) collective-permute-start(bf16[2,16,8,512]{3,2,1,0:T(8,128)(2,1)} %get-tuple-element.36), channel_id=1, source_target_pairs={{0,4},{1,5},{2,6},{3,7},{4,0},{5,1},{6,2},{7,3},{8,12},{9,13},{10,... | collective-permute-start | bytes 786440 | tf_op jit(solution)/shard_map/ppermute | solution.py:405
  23.3 27.5 %collective-permute-start.9 = (bf16[2,16,8,512]{3,2,1,0:T(8,128)(2,1)}, bf16[2,16,8,512]{3,2,1,0:T(8,128)(2,1)}, u32[]{:S(2)}, u32[]{:S(2)}) collective-permute-start(bf16[2,16,8,512]{3,2,1,0:T(8,128)(2,1)} %get-tuple-element.37), channel_id=1, source_target_pairs={{0,6},{1,7},{2,4},{3,5},{4,2},{5,3},{6,0},{7,1},{8,14},{9,15},{10,... | collective-permute-start | bytes 786440 | tf_op jit(solution)/shard_map/ppermute | solution.py:405
  29.8 5.4 %copy-start.1 = (bf16[2,16,8,256]{3,2,1,0:T(8,128)(2,1)}, bf16[2,16,8,256]{3,2,1,0:T(8,128)(2,1)S(1)}, u32[]{:S(2)}) copy-start(bf16[2,16,8,256]{3,2,1,0:T(8,128)(2,1)S(1)} %collective-permute-done.1.refs_4_) | copy-start | bytes 393220
  29.8 13.3 %collective-permute-start.10 = (bf16[2,16,8,256]{3,2,1,0:T(8,128)(2,1)}, bf16[2,16,8,256]{3,2,1,0:T(8,128)(2,1)S(1)}, u32[]{:S(2)}, u32[]{:S(2)}) collective-permute-start(bf16[2,16,8,256]{3,2,1,0:T(8,128)(2,1)} %get-tuple-element.41), channel_id=1, source_target_pairs={{0,12},{1,13},{2,14},{3,15},{4,8},{5,9},{6,10},{7,11},{8,4},{9,5},... | collective-permute-start | bytes 393224 | tf_op jit(solution)/shard_map/ppermute | solution.py:405
  32.5 2.6 %copy-start.3 = (bf16[2,16,8,256]{3,2,1,0:T(8,128)(2,1)}, bf16[2,16,8,256]{3,2,1,0:T(8,128)(2,1)S(1)}, u32[]{:S(2)}) copy-start(bf16[2,16,8,256]{3,2,1,0:T(8,128)(2,1)S(1)} %collective-permute-done.2.refs_5_) | copy-start | bytes 393220
  32.5 12.8 %collective-permute-start.11 = (bf16[2,16,8,256]{3,2,1,0:T(8,128)(2,1)}, bf16[2,16,8,256]{3,2,1,0:T(8,128)(2,1)}, u32[]{:S(2)}, u32[]{:S(2)}) collective-permute-start(bf16[2,16,8,256]{3,2,1,0:T(8,128)(2,1)} %get-tuple-element.42), channel_id=1, source_target_pairs={{0,14},{1,15},{2,12},{3,13},{4,10},{5,11},{6,8},{7,9},{8,6},{9,7},... | collective-permute-start | bytes 393224 | tf_op jit(solution)/shard_map/ppermute | solution.py:405
  43.1 24.5 %collective-permute-start.3 = (bf16[2,16,8,256]{3,2,1,0:T(8,128)(2,1)}, bf16[2,16,8,256]{3,2,1,0:T(8,128)(2,1)S(1)}, u32[]{:S(2)}, u32[]{:S(2)}) collective-permute-start(bf16[2,16,8,256]{3,2,1,0:T(8,128)(2,1)} %get-tuple-element.30), channel_id=1, source_target_pairs={{0,8},{1,9},{2,10},{3,11},{4,12},{5,13},{6,14},{7,15},{8,0},{9,1},... | collective-permute-start | bytes 393224 | tf_op jit(solution)/shard_map/ppermute | solution.py:405
  45.3 22.3 %collective-permute-start.4 = (bf16[2,16,8,256]{3,2,1,0:T(8,128)(2,1)}, bf16[2,16,8,256]{3,2,1,0:T(8,128)(2,1)S(1)}, u32[]{:S(2)}, u32[]{:S(2)}) collective-permute-start(bf16[2,16,8,256]{3,2,1,0:T(8,128)(2,1)} %get-tuple-element.31), channel_id=1, source_target_pairs={{0,10},{1,11},{2,8},{3,9},{4,14},{5,15},{6,12},{7,13},{8,2},{9,3},... | collective-permute-start | bytes 393224 | tf_op jit(solution)/shard_map/ppermute | solution.py:405
  45.8 21.8 %collective-permute-start.5 = (bf16[2,16,8,256]{3,2,1,0:T(8,128)(2,1)}, bf16[2,16,8,256]{3,2,1,0:T(8,128)(2,1)S(1)}, u32[]{:S(2)}, u32[]{:S(2)}) collective-permute-start(bf16[2,16,8,256]{3,2,1,0:T(8,128)(2,1)} %get-tuple-element.32), channel_id=1, source_target_pairs={{0,12},{1,13},{2,14},{3,15},{4,8},{5,9},{6,10},{7,11},{8,4},{9,5},... | collective-permute-start | bytes 393224 | tf_op jit(solution)/shard_map/ppermute | solution.py:405
  47.5 20.1 %collective-permute-start.6 = (bf16[2,16,8,256]{3,2,1,0:T(8,128)(2,1)}, bf16[2,16,8,256]{3,2,1,0:T(8,128)(2,1)S(1)}, u32[]{:S(2)}, u32[]{:S(2)}) collective-permute-start(bf16[2,16,8,256]{3,2,1,0:T(8,128)(2,1)} %get-tuple-element.33), channel_id=1, source_target_pairs={{0,14},{1,15},{2,12},{3,13},{4,10},{5,11},{6,8},{7,9},{8,6},{9,7},... | collective-permute-start | bytes 393224 | tf_op jit(solution)/shard_map/ppermute | solution.py:405
  50.8 0.9 %copy-start.2 = (bf16[2,16,8,256]{3,2,1,0:T(8,128)(2,1)S(1)}, bf16[2,16,8,256]{3,2,1,0:T(8,128)(2,1)}, u32[]{:S(2)}) copy-start(bf16[2,16,8,256]{3,2,1,0:T(8,128)(2,1)} %copy-done.1) | copy-start | bytes 393220
  51.8 0.9 %copy-start.4 = (bf16[2,16,8,256]{3,2,1,0:T(8,128)(2,1)S(1)}, bf16[2,16,8,256]{3,2,1,0:T(8,128)(2,1)}, u32[]{:S(2)}) copy-start(bf16[2,16,8,256]{3,2,1,0:T(8,128)(2,1)} %copy-done.3) | copy-start | bytes 393220

commit v5 on v4

--- a/solution.py
+++ b/solution.py
@@ -91,65 +91,47 @@
 
 def gather_kernel(mine_ref, wanted_ref, own_ref, mate_ref, *rest, pieces):
     out_refs = rest[: len(pieces)]
-    held_refs = rest[len(pieces) : -2]
-    load_sem, store_sem = rest[-2:]
-    chips = wanted_ref.shape[0]
-    capacity = out_refs[0].shape[-3] // 2
+    held_ref, load_sem, store_sem = rest[len(pieces) :]
+    chips, _, pages = held_ref.shape[:3]
+    capacity = pages // 2
     whole = pieces[0][0] is None
-    places = range(chips)[::-1]
-
-    def parts_of(x):
-        return [i for i, piece in enumerate(pieces) if whole or piece[0] == x]
-
-    def place_of(i, x, asker, n):
-        held_ref = held_refs[i].at[asker] if whole else held_refs[i]
-        return held_ref.at[:, n]
-
-    def columns(i):
-        _, first, count = pieces[i]
-        return pl.ds(first * HD, count * HD)
-
-    def loads(x, asker):
+
+    def start_loads(x, asker):
         for n in range(capacity):
-            for i in parts_of(x):
-                yield pltpu.make_async_copy(
-                    own_ref.at[wanted_ref[asker, 0, n], :, :, columns(i)],
-                    place_of(i, x, asker, n),
-                    load_sem.at[0 if whole else x],
-                )
-
-    def copy(x, asker):
-        for n in range(capacity, 2 * capacity):
-            page_ref = mate_ref.at[wanted_ref[asker, 0, n]]
-            for i in parts_of(x):
-                place_of(i, x, asker, n)[...] = page_ref[:, :, columns(i)]
+            slot = wanted_ref[asker, 0, n]
+            place = held_ref.at[x, :, n]
+            pltpu.make_async_copy(own_ref.at[slot], place, load_sem.at[x]).start()
+
+    def fill(x, asker):
+        for n in range(capacity, pages):
+            held_ref[x, :, n] = mate_ref[wanted_ref[asker, 0, n]]
+        loaded = held_ref.at[x, :, pl.ds(0, capacity)]
+        pltpu.make_async_copy(loaded, loaded, load_sem.at[x]).wait()
 
     def store(i):
-        return pltpu.make_async_copy(held_refs[i], out_refs[i], store_sem.at[i])
+        x, first, count = pieces[i]
+        held = held_ref if whole else held_ref.at[x]
+        lead = (slice(None),) * (len(held.shape) - 1)
+        held = held.at[lead + (pl.ds(first * HD, count * HD),)]
+        return pltpu.make_async_copy(held, out_refs[i], store_sem.at[i])
 
     if whole:
 
         @pl.loop(0, chips)
         def _(x):
-            for load in loads(None, x):
-                load.start()
-            copy(None, x)
-            for load in loads(None, x):
-                load.wait()
+            start_loads(x, x)
+            fill(x, x)
 
         for i in range(len(pieces)):
             store(i).start()
     else:
-        for x in places:
-            for load in loads(x, mine_ref[0] ^ x):
-                load.start()
-        for x in places:
-            copy(x, mine_ref[0] ^ x)
-            for i in parts_of(x):
-                half = held_refs[i].at[:, pl.ds(0, capacity)]
-                pltpu.make_async_copy(half, half, load_sem.at[x]).wait()
-            for i in parts_of(x):
-                store(i).start()
+        for x in reversed(range(chips)):
+            start_loads(x, mine_ref[0] ^ x)
+        for x in reversed(range(chips)):
+            fill(x, mine_ref[0] ^ x)
+            for i, piece in enumerate(pieces):
+                if piece[0] == x:
+                    store(i).start()
     for i in range(len(pieces)):
         store(i).wait()
 
@@ -170,8 +152,8 @@
             pl.BlockSpec(memory_space=pltpu.VMEM),
         ],
         out_specs=[pl.BlockSpec(memory_space=pltpu.HBM)] * len(pieces),
-        scratch_shapes=[pltpu.VMEM(shape, own.dtype) for shape in shapes]
-        + [
+        scratch_shapes=[
+            pltpu.VMEM((chips, 2, MP // chips) + own.shape[2:], own.dtype),
             pltpu.SemaphoreType.DMA((chips,)),
             pltpu.SemaphoreType.DMA((len(shapes),)),
         ],
@@ -196,13 +178,16 @@
     )(*pieces, *after)
 
 
-def attend_kernel(*refs, first, count, starts, rows, fresh, earlier, last):
+def attend_kernel(*refs, first, count, starts, rows, fresh, earlier, last, fetch):
     filled_ref, live_ref, q_ref, fk_ref, fv_ref = refs[:5]
     piece_refs = refs[5 : 5 + len(starts)]
     rest = refs[5 + len(starts) :]
     if earlier:
         old_ref, old_top_ref, old_sum_ref = rest[:3]
     k_ref, v_ref = rest[-2:]
+    if fetch:
+        raw_ref, raw_sem = rest[-4:-2]
+        rest = rest[:-2]
     if last:
         out_ref, held_ref, sem = rest[-5:-2]
     else:
@@ -233,16 +218,34 @@
             sem.at[h * (GROUP // heads) + g // heads],
         )
 
+    def load(p):
+        piece_ref, start = parts[p]
+        cols = pl.ds((first - start) * HD, count * HD)
+        return pltpu.make_async_copy(
+            piece_ref.at[:, :, cols], raw_ref.at[p], raw_sem.at[p]
+        )
+
+    if fetch:
+        for p in range(len(parts)):
+            load(p).start()
+        for p in range(len(parts)):
+            load(p).wait()
+
+    def part(p, kind, h):
+        if fetch:
+            return raw_ref[p, kind, :, span(h, 1)]
+        piece_ref, start = parts[p]
+        return piece_ref[kind, :, span(first + h - start, 1)]
+
     def one_head(h):
         head = first + h
         base = head * GROUP
         fk = fk_ref[:, span(head, 1)]
-        for p, (piece_ref, start) in enumerate(parts):
+        for p in range(len(parts)):
             at = slice(p * tokens, (p + 1) * tokens)
             live = live_ref[rows * cached + p * tokens : rows * cached + (p + 1) * tokens]
-            col = span(head - start, 1)
-            k_ref[at] = jnp.where(live > 0, piece_ref[0, :, col], fk[:1])
-            v_ref[at, :HD] = jnp.where(live > 0, piece_ref[1, :, col], jnp.zeros_like(live))
+            k_ref[at] = jnp.where(live > 0, part(p, 0, h), fk[:1])
+            v_ref[at, :HD] = jnp.where(live > 0, part(p, 1, h), jnp.zeros_like(live))
             v_ref[at, HD:] = live
         if fresh:
             k_ref[cached:] = fk
@@ -303,26 +306,39 @@
                 store(h, g).wait()
 
 
-def attend(first, count, filled, live, queries, fresh_k, fresh_v, pieces, rows, out=None, earlier=None, fresh=True, last=True):
+def attend(first, count, filled, live, queries, fresh_k, fresh_v, pieces, rows, out=None, earlier=None, fresh=True, last=True, fetch=True):
     width = GROUP * HD
     tokens = sum(
         p.shape[-2] * (p.shape[0] if p.ndim == 4 else 1) for p, start in pieces
     )
-    operands = [filled, live, queries, fresh_k, fresh_v] + [p for p, start in pieces]
+    operands = [filled, live, queries, fresh_k, fresh_v]
+    operands += [
+        pltpu.with_memory_space_constraint(p, pltpu.HBM) if fetch else p
+        for p, start in pieces
+    ]
     if earlier is not None:
         operands += earlier
     inside = pl.BlockSpec(memory_space=pltpu.VMEM)
+    outside = pl.BlockSpec(memory_space=pltpu.HBM)
     in_specs = [pl.BlockSpec(memory_space=pltpu.SMEM)] + [inside] * (len(operands) - 1)
+    if fetch:
+        in_specs[5 : 5 + len(pieces)] = [outside] * len(pieces)
     aliases = {}
     if out is not None:
         operands.append(out)
         in_specs.append(pl.BlockSpec(memory_space=pl.ANY))
         aliases = {len(operands) - 1: 0}
     keys = tokens + (C if fresh else 0)
+    each = pieces[0][0].shape[-2]
     scratch_shapes = [
         pltpu.VMEM((keys, HD), jnp.bfloat16),
         pltpu.VMEM((keys, 2 * HD), jnp.bfloat16),
     ]
+    if fetch:
+        scratch_shapes = [
+            pltpu.VMEM((tokens // each, 2, each, count * HD), jnp.bfloat16),
+            pltpu.SemaphoreType.DMA((tokens // each,)),
+        ] + scratch_shapes
     if last:
         out_shape = pltpu.HBM((C, H * HD), jnp.bfloat16)
         out_specs = pl.BlockSpec(memory_space=pltpu.HBM)
@@ -345,6 +361,7 @@
             fresh=fresh,
             earlier=earlier is not None,
             last=last,
+            fetch=fetch,
         ),
         out_shape=out_shape,
         in_specs=in_specs,
@@ -422,7 +439,7 @@
         else:
             earlier = attend_some(first, count, close, 0, last=False)
             out = attend_some(
-                first, count, pieces, 1, out, earlier=earlier, fresh=False
+                first, count, pieces, 1, out, earlier=earlier, fresh=False, fetch=False
             )
     return out[None]
 

time: 72.6 us -> 71 us (0.978)
  local copies, waits for them, and re-layouts: 4.04 us -> 0.42 us
  waiting for transfers between devices: 19.3 us -> 21.1 us
    ppermute x11, waiting for transfers between devices: 12.9 us -> 14.8 us  [swap(): return lax.ppermute(piece, 'dp', [(i, i ^ 2 * x) for i in range(devices)])]
    unnamed x14 -> x10, local copies, waits for them, and re-layouts: 1.82 us -> 0.02 us
    squeeze x1, local copies, waits for them, and re-layouts: 1.07 us -> 0.04 us  [local(): fresh_k, fresh_v = (fresh_kv[0, :, 0], fresh_kv[0, :, 1])]
    slice x1, local copies, waits for them, and re-layouts: 1.15 us -> 0.37 us  [local(): fresh_k, fresh_v = (fresh_kv[0, :, 0], fresh_kv[0, :, 1])]
  transfers between devices with their start and end apart: 13 -> 13, of which waited for: 5 -> 5; matrix products, arithmetic and copies ran while one was open for 3% -> 1% of each run, Pallas kernels for 24% -> 25%
where the time goes in v5:
time: 71 us; the launch traced here: 70.7 us
  Pallas kernels  25.4 us (36%)
  starting transfers between devices  22.3 us (31%)
  waiting for transfers between devices  21.1 us (30%)
  between operations  1.42 us (2%)
    pallas_call x3, Pallas kernels, attend(): pl.pallas_call(functools.partial(attend_kernel, first=first, count=count,...  19.9 us
    ppermute x11, starting transfers between devices, swap(): return lax.ppermute(piece, 'dp', [(i, i ^ 2 * x) for i in range(devices)])  15 us
    ppermute x11, waiting for transfers between devices, swap(): return lax.ppermute(piece, 'dp', [(i, i ^ 2 * x) for i in range(devices)])  14.8 us
    all_to_all x1, starting transfers between devices, local(): wanted = exchange(asked)  6.8 us
    all_to_all x1, waiting for transfers between devices, local(): wanted = exchange(asked)  6.39 us
    pallas_call x1, Pallas kernels, gather_pages(): pl.pallas_call(functools.partial(gather_kernel, pieces=tuple(pieces)), ou...  2.93 us
    pallas_call x1, Pallas kernels, ask(): pl.pallas_call(ask_kernel, out_shape=jax.ShapeDtypeStruct((chips, 1, MP),...  1.62 us
  transfers between devices with their start and end apart: 13, of which 5 were waited for; matrix products, arithmetic and copies ran while one was open for 1% of the time, Pallas kernels for 25%

profile of v5, /device:TPU:0, one launch (start us, length us, event | category | flops | bytes accessed | tf_op | source)
XLA Modules:
  0.0 70.7 jit_solution(10640093372207815890)
XLA Ops:
  0.0 0.5 collective-permute-start
  0.5 1.6 %ask.1 = s32[8,1,128]{2,1,0:T(1,128)} custom-call(s32[1]{0:T(128)} %bitcast.order_ref.me_ref, s32[1,128]{1,0:T(1,128)} %holder_ref.3, s32[1,128]{1,0:T(1,128)} %slot_ref.1), custom_call_target="tpu_custom_call" | custom-call | tf_op jit(solution)/shard_map/ask/pallas_call | solution.py:48
  2.1 6.8 %all-to-all-start = ((s32[8,1,128]{2,1,0:T(1,128)}), s32[8,1,128]{2,1,0:T(1,128)S(1)}, u32[]{:S(2)}, u32[]{:S(2)}) async-start(s32[8,1,128]{2,1,0:T(1,128)} %ask.1), calls=%async_computation | async-start | bytes 8192 | tf_op jit(solution)/shard_map/all_to_all | solution.py:397
  8.9 6.4 %all-to-all-done.wanted_ref = s32[8,1,128]{2,1,0:T(1,128)S(1)} async-done(((s32[8,1,128]{2,1,0:T(1,128)}), s32[8,1,128]{2,1,0:T(1,128)S(1)}, u32[]{:S(2)}, u32[]{:S(2)}) %all-to-all-start) | async-done | bytes 4128 | tf_op jit(solution)/shard_map/all_to_all | solution.py:397
  15.3 0.0 collective-permute-done.mate_ref
  15.3 0.0 copy-start.1
  15.3 2.9 %gather_pages.1 = (bf16[2,16,8,512]{3,2,1,0:T(8,128)(2,1)}, bf16[2,16,8,512]{3,2,1,0:T(8,128)(2,1)}, bf16[2,16,8,512]{3,2,1,0:T(8,128)(2,1)}, bf16[2,16,8,512]{3...) custom-call(s32[1]{0:T(128)} %bitcast.4.mine_ref, ...), custom_call_target="tpu_custom_call" | custom-call | bytes 4194304 | tf_op jit(solution)/shard_map/gather_pages/pallas_call | solution.py:145
  18.2 0.0 copy-start
  18.2 0.6 collective-permute-start.1
  18.8 2.4 %collective-permute-start.2 = (bf16[2,16,8,256]{3,2,1,0:T(8,128)(2,1)}, bf16[2,16,8,256]{3,2,1,0:T(8,128)(2,1)S(1)}, u32[]{:S(2)}, u32[]{:S(2)}) collective-permute-start(bf16[2,16,8,256]{3,2,1,0:T(8,128)(2,1)} %get-tuple-element.29), channel_id=1, source_target_pairs={{0,10},{1,11},{2,8},{3,9},{4,14},{5,15},{6,12},{7,13},{8,2},{9,3},... | collective-permute-start | bytes 393224 | tf_op jit(solution)/shard_map/ppermute | solution.py:422
  21.2 1.5 %collective-permute-start.7 = (bf16[2,16,8,512]{3,2,1,0:T(8,128)(2,1)}, bf16[2,16,8,512]{3,2,1,0:T(8,128)(2,1)}, u32[]{:S(2)}, u32[]{:S(2)}) collective-permute-start(bf16[2,16,8,512]{3,2,1,0:T(8,128)(2,1)} %get-tuple-element.35), channel_id=1, source_target_pairs={{0,2},{1,3},{2,0},{3,1},{4,6},{5,7},{6,4},{7,5},{8,10},{9,11},{10,... | collective-permute-start | bytes 786440 | tf_op jit(solution)/shard_map/ppermute | solution.py:422
  22.7 0.5 collective-permute-start.8
  23.2 1.5 %collective-permute-start.9 = (bf16[2,16,8,512]{3,2,1,0:T(8,128)(2,1)}, bf16[2,16,8,512]{3,2,1,0:T(8,128)(2,1)}, u32[]{:S(2)}, u32[]{:S(2)}) collective-permute-start(bf16[2,16,8,512]{3,2,1,0:T(8,128)(2,1)} %get-tuple-element.37), channel_id=1, source_target_pairs={{0,6},{1,7},{2,4},{3,5},{4,2},{5,3},{6,0},{7,1},{8,14},{9,15},{10,... | collective-permute-start | bytes 786440 | tf_op jit(solution)/shard_map/ppermute | solution.py:422
  24.7 0.0 copy-done.1
  24.7 0.4 fusion
  26.4 1.0 %live_tokens.1.refs_1_ = bf16[1024,128]{1,0:T(8,128)(2,1)S(1)} custom-call(s32[1]{0:T(128)} %bitcast.order_ref.me_ref, s32[1]{0:T(128)S(6)} %copy.24.length_ref, s32[1,128]{1,0:T(1,128)} %holder_ref.3), custom_call_target="tpu_custom_call" | custom-call | tf_op jit(solution)/shard_map/live_tokens/pallas_call | solution.py:79
  27.4 2.3 %collective-permute-done.1.refs_4_ = bf16[2,16,8,256]{3,2,1,0:T(8,128)(2,1)S(1)} collective-permute-done((bf16[2,16,8,256]{3,2,1,0:T(8,128)(2,1)}, bf16[2,16,8,256]{3,2,1,0:T(8,128)(2,1)S(1)}, u32[]{:S(2)}, u32[]{:S(2)}) %collective-permute-start.1) | collective-permute-done | bytes 131104 | tf_op jit(solution)/shard_map/ppermute | solution.py:422
  29.7 0.0 copy-start.2
  29.7 1.5 %collective-permute-start.10 = (bf16[2,16,8,256]{3,2,1,0:T(8,128)(2,1)}, bf16[2,16,8,256]{3,2,1,0:T(8,128)(2,1)S(1)}, u32[]{:S(2)}, u32[]{:S(2)}) collective-permute-start(bf16[2,16,8,256]{3,2,1,0:T(8,128)(2,1)} %get-tuple-element.41), channel_id=1, source_target_pairs={{0,12},{1,13},{2,14},{3,15},{4,8},{5,9},{6,10},{7,11},{8,4},{9,5},... | collective-permute-start | bytes 393224 | tf_op jit(solution)/shard_map/ppermute | solution.py:422
  31.2 1.2 %collective-permute-done.2.refs_5_ = bf16[2,16,8,256]{3,2,1,0:T(8,128)(2,1)S(1)} collective-permute-done((bf16[2,16,8,256]{3,2,1,0:T(8,128)(2,1)}, bf16[2,16,8,256]{3,2,1,0:T(8,128)(2,1)S(1)}, u32[]{:S(2)}, u32[]{:S(2)}) %collective-permute-start.2) | collective-permute-done | bytes 131104 | tf_op jit(solution)/shard_map/ppermute | solution.py:422
  32.5 0.0 copy-start.3
  32.5 1.5 %collective-permute-start.11 = (bf16[2,16,8,256]{3,2,1,0:T(8,128)(2,1)}, bf16[2,16,8,256]{3,2,1,0:T(8,128)(2,1)}, u32[]{:S(2)}, u32[]{:S(2)}) collective-permute-start(bf16[2,16,8,256]{3,2,1,0:T(8,128)(2,1)} %get-tuple-element.42), channel_id=1, source_target_pairs={{0,14},{1,15},{2,12},{3,13},{4,10},{5,11},{6,8},{7,9},{8,6},{9,7},... | collective-permute-start | bytes 393224 | tf_op jit(solution)/shard_map/ppermute | solution.py:422
  34.0 0.0 copy-done.2
  34.0 0.0 copy-done.3
  34.0 9.0 %collective-permute-done.10 = bf16[2,16,8,256]{3,2,1,0:T(8,128)(2,1)S(1)} collective-permute-done((bf16[2,16,8,256]{3,2,1,0:T(8,128)(2,1)}, bf16[2,16,8,256]{3,2,1,0:T(8,128)(2,1)S(1)}, u32[]{:S(2)}, u32[]{:S(2)}) %collective-permute-start.10) | collective-permute-done | bytes 131104 | tf_op jit(solution)/shard_map/ppermute | solution.py:422
  43.0 0.0 copy-start.4
  43.0 0.0 collective-permute-start.3
  43.0 2.2 %collective-permute-done.11 = bf16[2,16,8,256]{3,2,1,0:T(8,128)(2,1)} collective-permute-done((bf16[2,16,8,256]{3,2,1,0:T(8,128)(2,1)}, bf16[2,16,8,256]{3,2,1,0:T(8,128)(2,1)}, u32[]{:S(2)}, u32[]{:S(2)}) %collective-permute-start.11) | collective-permute-done | bytes 131104 | tf_op jit(solution)/shard_map/ppermute | solution.py:422
  45.2 0.5 collective-permute-start.4
  45.7 0.0 collective-permute-done.7
  45.7 1.8 %collective-permute-start.5 = (bf16[2,16,8,256]{3,2,1,0:T(8,128)(2,1)}, bf16[2,16,8,256]{3,2,1,0:T(8,128)(2,1)S(1)}, u32[]{:S(2)}, u32[]{:S(2)}) collective-permute-start(bf16[2,16,8,256]{3,2,1,0:T(8,128)(2,1)} %get-tuple-element.32), channel_id=1, source_target_pairs={{0,12},{1,13},{2,14},{3,15},{4,8},{5,9},{6,10},{7,11},{8,4},{9,5},... | collective-permute-start | bytes 393224 | tf_op jit(solution)/shard_map/ppermute | solution.py:422
  47.5 0.0 collective-permute-done.8
  47.5 3.3 %collective-permute-start.6 = (bf16[2,16,8,256]{3,2,1,0:T(8,128)(2,1)}, bf16[2,16,8,256]{3,2,1,0:T(8,128)(2,1)S(1)}, u32[]{:S(2)}, u32[]{:S(2)}) collective-permute-start(bf16[2,16,8,256]{3,2,1,0:T(8,128)(2,1)} %get-tuple-element.33), channel_id=1, source_target_pairs={{0,14},{1,15},{2,12},{3,13},{4,10},{5,11},{6,8},{7,9},{8,6},{9,7},... | collective-permute-start | bytes 393224 | tf_op jit(solution)/shard_map/ppermute | solution.py:422
  50.7 0.0 collective-permute-done.9
  50.7 0.0 copy-done.4
  50.8 0.0 copy-done
  50.8 9.4 %attend_0_0.1.refs_12_ = bf16[128,8192]{1,0:T(8,128)(2,1)} custom-call(s32[1]{0:T(128)S(6)} %copy.25.refs_0_, bf16[1024,128]{1,0:T(8,128)(2,1)S(1)} %live_tokens.1.refs_1_, bf16[128,8192]{1,0:T(8,128)(2,1)S(1)} %bitcast.20, bf16[128,512]{1,0:T(8,128)(2,1)S(1)} %get-tuple-element.46.refs_3_, bf16[128,512]{1,0:T(8,128)(2,1)S(1)} %get-tuple-element.45.refs_4_, ...), custom_call_target="tpu_custom_call" | custom-call | flops 2415919104 | bytes 4194304 | tf_op jit(solution)/shard_map/attend_0_0/pallas_call | solution.py:354
  60.2 5.8 %attend_2_0.1 = (f32[128,4096]{1,0:T(8,128)S(1)}, f32[128,4096]{1,0:T(8,128)S(1)}, f32[128,4096]{1,0:T(8,128)S(1)}) custom-call(s32[1]{0:T(128)S(6)} %copy.25.refs_0_, bf16[1024,128]{1,0:T(8,128)(2,1)S(1)} %live_tokens.1.refs_1_, bf16[128,8192]{1,0:T(8,128)(2,1)S(1)} %bitcast.21, bf16[128,512]{1,0:T(8,128)(2,1)S(1)} %get-tuple-element.46.refs_3_, ...), custom_call_target="tpu_custom_call" | custom-call | flops 1342177280 | bytes 4194304 | tf_op jit(solution)/shard_map/attend_2_0/pallas_call | solution.py:354
  66.0 0.0 collective-permute-done.3
  66.0 0.0 collective-permute-done.4
  66.0 0.0 collective-permute-done.5
  66.0 0.0 collective-permute-done.6
  66.0 4.6 %attend_2_1.1 = bf16[128,8192]{1,0:T(8,128)(2,1)} custom-call(s32[1]{0:T(128)S(6)} %copy.25.refs_0_, bf16[1024,128]{1,0:T(8,128)(2,1)S(1)} %live_tokens.1.refs_1_, bf16[128,8192]{1,0:T(8,128)(2,1)S(1)} %bitcast.22, bf16[128,512]{1,0:T(8,128)(2,1)S(1)} %get-tuple-element.46.refs_3_, ...), custom_call_target="tpu_custom_call", output_to_operand_aliasing={{}: (12, {})} | custom-call | flops 1073741824 | bytes 4194304 | tf_op jit(solution)/shard_map/attend_2_1/pallas_call | solution.py:354
  (2 shorter events, 0.0 us)
Async XLA Ops:
  0.0 15.3 %collective-permute-start = (bf16[128,2,8,512]{3,2,1,0:T(8,128)(2,1)}, bf16[128,2,8,512]{3,2,1,0:T(8,128)(2,1)S(1)}, u32[]{:S(2)}, u32[]{:S(2)}) collective-permute-start(bf16[128,2,8,512]{3,2,1,0:T(8,128)(2,1)} %own_ref.1), channel_id=1, source_target_pairs={{0,1},{1,0},{2,3},{3,2},{4,5},{5,4},{6,7},{7,6},{8,9},{9,8},{10,11... | collective-permute-start | bytes 6291464 | tf_op jit(solution)/shard_map/ppermute | solution.py:387
  2.1 13.2 %all-to-all-start = ((s32[8,1,128]{2,1,0:T(1,128)}), s32[8,1,128]{2,1,0:T(1,128)S(1)}, u32[]{:S(2)}, u32[]{:S(2)}) async-start(s32[8,1,128]{2,1,0:T(1,128)} %ask.1), calls=%async_computation | async-start | bytes 8192 | tf_op jit(solution)/shard_map/all_to_all | solution.py:397
  15.3 9.4 %copy-start.1 = (bf16[1,128,2,512]{3,2,1,0:T(2,128)(2,1)S(1)}, bf16[1,128,2,512]{3,2,1,0:T(2,128)(2,1)}, u32[]{:S(2)}) copy-start(bf16[1,128,2,512]{3,2,1,0:T(2,128)(2,1)} %param.8) | copy-start | bytes 786436
  18.2 32.5 %copy-start = (bf16[1,128,8192]{2,1,0:T(8,128)(2,1)S(1)}, bf16[1,128,8192]{2,1,0:T(8,128)(2,1)}, u32[]{:S(2)}) copy-start(bf16[1,128,8192]{2,1,0:T(8,128)(2,1)} %param.7) | copy-start | bytes 6291460
  18.2 11.4 %collective-permute-start.1 = (bf16[2,16,8,256]{3,2,1,0:T(8,128)(2,1)}, bf16[2,16,8,256]{3,2,1,0:T(8,128)(2,1)S(1)}, u32[]{:S(2)}, u32[]{:S(2)}) collective-permute-start(bf16[2,16,8,256]{3,2,1,0:T(8,128)(2,1)} %get-tuple-element.28), channel_id=1, source_target_pairs={{0,8},{1,9},{2,10},{3,11},{4,12},{5,13},{6,14},{7,15},{8,0},{9,1},... | collective-permute-start | bytes 393224 | tf_op jit(solution)/shard_map/ppermute | solution.py:422
  18.8 13.6 %collective-permute-start.2 = (bf16[2,16,8,256]{3,2,1,0:T(8,128)(2,1)}, bf16[2,16,8,256]{3,2,1,0:T(8,128)(2,1)S(1)}, u32[]{:S(2)}, u32[]{:S(2)}) collective-permute-start(bf16[2,16,8,256]{3,2,1,0:T(8,128)(2,1)} %get-tuple-element.29), channel_id=1, source_target_pairs={{0,10},{1,11},{2,8},{3,9},{4,14},{5,15},{6,12},{7,13},{8,2},{9,3},... | collective-permute-start | bytes 393224 | tf_op jit(solution)/shard_map/ppermute | solution.py:422
  21.2 24.5 %collective-permute-start.7 = (bf16[2,16,8,512]{3,2,1,0:T(8,128)(2,1)}, bf16[2,16,8,512]{3,2,1,0:T(8,128)(2,1)}, u32[]{:S(2)}, u32[]{:S(2)}) collective-permute-start(bf16[2,16,8,512]{3,2,1,0:T(8,128)(2,1)} %get-tuple-element.35), channel_id=1, source_target_pairs={{0,2},{1,3},{2,0},{3,1},{4,6},{5,7},{6,4},{7,5},{8,10},{9,11},{10,... | collective-permute-start | bytes 786440 | tf_op jit(solution)/shard_map/ppermute | solution.py:422
  22.7 24.8 %collective-permute-start.8 = (bf16[2,16,8,512]{3,2,1,0:T(8,128)(2,1)}, bf16[2,16,8,512]{3,2,1,0:T(8,128)(2,1)}, u32[]{:S(2)}, u32[]{:S(2)}) collective-permute-start(bf16[2,16,8,512]{3,2,1,0:T(8,128)(2,1)} %get-tuple-element.36), channel_id=1, source_target_pairs={{0,4},{1,5},{2,6},{3,7},{4,0},{5,1},{6,2},{7,3},{8,12},{9,13},{10,... | collective-permute-start | bytes 786440 | tf_op jit(solution)/shard_map/ppermute | solution.py:422
  23.2 27.5 %collective-permute-start.9 = (bf16[2,16,8,512]{3,2,1,0:T(8,128)(2,1)}, bf16[2,16,8,512]{3,2,1,0:T(8,128)(2,1)}, u32[]{:S(2)}, u32[]{:S(2)}) collective-permute-start(bf16[2,16,8,512]{3,2,1,0:T(8,128)(2,1)} %get-tuple-element.37), channel_id=1, source_target_pairs={{0,6},{1,7},{2,4},{3,5},{4,2},{5,3},{6,0},{7,1},{8,14},{9,15},{10,... | collective-permute-start | bytes 786440 | tf_op jit(solution)/shard_map/ppermute | solution.py:422
  29.7 4.3 %copy-start.2 = (bf16[2,16,8,256]{3,2,1,0:T(8,128)(2,1)}, bf16[2,16,8,256]{3,2,1,0:T(8,128)(2,1)S(1)}, u32[]{:S(2)}) copy-start(bf16[2,16,8,256]{3,2,1,0:T(8,128)(2,1)S(1)} %collective-permute-done.1.refs_4_) | copy-start | bytes 393220
  29.7 13.3 %collective-permute-start.10 = (bf16[2,16,8,256]{3,2,1,0:T(8,128)(2,1)}, bf16[2,16,8,256]{3,2,1,0:T(8,128)(2,1)S(1)}, u32[]{:S(2)}, u32[]{:S(2)}) collective-permute-start(bf16[2,16,8,256]{3,2,1,0:T(8,128)(2,1)} %get-tuple-element.41), channel_id=1, source_target_pairs={{0,12},{1,13},{2,14},{3,15},{4,8},{5,9},{6,10},{7,11},{8,4},{9,5},... | collective-permute-start | bytes 393224 | tf_op jit(solution)/shard_map/ppermute | solution.py:422
  32.5 1.6 %copy-start.3 = (bf16[2,16,8,256]{3,2,1,0:T(8,128)(2,1)}, bf16[2,16,8,256]{3,2,1,0:T(8,128)(2,1)S(1)}, u32[]{:S(2)}) copy-start(bf16[2,16,8,256]{3,2,1,0:T(8,128)(2,1)S(1)} %collective-permute-done.2.refs_5_) | copy-start | bytes 393220
  32.5 12.8 %collective-permute-start.11 = (bf16[2,16,8,256]{3,2,1,0:T(8,128)(2,1)}, bf16[2,16,8,256]{3,2,1,0:T(8,128)(2,1)}, u32[]{:S(2)}, u32[]{:S(2)}) collective-permute-start(bf16[2,16,8,256]{3,2,1,0:T(8,128)(2,1)} %get-tuple-element.42), channel_id=1, source_target_pairs={{0,14},{1,15},{2,12},{3,13},{4,10},{5,11},{6,8},{7,9},{8,6},{9,7},... | collective-permute-start | bytes 393224 | tf_op jit(solution)/shard_map/ppermute | solution.py:422
  43.0 7.7 %copy-start.4 = (bf16[2,16,8,256]{3,2,1,0:T(8,128)(2,1)}, bf16[2,16,8,256]{3,2,1,0:T(8,128)(2,1)S(1)}, u32[]{:S(2)}) copy-start(bf16[2,16,8,256]{3,2,1,0:T(8,128)(2,1)S(1)} %collective-permute-done.10) | copy-start | bytes 393220
  43.0 23.0 %collective-permute-start.3 = (bf16[2,16,8,256]{3,2,1,0:T(8,128)(2,1)}, bf16[2,16,8,256]{3,2,1,0:T(8,128)(2,1)S(1)}, u32[]{:S(2)}, u32[]{:S(2)}) collective-permute-start(bf16[2,16,8,256]{3,2,1,0:T(8,128)(2,1)} %get-tuple-element.30), channel_id=1, source_target_pairs={{0,8},{1,9},{2,10},{3,11},{4,12},{5,13},{6,14},{7,15},{8,0},{9,1},... | collective-permute-start | bytes 393224 | tf_op jit(solution)/shard_map/ppermute | solution.py:422
  45.2 20.8 %collective-permute-start.4 = (bf16[2,16,8,256]{3,2,1,0:T(8,128)(2,1)}, bf16[2,16,8,256]{3,2,1,0:T(8,128)(2,1)S(1)}, u32[]{:S(2)}, u32[]{:S(2)}) collective-permute-start(bf16[2,16,8,256]{3,2,1,0:T(8,128)(2,1)} %get-tuple-element.31), channel_id=1, source_target_pairs={{0,10},{1,11},{2,8},{3,9},{4,14},{5,15},{6,12},{7,13},{8,2},{9,3},... | collective-permute-start | bytes 393224 | tf_op jit(solution)/shard_map/ppermute | solution.py:422
  45.7 20.3 %collective-permute-start.5 = (bf16[2,16,8,256]{3,2,1,0:T(8,128)(2,1)}, bf16[2,16,8,256]{3,2,1,0:T(8,128)(2,1)S(1)}, u32[]{:S(2)}, u32[]{:S(2)}) collective-permute-start(bf16[2,16,8,256]{3,2,1,0:T(8,128)(2,1)} %get-tuple-element.32), channel_id=1, source_target_pairs={{0,12},{1,13},{2,14},{3,15},{4,8},{5,9},{6,10},{7,11},{8,4},{9,5},... | collective-permute-start | bytes 393224 | tf_op jit(solution)/shard_map/ppermute | solution.py:422
  47.5 18.6 %collective-permute-start.6 = (bf16[2,16,8,256]{3,2,1,0:T(8,128)(2,1)}, bf16[2,16,8,256]{3,2,1,0:T(8,128)(2,1)S(1)}, u32[]{:S(2)}, u32[]{:S(2)}) collective-permute-start(bf16[2,16,8,256]{3,2,1,0:T(8,128)(2,1)} %get-tuple-element.33), channel_id=1, source_target_pairs={{0,14},{1,15},{2,12},{3,13},{4,10},{5,11},{6,8},{7,9},{8,6},{9,7},... | collective-permute-start | bytes 393224 | tf_op jit(solution)/shard_map/ppermute | solution.py:422

commit v6 on v5

--- a/solution.py
+++ b/solution.py
@@ -142,16 +142,20 @@
     for x, _, count in pieces:
         shape = (2, MP // chips, PAGE, count * HD)
         shapes.append((chips,) + shape if x is None else shape)
+    spaces = [
+        pltpu.VMEM if x is not None and (0 < x < chips // 2 or (first == 0 and 0 <= x - chips // 2 < 2)) else pltpu.HBM
+        for x, first, _ in pieces
+    ]
     return pl.pallas_call(
         functools.partial(gather_kernel, pieces=tuple(pieces)),
-        out_shape=[pltpu.HBM(shape, own.dtype) for shape in shapes],
+        out_shape=[space(shape, own.dtype) for space, shape in zip(spaces, shapes)],
         in_specs=[
             pl.BlockSpec(memory_space=pltpu.SMEM),
             pl.BlockSpec(memory_space=pltpu.SMEM),
             pl.BlockSpec(memory_space=pltpu.HBM),
             pl.BlockSpec(memory_space=pltpu.VMEM),
         ],
-        out_specs=[pl.BlockSpec(memory_space=pltpu.HBM)] * len(pieces),
+        out_specs=[pl.BlockSpec(memory_space=space) for space in spaces],
         scratch_shapes=[
             pltpu.VMEM((chips, 2, MP // chips) + own.shape[2:], own.dtype),
             pltpu.SemaphoreType.DMA((chips,)),
@@ -209,7 +213,7 @@
     filled = token < filled_ref[0]
 
     def span(start, size):
-        return pl.ds(pl.multiple_of(start * HD, HD), size * HD)
+        return pl.ds(start * HD, size * HD)
 
     def store(h, g):
         return pltpu.make_async_copy(
@@ -228,8 +232,6 @@
     if fetch:
         for p in range(len(parts)):
             load(p).start()
-        for p in range(len(parts)):
-            load(p).wait()
 
     def part(p, kind, h):
         if fetch:
@@ -243,6 +245,8 @@
         fk = fk_ref[:, span(head, 1)]
         for p in range(len(parts)):
             at = slice(p * tokens, (p + 1) * tokens)
+            if fetch and h == 0:
+                load(p).wait()
             live = live_ref[rows * cached + p * tokens : rows * cached + (p + 1) * tokens]
             k_ref[at] = jnp.where(live > 0, part(p, 0, h), fk[:1])
             v_ref[at, :HD] = jnp.where(live > 0, part(p, 1, h), jnp.zeros_like(live))
@@ -296,10 +300,8 @@
             if last:
                 store(h, g).start()
 
-    if count == 1:
-        one_head(0)
-    else:
-        pl.loop(0, count)(one_head)
+    for h in range(count):
+        one_head(h)
     if last:
         for h in range(count):
             for g in range(0, GROUP, heads):

time: 71 us -> 69 us (0.972)
  waiting for transfers between devices: 21.1 us -> 19.1 us
  Pallas kernels: 25.4 us -> 23.5 us
  local copies, waits for them, and re-layouts: 0.42 us -> 2.23 us
    ppermute x11, waiting for transfers between devices: 14.8 us -> 12.7 us  [swap(): return lax.ppermute(piece, 'dp', [(i, i ^ 2 * x) for i in range(devices)])]
    pallas_call x3, Pallas kernels: 19.9 us -> 18.2 us  [attend(): pl.pallas_call(functools.partial(attend_kernel, first=first, count=count,...]
    squeeze x1, local copies, waits for them, and re-layouts: 0.04 us -> 1.07 us  [local(): fresh_k, fresh_v = (fresh_kv[0, :, 0], fresh_kv[0, :, 1])]
    slice x1, local copies, waits for them, and re-layouts: 0.37 us -> 1.15 us  [local(): fresh_k, fresh_v = (fresh_kv[0, :, 0], fresh_kv[0, :, 1])]
  transfers between devices with their start and end apart: 13 -> 13, of which waited for: 5 -> 5; matrix products, arithmetic and copies ran while one was open for 1% -> 3% of each run, Pallas kernels for 25% -> 24%
where the time goes in v6:
time: 69 us; the launch traced here: 68.7 us
  Pallas kernels  23.5 us (34%)
  starting transfers between devices  22.4 us (32%)
  waiting for transfers between devices  19.1 us (28%)
  local copies, waits for them, and re-layouts  2.23 us (3%)
  between operations  1.56 us (2%)
    pallas_call x3, Pallas kernels, attend(): pl.pallas_call(functools.partial(attend_kernel, first=first, count=count,...  18.2 us
    ppermute x11, starting transfers between devices, swap(): return lax.ppermute(piece, 'dp', [(i, i ^ 2 * x) for i in range(devices)])  15.1 us
    ppermute x11, waiting for transfers between devices, swap(): return lax.ppermute(piece, 'dp', [(i, i ^ 2 * x) for i in range(devices)])  12.7 us
    all_to_all x1, starting transfers between devices, local(): wanted = exchange(asked)  6.8 us
    all_to_all x1, waiting for transfers between devices, local(): wanted = exchange(asked)  6.39 us
    pallas_call x1, Pallas kernels, gather_pages(): pl.pallas_call(functools.partial(gather_kernel, pieces=tuple(pieces)), ou...  2.67 us
    pallas_call x1, Pallas kernels, ask(): pl.pallas_call(ask_kernel, out_shape=jax.ShapeDtypeStruct((chips, 1, MP),...  1.62 us
  transfers between devices with their start and end apart: 13, of which 5 were waited for; matrix products, arithmetic and copies ran while one was open for 3% of the time, Pallas kernels for 24%

profile of v6, /device:TPU:0, one launch (start us, length us, event | category | flops | bytes accessed | tf_op | source)
XLA Modules:
  0.0 68.7 jit_solution(1834408739314041352)
XLA Ops:
  0.0 0.5 collective-permute-start
  0.5 1.6 %ask.1 = s32[8,1,128]{2,1,0:T(1,128)} custom-call(s32[1]{0:T(128)} %bitcast.order_ref.me_ref, s32[1,128]{1,0:T(1,128)} %holder_ref.3, s32[1,128]{1,0:T(1,128)} %slot_ref.1), custom_call_target="tpu_custom_call" | custom-call | tf_op jit(solution)/shard_map/ask/pallas_call | solution.py:48
  2.1 6.8 %all-to-all-start = ((s32[8,1,128]{2,1,0:T(1,128)}), s32[8,1,128]{2,1,0:T(1,128)S(1)}, u32[]{:S(2)}, u32[]{:S(2)}) async-start(s32[8,1,128]{2,1,0:T(1,128)} %ask.1), calls=%async_computation | async-start | bytes 8192 | tf_op jit(solution)/shard_map/all_to_all | solution.py:399
  8.9 6.4 %all-to-all-done.wanted_ref = s32[8,1,128]{2,1,0:T(1,128)S(1)} async-done(((s32[8,1,128]{2,1,0:T(1,128)}), s32[8,1,128]{2,1,0:T(1,128)S(1)}, u32[]{:S(2)}, u32[]{:S(2)}) %all-to-all-start) | async-done | bytes 4128 | tf_op jit(solution)/shard_map/all_to_all | solution.py:399
  15.3 0.0 collective-permute-done.mate_ref
  15.3 0.0 copy-start.1
  15.3 2.7 %gather_pages.1 = (bf16[2,16,8,512]{3,2,1,0:T(8,128)(2,1)}, bf16[2,16,8,512]{3,2,1,0:T(8,128)(2,1)S(1)}, bf16[2,16,8,512]{3,2,1,0:T(8,128)(2,1)S(1)}, bf16[2,16,...) custom-call(s32[1]{0:T(128)} %bitcast.4.mine_ref, ...), custom_call_target="tpu_custom_call" | custom-call | bytes 4194304 | tf_op jit(solution)/shard_map/gather_pages/pallas_call | solution.py:149
  18.0 0.0 copy-start
  18.0 0.6 collective-permute-start.1
  18.6 2.4 %collective-permute-start.2 = (bf16[2,16,8,256]{3,2,1,0:T(8,128)(2,1)S(1)}, bf16[2,16,8,256]{3,2,1,0:T(8,128)(2,1)}, u32[]{:S(2)}, u32[]{:S(2)}) collective-permute-start(bf16[2,16,8,256]{3,2,1,0:T(8,128)(2,1)S(1)} %get-tuple-element.29), channel_id=1, source_target_pairs={{0,10},{1,11},{2,8},{3,9},{4,14},{5,15},{6,12},{7,13},{8,2},{9,3},... | collective-permute-start | bytes 393224 | tf_op jit(solution)/shard_map/ppermute | solution.py:424
  20.9 1.5 %collective-permute-start.7 = (bf16[2,16,8,512]{3,2,1,0:T(8,128)(2,1)S(1)}, bf16[2,16,8,512]{3,2,1,0:T(8,128)(2,1)}, u32[]{:S(2)}, u32[]{:S(2)}) collective-permute-start(bf16[2,16,8,512]{3,2,1,0:T(8,128)(2,1)S(1)} %get-tuple-element.35), channel_id=1, source_target_pairs={{0,2},{1,3},{2,0},{3,1},{4,6},{5,7},{6,4},{7,5},{8,10},{9,11},{10,... | collective-permute-start | bytes 786440 | tf_op jit(solution)/shard_map/ppermute | solution.py:424
  22.4 0.5 collective-permute-start.8
  23.0 1.5 %collective-permute-start.9 = (bf16[2,16,8,512]{3,2,1,0:T(8,128)(2,1)S(1)}, bf16[2,16,8,512]{3,2,1,0:T(8,128)(2,1)}, u32[]{:S(2)}, u32[]{:S(2)}) collective-permute-start(bf16[2,16,8,512]{3,2,1,0:T(8,128)(2,1)S(1)} %get-tuple-element.37), channel_id=1, source_target_pairs={{0,6},{1,7},{2,4},{3,5},{4,2},{5,3},{6,0},{7,1},{8,14},{9,15},{10,... | collective-permute-start | bytes 786440 | tf_op jit(solution)/shard_map/ppermute | solution.py:424
  24.4 0.0 copy-done.1
  24.4 1.2 %fusion = (bf16[1,128,1,512]{3,2,1,0:T(2,128)(2,1)}, bf16[1,128,1,512]{3,2,1,0:T(2,128)(2,1)}) fusion(bf16[1,128,2,512]{3,2,1,0:T(2,128)(2,1)S(1)} %copy-done.1), kind=kLoop, calls=%fused_computation.2 | loop fusion | bytes 524288 | tf_op jit(solution)/shard_map/slice | solution.py:406
  26.9 1.0 %live_tokens.1.refs_1_ = bf16[1024,128]{1,0:T(8,128)(2,1)S(1)} custom-call(s32[1]{0:T(128)} %bitcast.order_ref.me_ref, s32[1]{0:T(128)S(6)} %copy.24.length_ref, s32[1,128]{1,0:T(1,128)} %holder_ref.3), custom_call_target="tpu_custom_call" | custom-call | tf_op jit(solution)/shard_map/live_tokens/pallas_call | solution.py:79
  27.9 1.3 %collective-permute-done.1.refs_4_ = bf16[2,16,8,256]{3,2,1,0:T(8,128)(2,1)S(1)} collective-permute-done((bf16[2,16,8,256]{3,2,1,0:T(8,128)(2,1)S(1)}, bf16[2,16,8,256]{3,2,1,0:T(8,128)(2,1)S(1)}, u32[]{:S(2)}, u32[]{:S(2)}) %collective-permute-start.1) | collective-permute-done | bytes 131104 | tf_op jit(solution)/shard_map/ppermute | solution.py:424
  29.2 0.0 copy-start.2
  29.2 1.5 %collective-permute-start.10 = (bf16[2,16,8,256]{3,2,1,0:T(8,128)(2,1)}, bf16[2,16,8,256]{3,2,1,0:T(8,128)(2,1)}, u32[]{:S(2)}, u32[]{:S(2)}) collective-permute-start(bf16[2,16,8,256]{3,2,1,0:T(8,128)(2,1)} %get-tuple-element.41), channel_id=1, source_target_pairs={{0,12},{1,13},{2,14},{3,15},{4,8},{5,9},{6,10},{7,11},{8,4},{9,5},... | collective-permute-start | bytes 393224 | tf_op jit(solution)/shard_map/ppermute | solution.py:424
  30.7 1.3 %collective-permute-done.2.refs_5_ = bf16[2,16,8,256]{3,2,1,0:T(8,128)(2,1)} collective-permute-done((bf16[2,16,8,256]{3,2,1,0:T(8,128)(2,1)S(1)}, bf16[2,16,8,256]{3,2,1,0:T(8,128)(2,1)}, u32[]{:S(2)}, u32[]{:S(2)}) %collective-permute-start.2) | collective-permute-done | bytes 131104 | tf_op jit(solution)/shard_map/ppermute | solution.py:424
  32.1 1.6 %collective-permute-start.11 = (bf16[2,16,8,256]{3,2,1,0:T(8,128)(2,1)}, bf16[2,16,8,256]{3,2,1,0:T(8,128)(2,1)}, u32[]{:S(2)}, u32[]{:S(2)}) collective-permute-start(bf16[2,16,8,256]{3,2,1,0:T(8,128)(2,1)} %get-tuple-element.42), channel_id=1, source_target_pairs={{0,14},{1,15},{2,12},{3,13},{4,10},{5,11},{6,8},{7,9},{8,6},{9,7},... | collective-permute-start | bytes 393224 | tf_op jit(solution)/shard_map/ppermute | solution.py:424
  33.7 1.1 %copy_bitcast_fusion = (bf16[128,512]{1,0:T(8,128)(2,1)S(1)}, bf16[128,512]{1,0:T(8,128)(2,1)S(1)}) fusion(bf16[1,128,1,512]{3,2,1,0:T(2,128)(2,1)} %get-tuple-element.43, bf16[1,128,1,512]{3,2,1,0:T(2,128)(2,1)} %get-tuple-element.44), kind=kLoop, calls=%fused_computation | loop fusion | bytes 524288 | tf_op jit(solution)/shard_map/squeeze | solution.py:406
  34.8 0.0 copy-done.2
  34.8 7.8 %collective-permute-done.10 = bf16[2,16,8,256]{3,2,1,0:T(8,128)(2,1)} collective-permute-done((bf16[2,16,8,256]{3,2,1,0:T(8,128)(2,1)}, bf16[2,16,8,256]{3,2,1,0:T(8,128)(2,1)}, u32[]{:S(2)}, u32[]{:S(2)}) %collective-permute-start.10) | collective-permute-done | bytes 131104 | tf_op jit(solution)/shard_map/ppermute | solution.py:424
  42.6 0.0 collective-permute-start.3
  42.6 2.2 %collective-permute-done.11 = bf16[2,16,8,256]{3,2,1,0:T(8,128)(2,1)} collective-permute-done((bf16[2,16,8,256]{3,2,1,0:T(8,128)(2,1)}, bf16[2,16,8,256]{3,2,1,0:T(8,128)(2,1)}, u32[]{:S(2)}, u32[]{:S(2)}) %collective-permute-start.11) | collective-permute-done | bytes 131104 | tf_op jit(solution)/shard_map/ppermute | solution.py:424
  44.8 0.4 collective-permute-start.4
  45.1 0.0 collective-permute-done.7
  45.1 2.0 %collective-permute-start.5 = (bf16[2,16,8,256]{3,2,1,0:T(8,128)(2,1)}, bf16[2,16,8,256]{3,2,1,0:T(8,128)(2,1)S(1)}, u32[]{:S(2)}, u32[]{:S(2)}) collective-permute-start(bf16[2,16,8,256]{3,2,1,0:T(8,128)(2,1)} %get-tuple-element.32), channel_id=1, source_target_pairs={{0,12},{1,13},{2,14},{3,15},{4,8},{5,9},{6,10},{7,11},{8,4},{9,5},... | collective-permute-start | bytes 393224 | tf_op jit(solution)/shard_map/ppermute | solution.py:424
  47.1 0.0 collective-permute-done.8
  47.1 3.1 %collective-permute-start.6 = (bf16[2,16,8,256]{3,2,1,0:T(8,128)(2,1)}, bf16[2,16,8,256]{3,2,1,0:T(8,128)(2,1)S(1)}, u32[]{:S(2)}, u32[]{:S(2)}) collective-permute-start(bf16[2,16,8,256]{3,2,1,0:T(8,128)(2,1)} %get-tuple-element.33), channel_id=1, source_target_pairs={{0,14},{1,15},{2,12},{3,13},{4,10},{5,11},{6,8},{7,9},{8,6},{9,7},... | collective-permute-start | bytes 393224 | tf_op jit(solution)/shard_map/ppermute | solution.py:424
  50.3 0.0 collective-permute-done.9
  50.3 0.0 copy-done
  50.3 8.7 %attend_0_0.1.refs_12_ = bf16[128,8192]{1,0:T(8,128)(2,1)} custom-call(s32[1]{0:T(128)S(6)} %copy.25.refs_0_, bf16[1024,128]{1,0:T(8,128)(2,1)S(1)} %live_tokens.1.refs_1_, bf16[128,8192]{1,0:T(8,128)(2,1)S(1)} %bitcast.20, bf16[128,512]{1,0:T(8,128)(2,1)S(1)} %get-tuple-element.46.refs_3_, bf16[128,512]{1,0:T(8,128)(2,1)S(1)} %get-tuple-element.45.refs_4_, ...), custom_call_target="tpu_custom_call" | custom-call | flops 2415919104 | bytes 4194304 | tf_op jit(solution)/shard_map/attend_0_0/pallas_call | solution.py:356
  59.0 5.3 %attend_2_0.1 = (f32[128,4096]{1,0:T(8,128)S(1)}, f32[128,4096]{1,0:T(8,128)S(1)}, f32[128,4096]{1,0:T(8,128)S(1)}) custom-call(s32[1]{0:T(128)S(6)} %copy.25.refs_0_, bf16[1024,128]{1,0:T(8,128)(2,1)S(1)} %live_tokens.1.refs_1_, bf16[128,8192]{1,0:T(8,128)(2,1)S(1)} %bitcast.21, bf16[128,512]{1,0:T(8,128)(2,1)S(1)} %get-tuple-element.46.refs_3_, ...), custom_call_target="tpu_custom_call" | custom-call | flops 1342177280 | bytes 4194304 | tf_op jit(solution)/shard_map/attend_2_0/pallas_call | solution.py:356
  64.3 0.0 collective-permute-done.3
  64.3 0.0 collective-permute-done.4
  64.3 0.0 collective-permute-done.5
  64.4 0.0 collective-permute-done.6
  64.4 4.2 %attend_2_1.1 = bf16[128,8192]{1,0:T(8,128)(2,1)} custom-call(s32[1]{0:T(128)S(6)} %copy.25.refs_0_, bf16[1024,128]{1,0:T(8,128)(2,1)S(1)} %live_tokens.1.refs_1_, bf16[128,8192]{1,0:T(8,128)(2,1)S(1)} %bitcast.22, bf16[128,512]{1,0:T(8,128)(2,1)S(1)} %get-tuple-element.46.refs_3_, ...), custom_call_target="tpu_custom_call", output_to_operand_aliasing={{}: (12, {})} | custom-call | flops 1073741824 | bytes 4194304 | tf_op jit(solution)/shard_map/attend_2_1/pallas_call | solution.py:356
  (1 shorter events, 0.0 us)
Async XLA Ops:
  0.0 15.3 %collective-permute-start = (bf16[128,2,8,512]{3,2,1,0:T(8,128)(2,1)}, bf16[128,2,8,512]{3,2,1,0:T(8,128)(2,1)S(1)}, u32[]{:S(2)}, u32[]{:S(2)}) collective-permute-start(bf16[128,2,8,512]{3,2,1,0:T(8,128)(2,1)} %own_ref.1), channel_id=1, source_target_pairs={{0,1},{1,0},{2,3},{3,2},{4,5},{5,4},{6,7},{7,6},{8,9},{9,8},{10,11... | collective-permute-start | bytes 6291464 | tf_op jit(solution)/shard_map/ppermute | solution.py:389
  2.1 13.2 %all-to-all-start = ((s32[8,1,128]{2,1,0:T(1,128)}), s32[8,1,128]{2,1,0:T(1,128)S(1)}, u32[]{:S(2)}, u32[]{:S(2)}) async-start(s32[8,1,128]{2,1,0:T(1,128)} %ask.1), calls=%async_computation | async-start | bytes 8192 | tf_op jit(solution)/shard_map/all_to_all | solution.py:399
  15.3 9.2 %copy-start.1 = (bf16[1,128,2,512]{3,2,1,0:T(2,128)(2,1)S(1)}, bf16[1,128,2,512]{3,2,1,0:T(2,128)(2,1)}, u32[]{:S(2)}) copy-start(bf16[1,128,2,512]{3,2,1,0:T(2,128)(2,1)} %param.8) | copy-start | bytes 786436
  18.0 32.3 %copy-start = (bf16[1,128,8192]{2,1,0:T(8,128)(2,1)S(1)}, bf16[1,128,8192]{2,1,0:T(8,128)(2,1)}, u32[]{:S(2)}) copy-start(bf16[1,128,8192]{2,1,0:T(8,128)(2,1)} %param.7) | copy-start | bytes 6291460
  18.0 11.2 %collective-permute-start.1 = (bf16[2,16,8,256]{3,2,1,0:T(8,128)(2,1)S(1)}, bf16[2,16,8,256]{3,2,1,0:T(8,128)(2,1)S(1)}, u32[]{:S(2)}, u32[]{:S(2)}) collective-permute-start(bf16[2,16,8,256]{3,2,1,0:T(8,128)(2,1)S(1)} %get-tuple-element.28), channel_id=1, source_target_pairs={{0,8},{1,9},{2,10},{3,11},{4,12},{5,13},{6,14},{7,15},{8,0},{9,1},... | collective-permute-start | bytes 393224 | tf_op jit(solution)/shard_map/ppermute | solution.py:424
  18.6 13.5 %collective-permute-start.2 = (bf16[2,16,8,256]{3,2,1,0:T(8,128)(2,1)S(1)}, bf16[2,16,8,256]{3,2,1,0:T(8,128)(2,1)}, u32[]{:S(2)}, u32[]{:S(2)}) collective-permute-start(bf16[2,16,8,256]{3,2,1,0:T(8,128)(2,1)S(1)} %get-tuple-element.29), channel_id=1, source_target_pairs={{0,10},{1,11},{2,8},{3,9},{4,14},{5,15},{6,12},{7,13},{8,2},{9,3},... | collective-permute-start | bytes 393224 | tf_op jit(solution)/shard_map/ppermute | solution.py:424
  20.9 24.2 %collective-permute-start.7 = (bf16[2,16,8,512]{3,2,1,0:T(8,128)(2,1)S(1)}, bf16[2,16,8,512]{3,2,1,0:T(8,128)(2,1)}, u32[]{:S(2)}, u32[]{:S(2)}) collective-permute-start(bf16[2,16,8,512]{3,2,1,0:T(8,128)(2,1)S(1)} %get-tuple-element.35), channel_id=1, source_target_pairs={{0,2},{1,3},{2,0},{3,1},{4,6},{5,7},{6,4},{7,5},{8,10},{9,11},{10,... | collective-permute-start | bytes 786440 | tf_op jit(solution)/shard_map/ppermute | solution.py:424
  22.4 24.7 %collective-permute-start.8 = (bf16[2,16,8,512]{3,2,1,0:T(8,128)(2,1)S(1)}, bf16[2,16,8,512]{3,2,1,0:T(8,128)(2,1)}, u32[]{:S(2)}, u32[]{:S(2)}) collective-permute-start(bf16[2,16,8,512]{3,2,1,0:T(8,128)(2,1)S(1)} %get-tuple-element.36), channel_id=1, source_target_pairs={{0,4},{1,5},{2,6},{3,7},{4,0},{5,1},{6,2},{7,3},{8,12},{9,13},{10,... | collective-permute-start | bytes 786440 | tf_op jit(solution)/shard_map/ppermute | solution.py:424
  23.0 27.3 %collective-permute-start.9 = (bf16[2,16,8,512]{3,2,1,0:T(8,128)(2,1)S(1)}, bf16[2,16,8,512]{3,2,1,0:T(8,128)(2,1)}, u32[]{:S(2)}, u32[]{:S(2)}) collective-permute-start(bf16[2,16,8,512]{3,2,1,0:T(8,128)(2,1)S(1)} %get-tuple-element.37), channel_id=1, source_target_pairs={{0,6},{1,7},{2,4},{3,5},{4,2},{5,3},{6,0},{7,1},{8,14},{9,15},{10,... | collective-permute-start | bytes 786440 | tf_op jit(solution)/shard_map/ppermute | solution.py:424
  29.2 5.6 %copy-start.2 = (bf16[2,16,8,256]{3,2,1,0:T(8,128)(2,1)}, bf16[2,16,8,256]{3,2,1,0:T(8,128)(2,1)S(1)}, u32[]{:S(2)}) copy-start(bf16[2,16,8,256]{3,2,1,0:T(8,128)(2,1)S(1)} %collective-permute-done.1.refs_4_) | copy-start | bytes 393220
  29.2 13.4 %collective-permute-start.10 = (bf16[2,16,8,256]{3,2,1,0:T(8,128)(2,1)}, bf16[2,16,8,256]{3,2,1,0:T(8,128)(2,1)}, u32[]{:S(2)}, u32[]{:S(2)}) collective-permute-start(bf16[2,16,8,256]{3,2,1,0:T(8,128)(2,1)} %get-tuple-element.41), channel_id=1, source_target_pairs={{0,12},{1,13},{2,14},{3,15},{4,8},{5,9},{6,10},{7,11},{8,4},{9,5},... | collective-permute-start | bytes 393224 | tf_op jit(solution)/shard_map/ppermute | solution.py:424
  32.1 12.7 %collective-permute-start.11 = (bf16[2,16,8,256]{3,2,1,0:T(8,128)(2,1)}, bf16[2,16,8,256]{3,2,1,0:T(8,128)(2,1)}, u32[]{:S(2)}, u32[]{:S(2)}) collective-permute-start(bf16[2,16,8,256]{3,2,1,0:T(8,128)(2,1)} %get-tuple-element.42), channel_id=1, source_target_pairs={{0,14},{1,15},{2,12},{3,13},{4,10},{5,11},{6,8},{7,9},{8,6},{9,7},... | collective-permute-start | bytes 393224 | tf_op jit(solution)/shard_map/ppermute | solution.py:424
  42.6 21.7 %collective-permute-start.3 = (bf16[2,16,8,256]{3,2,1,0:T(8,128)(2,1)}, bf16[2,16,8,256]{3,2,1,0:T(8,128)(2,1)S(1)}, u32[]{:S(2)}, u32[]{:S(2)}) collective-permute-start(bf16[2,16,8,256]{3,2,1,0:T(8,128)(2,1)} %get-tuple-element.30), channel_id=1, source_target_pairs={{0,8},{1,9},{2,10},{3,11},{4,12},{5,13},{6,14},{7,15},{8,0},{9,1},... | collective-permute-start | bytes 393224 | tf_op jit(solution)/shard_map/ppermute | solution.py:424
  44.8 19.5 %collective-permute-start.4 = (bf16[2,16,8,256]{3,2,1,0:T(8,128)(2,1)}, bf16[2,16,8,256]{3,2,1,0:T(8,128)(2,1)S(1)}, u32[]{:S(2)}, u32[]{:S(2)}) collective-permute-start(bf16[2,16,8,256]{3,2,1,0:T(8,128)(2,1)} %get-tuple-element.31), channel_id=1, source_target_pairs={{0,10},{1,11},{2,8},{3,9},{4,14},{5,15},{6,12},{7,13},{8,2},{9,3},... | collective-permute-start | bytes 393224 | tf_op jit(solution)/shard_map/ppermute | solution.py:424
  45.1 19.2 %collective-permute-start.5 = (bf16[2,16,8,256]{3,2,1,0:T(8,128)(2,1)}, bf16[2,16,8,256]{3,2,1,0:T(8,128)(2,1)S(1)}, u32[]{:S(2)}, u32[]{:S(2)}) collective-permute-start(bf16[2,16,8,256]{3,2,1,0:T(8,128)(2,1)} %get-tuple-element.32), channel_id=1, source_target_pairs={{0,12},{1,13},{2,14},{3,15},{4,8},{5,9},{6,10},{7,11},{8,4},{9,5},... | collective-permute-start | bytes 393224 | tf_op jit(solution)/shard_map/ppermute | solution.py:424
  47.1 17.2 %collective-permute-start.6 = (bf16[2,16,8,256]{3,2,1,0:T(8,128)(2,1)}, bf16[2,16,8,256]{3,2,1,0:T(8,128)(2,1)S(1)}, u32[]{:S(2)}, u32[]{:S(2)}) collective-permute-start(bf16[2,16,8,256]{3,2,1,0:T(8,128)(2,1)} %get-tuple-element.33), channel_id=1, source_target_pairs={{0,14},{1,15},{2,12},{3,13},{4,10},{5,11},{6,8},{7,9},{8,6},{9,7},... | collective-permute-start | bytes 393224 | tf_op jit(solution)/shard_map/ppermute | solution.py:424

commit v7 on v6

--- a/solution.py
+++ b/solution.py
@@ -433,7 +433,7 @@
     for c, (first, count) in enumerate(CHUNKS):
         batch = sent[len(near) + c * len(far) : len(near) + (c + 1) * len(far)]
         if c > 0:
-            batch = hold_back(batch, arrived[:2])
+            batch = hold_back(batch, arrived[:1])
         arrived = [swap(piece, x) for piece, x in zip(batch, far)]
         pieces = [(piece, first) for piece in arrived]
         if c < len(CHUNKS) - 1:

time: 69 us -> 69 us (level)
  no operation moved by 1% of the time
where the time goes in v7:
time: 69 us; the launch traced here: 68.7 us
  Pallas kernels  23.5 us (34%)
  starting transfers between devices  22.4 us (32%)
  waiting for transfers between devices  19.1 us (28%)
  local copies, waits for them, and re-layouts  2.23 us (3%)
  between operations  1.56 us (2%)
    pallas_call x3, Pallas kernels, attend(): pl.pallas_call(functools.partial(attend_kernel, first=first, count=count,...  18.2 us
    ppermute x11, starting transfers between devices, swap(): return lax.ppermute(piece, 'dp', [(i, i ^ 2 * x) for i in range(devices)])  15.1 us
    ppermute x11, waiting for transfers between devices, swap(): return lax.ppermute(piece, 'dp', [(i, i ^ 2 * x) for i in range(devices)])  12.7 us
    all_to_all x1, starting transfers between devices, local(): wanted = exchange(asked)  6.8 us
    all_to_all x1, waiting for transfers between devices, local(): wanted = exchange(asked)  6.39 us
    pallas_call x1, Pallas kernels, gather_pages(): pl.pallas_call(functools.partial(gather_kernel, pieces=tuple(pieces)), ou...  2.67 us
    pallas_call x1, Pallas kernels, ask(): pl.pallas_call(ask_kernel, out_shape=jax.ShapeDtypeStruct((chips, 1, MP),...  1.62 us
  transfers between devices with their start and end apart: 13, of which 5 were waited for; matrix products, arithmetic and copies ran while one was open for 3% of the time, Pallas kernels for 24%

profile of v7, /device:TPU:0, one launch (start us, length us, event | category | flops | bytes accessed | tf_op | source)
XLA Modules:
  0.0 68.7 jit_solution(8052567534075218836)
XLA Ops:
  0.0 0.5 collective-permute-start
  0.5 1.6 %ask.1 = s32[8,1,128]{2,1,0:T(1,128)} custom-call(s32[1]{0:T(128)} %bitcast.order_ref.me_ref, s32[1,128]{1,0:T(1,128)} %holder_ref.3, s32[1,128]{1,0:T(1,128)} %slot_ref.1), custom_call_target="tpu_custom_call" | custom-call | tf_op jit(solution)/shard_map/ask/pallas_call | solution.py:48
  2.1 6.8 %all-to-all-start = ((s32[8,1,128]{2,1,0:T(1,128)}), s32[8,1,128]{2,1,0:T(1,128)S(1)}, u32[]{:S(2)}, u32[]{:S(2)}) async-start(s32[8,1,128]{2,1,0:T(1,128)} %ask.1), calls=%async_computation | async-start | bytes 8192 | tf_op jit(solution)/shard_map/all_to_all | solution.py:399
  8.9 6.4 %all-to-all-done.wanted_ref = s32[8,1,128]{2,1,0:T(1,128)S(1)} async-done(((s32[8,1,128]{2,1,0:T(1,128)}), s32[8,1,128]{2,1,0:T(1,128)S(1)}, u32[]{:S(2)}, u32[]{:S(2)}) %all-to-all-start) | async-done | bytes 4128 | tf_op jit(solution)/shard_map/all_to_all | solution.py:399
  15.3 0.0 collective-permute-done.mate_ref
  15.3 0.0 copy-start.1
  15.3 2.7 %gather_pages.1 = (bf16[2,16,8,512]{3,2,1,0:T(8,128)(2,1)}, bf16[2,16,8,512]{3,2,1,0:T(8,128)(2,1)S(1)}, bf16[2,16,8,512]{3,2,1,0:T(8,128)(2,1)S(1)}, bf16[2,16,...) custom-call(s32[1]{0:T(128)} %bitcast.4.mine_ref, ...), custom_call_target="tpu_custom_call" | custom-call | bytes 4194304 | tf_op jit(solution)/shard_map/gather_pages/pallas_call | solution.py:149
  18.0 0.0 copy-start
  18.0 0.6 collective-permute-start.1
  18.6 2.4 %collective-permute-start.9 = (bf16[2,16,8,256]{3,2,1,0:T(8,128)(2,1)S(1)}, bf16[2,16,8,256]{3,2,1,0:T(8,128)(2,1)}, u32[]{:S(2)}, u32[]{:S(2)}) collective-permute-start(bf16[2,16,8,256]{3,2,1,0:T(8,128)(2,1)S(1)} %get-tuple-element.40), channel_id=1, source_target_pairs={{0,10},{1,11},{2,8},{3,9},{4,14},{5,15},{6,12},{7,13},{8,2},{9,3},... | collective-permute-start | bytes 393224 | tf_op jit(solution)/shard_map/ppermute | solution.py:424
  20.9 1.5 %collective-permute-start.6 = (bf16[2,16,8,512]{3,2,1,0:T(8,128)(2,1)S(1)}, bf16[2,16,8,512]{3,2,1,0:T(8,128)(2,1)}, u32[]{:S(2)}, u32[]{:S(2)}) collective-permute-start(bf16[2,16,8,512]{3,2,1,0:T(8,128)(2,1)S(1)} %get-tuple-element.34), channel_id=1, source_target_pairs={{0,2},{1,3},{2,0},{3,1},{4,6},{5,7},{6,4},{7,5},{8,10},{9,11},{10,... | collective-permute-start | bytes 786440 | tf_op jit(solution)/shard_map/ppermute | solution.py:424
  22.4 0.5 collective-permute-start.7
  23.0 1.5 %collective-permute-start.8 = (bf16[2,16,8,512]{3,2,1,0:T(8,128)(2,1)S(1)}, bf16[2,16,8,512]{3,2,1,0:T(8,128)(2,1)}, u32[]{:S(2)}, u32[]{:S(2)}) collective-permute-start(bf16[2,16,8,512]{3,2,1,0:T(8,128)(2,1)S(1)} %get-tuple-element.36), channel_id=1, source_target_pairs={{0,6},{1,7},{2,4},{3,5},{4,2},{5,3},{6,0},{7,1},{8,14},{9,15},{10,... | collective-permute-start | bytes 786440 | tf_op jit(solution)/shard_map/ppermute | solution.py:424
  24.4 0.0 copy-done.1
  24.4 1.2 %fusion = (bf16[1,128,1,512]{3,2,1,0:T(2,128)(2,1)}, bf16[1,128,1,512]{3,2,1,0:T(2,128)(2,1)}) fusion(bf16[1,128,2,512]{3,2,1,0:T(2,128)(2,1)S(1)} %copy-done.1), kind=kLoop, calls=%fused_computation.2 | loop fusion | bytes 524288 | tf_op jit(solution)/shard_map/slice | solution.py:406
  26.9 1.0 %live_tokens.1.refs_1_ = bf16[1024,128]{1,0:T(8,128)(2,1)S(1)} custom-call(s32[1]{0:T(128)} %bitcast.order_ref.me_ref, s32[1]{0:T(128)S(6)} %copy.24.length_ref, s32[1,128]{1,0:T(1,128)} %holder_ref.3), custom_call_target="tpu_custom_call" | custom-call | tf_op jit(solution)/shard_map/live_tokens/pallas_call | solution.py:79
  27.9 1.3 %collective-permute-done.1.refs_4_ = bf16[2,16,8,256]{3,2,1,0:T(8,128)(2,1)S(1)} collective-permute-done((bf16[2,16,8,256]{3,2,1,0:T(8,128)(2,1)S(1)}, bf16[2,16,8,256]{3,2,1,0:T(8,128)(2,1)S(1)}, u32[]{:S(2)}, u32[]{:S(2)}) %collective-permute-start.1) | collective-permute-done | bytes 131104 | tf_op jit(solution)/shard_map/ppermute | solution.py:424
  29.2 0.0 copy-start.2
  29.2 1.5 %collective-permute-start.10 = (bf16[2,16,8,256]{3,2,1,0:T(8,128)(2,1)}, bf16[2,16,8,256]{3,2,1,0:T(8,128)(2,1)}, u32[]{:S(2)}, u32[]{:S(2)}) collective-permute-start(bf16[2,16,8,256]{3,2,1,0:T(8,128)(2,1)} %get-tuple-element.41), channel_id=1, source_target_pairs={{0,12},{1,13},{2,14},{3,15},{4,8},{5,9},{6,10},{7,11},{8,4},{9,5},... | collective-permute-start | bytes 393224 | tf_op jit(solution)/shard_map/ppermute | solution.py:424
  30.7 1.3 %collective-permute-done.9 = bf16[2,16,8,256]{3,2,1,0:T(8,128)(2,1)} collective-permute-done((bf16[2,16,8,256]{3,2,1,0:T(8,128)(2,1)S(1)}, bf16[2,16,8,256]{3,2,1,0:T(8,128)(2,1)}, u32[]{:S(2)}, u32[]{:S(2)}) %collective-permute-start.9) | collective-permute-done | bytes 131104 | tf_op jit(solution)/shard_map/ppermute | solution.py:424
  32.1 1.6 %collective-permute-start.11 = (bf16[2,16,8,256]{3,2,1,0:T(8,128)(2,1)}, bf16[2,16,8,256]{3,2,1,0:T(8,128)(2,1)}, u32[]{:S(2)}, u32[]{:S(2)}) collective-permute-start(bf16[2,16,8,256]{3,2,1,0:T(8,128)(2,1)} %get-tuple-element.42), channel_id=1, source_target_pairs={{0,14},{1,15},{2,12},{3,13},{4,10},{5,11},{6,8},{7,9},{8,6},{9,7},... | collective-permute-start | bytes 393224 | tf_op jit(solution)/shard_map/ppermute | solution.py:424
  33.7 1.1 %copy_bitcast_fusion = (bf16[128,512]{1,0:T(8,128)(2,1)S(1)}, bf16[128,512]{1,0:T(8,128)(2,1)S(1)}) fusion(bf16[1,128,1,512]{3,2,1,0:T(2,128)(2,1)} %get-tuple-element.43, bf16[1,128,1,512]{3,2,1,0:T(2,128)(2,1)} %get-tuple-element.44), kind=kLoop, calls=%fused_computation | loop fusion | bytes 524288 | tf_op jit(solution)/shard_map/squeeze | solution.py:406
  34.8 0.0 copy-done.2
  34.8 7.8 %collective-permute-done.10 = bf16[2,16,8,256]{3,2,1,0:T(8,128)(2,1)} collective-permute-done((bf16[2,16,8,256]{3,2,1,0:T(8,128)(2,1)}, bf16[2,16,8,256]{3,2,1,0:T(8,128)(2,1)}, u32[]{:S(2)}, u32[]{:S(2)}) %collective-permute-start.10) | collective-permute-done | bytes 131104 | tf_op jit(solution)/shard_map/ppermute | solution.py:424
  42.6 0.0 collective-permute-start.2
  42.6 2.2 %collective-permute-done.11 = bf16[2,16,8,256]{3,2,1,0:T(8,128)(2,1)} collective-permute-done((bf16[2,16,8,256]{3,2,1,0:T(8,128)(2,1)}, bf16[2,16,8,256]{3,2,1,0:T(8,128)(2,1)}, u32[]{:S(2)}, u32[]{:S(2)}) %collective-permute-start.11) | collective-permute-done | bytes 131104 | tf_op jit(solution)/shard_map/ppermute | solution.py:424
  44.8 0.4 collective-permute-start.3
  45.1 0.0 collective-permute-done.6
  45.1 2.0 %collective-permute-start.4 = (bf16[2,16,8,256]{3,2,1,0:T(8,128)(2,1)}, bf16[2,16,8,256]{3,2,1,0:T(8,128)(2,1)S(1)}, u32[]{:S(2)}, u32[]{:S(2)}) collective-permute-start(bf16[2,16,8,256]{3,2,1,0:T(8,128)(2,1)} %get-tuple-element.31), channel_id=1, source_target_pairs={{0,12},{1,13},{2,14},{3,15},{4,8},{5,9},{6,10},{7,11},{8,4},{9,5},... | collective-permute-start | bytes 393224 | tf_op jit(solution)/shard_map/ppermute | solution.py:424
  47.1 0.0 collective-permute-done.7
  47.1 3.1 %collective-permute-start.5 = (bf16[2,16,8,256]{3,2,1,0:T(8,128)(2,1)}, bf16[2,16,8,256]{3,2,1,0:T(8,128)(2,1)S(1)}, u32[]{:S(2)}, u32[]{:S(2)}) collective-permute-start(bf16[2,16,8,256]{3,2,1,0:T(8,128)(2,1)} %get-tuple-element.32), channel_id=1, source_target_pairs={{0,14},{1,15},{2,12},{3,13},{4,10},{5,11},{6,8},{7,9},{8,6},{9,7},... | collective-permute-start | bytes 393224 | tf_op jit(solution)/shard_map/ppermute | solution.py:424
  50.3 0.0 collective-permute-done.8
  50.3 0.0 copy-done
  50.3 8.7 %attend_0_0.1.refs_12_ = bf16[128,8192]{1,0:T(8,128)(2,1)} custom-call(s32[1]{0:T(128)S(6)} %copy.25.refs_0_, bf16[1024,128]{1,0:T(8,128)(2,1)S(1)} %live_tokens.1.refs_1_, bf16[128,8192]{1,0:T(8,128)(2,1)S(1)} %bitcast.20, bf16[128,512]{1,0:T(8,128)(2,1)S(1)} %get-tuple-element.46.refs_3_, bf16[128,512]{1,0:T(8,128)(2,1)S(1)} %get-tuple-element.45.refs_4_, ...), custom_call_target="tpu_custom_call" | custom-call | flops 2415919104 | bytes 4194304 | tf_op jit(solution)/shard_map/attend_0_0/pallas_call | solution.py:356
  59.0 5.3 %attend_2_0.1 = (f32[128,4096]{1,0:T(8,128)S(1)}, f32[128,4096]{1,0:T(8,128)S(1)}, f32[128,4096]{1,0:T(8,128)S(1)}) custom-call(s32[1]{0:T(128)S(6)} %copy.25.refs_0_, bf16[1024,128]{1,0:T(8,128)(2,1)S(1)} %live_tokens.1.refs_1_, bf16[128,8192]{1,0:T(8,128)(2,1)S(1)} %bitcast.21, bf16[128,512]{1,0:T(8,128)(2,1)S(1)} %get-tuple-element.46.refs_3_, ...), custom_call_target="tpu_custom_call" | custom-call | flops 1342177280 | bytes 4194304 | tf_op jit(solution)/shard_map/attend_2_0/pallas_call | solution.py:356
  64.3 0.0 collective-permute-done.2
  64.3 0.0 collective-permute-done.3
  64.3 0.0 collective-permute-done.4
  64.4 0.0 collective-permute-done.5
  64.4 4.2 %attend_2_1.1 = bf16[128,8192]{1,0:T(8,128)(2,1)} custom-call(s32[1]{0:T(128)S(6)} %copy.25.refs_0_, bf16[1024,128]{1,0:T(8,128)(2,1)S(1)} %live_tokens.1.refs_1_, bf16[128,8192]{1,0:T(8,128)(2,1)S(1)} %bitcast.22, bf16[128,512]{1,0:T(8,128)(2,1)S(1)} %get-tuple-element.46.refs_3_, ...), custom_call_target="tpu_custom_call", output_to_operand_aliasing={{}: (12, {})} | custom-call | flops 1073741824 | bytes 4194304 | tf_op jit(solution)/shard_map/attend_2_1/pallas_call | solution.py:356
  (1 shorter events, 0.0 us)
Async XLA Ops:
  0.0 15.3 %collective-permute-start = (bf16[128,2,8,512]{3,2,1,0:T(8,128)(2,1)}, bf16[128,2,8,512]{3,2,1,0:T(8,128)(2,1)S(1)}, u32[]{:S(2)}, u32[]{:S(2)}) collective-permute-start(bf16[128,2,8,512]{3,2,1,0:T(8,128)(2,1)} %own_ref.1), channel_id=1, source_target_pairs={{0,1},{1,0},{2,3},{3,2},{4,5},{5,4},{6,7},{7,6},{8,9},{9,8},{10,11... | collective-permute-start | bytes 6291464 | tf_op jit(solution)/shard_map/ppermute | solution.py:389
  2.1 13.2 %all-to-all-start = ((s32[8,1,128]{2,1,0:T(1,128)}), s32[8,1,128]{2,1,0:T(1,128)S(1)}, u32[]{:S(2)}, u32[]{:S(2)}) async-start(s32[8,1,128]{2,1,0:T(1,128)} %ask.1), calls=%async_computation | async-start | bytes 8192 | tf_op jit(solution)/shard_map/all_to_all | solution.py:399
  15.3 9.2 %copy-start.1 = (bf16[1,128,2,512]{3,2,1,0:T(2,128)(2,1)S(1)}, bf16[1,128,2,512]{3,2,1,0:T(2,128)(2,1)}, u32[]{:S(2)}) copy-start(bf16[1,128,2,512]{3,2,1,0:T(2,128)(2,1)} %param.8) | copy-start | bytes 786436
  18.0 32.3 %copy-start = (bf16[1,128,8192]{2,1,0:T(8,128)(2,1)S(1)}, bf16[1,128,8192]{2,1,0:T(8,128)(2,1)}, u32[]{:S(2)}) copy-start(bf16[1,128,8192]{2,1,0:T(8,128)(2,1)} %param.7) | copy-start | bytes 6291460
  18.0 11.2 %collective-permute-start.1 = (bf16[2,16,8,256]{3,2,1,0:T(8,128)(2,1)S(1)}, bf16[2,16,8,256]{3,2,1,0:T(8,128)(2,1)S(1)}, u32[]{:S(2)}, u32[]{:S(2)}) collective-permute-start(bf16[2,16,8,256]{3,2,1,0:T(8,128)(2,1)S(1)} %get-tuple-element.28), channel_id=1, source_target_pairs={{0,8},{1,9},{2,10},{3,11},{4,12},{5,13},{6,14},{7,15},{8,0},{9,1},... | collective-permute-start | bytes 393224 | tf_op jit(solution)/shard_map/ppermute | solution.py:424
  18.6 13.5 %collective-permute-start.9 = (bf16[2,16,8,256]{3,2,1,0:T(8,128)(2,1)S(1)}, bf16[2,16,8,256]{3,2,1,0:T(8,128)(2,1)}, u32[]{:S(2)}, u32[]{:S(2)}) collective-permute-start(bf16[2,16,8,256]{3,2,1,0:T(8,128)(2,1)S(1)} %get-tuple-element.40), channel_id=1, source_target_pairs={{0,10},{1,11},{2,8},{3,9},{4,14},{5,15},{6,12},{7,13},{8,2},{9,3},... | collective-permute-start | bytes 393224 | tf_op jit(solution)/shard_map/ppermute | solution.py:424
  20.9 24.2 %collective-permute-start.6 = (bf16[2,16,8,512]{3,2,1,0:T(8,128)(2,1)S(1)}, bf16[2,16,8,512]{3,2,1,0:T(8,128)(2,1)}, u32[]{:S(2)}, u32[]{:S(2)}) collective-permute-start(bf16[2,16,8,512]{3,2,1,0:T(8,128)(2,1)S(1)} %get-tuple-element.34), channel_id=1, source_target_pairs={{0,2},{1,3},{2,0},{3,1},{4,6},{5,7},{6,4},{7,5},{8,10},{9,11},{10,... | collective-permute-start | bytes 786440 | tf_op jit(solution)/shard_map/ppermute | solution.py:424
  22.4 24.7 %collective-permute-start.7 = (bf16[2,16,8,512]{3,2,1,0:T(8,128)(2,1)S(1)}, bf16[2,16,8,512]{3,2,1,0:T(8,128)(2,1)}, u32[]{:S(2)}, u32[]{:S(2)}) collective-permute-start(bf16[2,16,8,512]{3,2,1,0:T(8,128)(2,1)S(1)} %get-tuple-element.35), channel_id=1, source_target_pairs={{0,4},{1,5},{2,6},{3,7},{4,0},{5,1},{6,2},{7,3},{8,12},{9,13},{10,... | collective-permute-start | bytes 786440 | tf_op jit(solution)/shard_map/ppermute | solution.py:424
  23.0 27.3 %collective-permute-start.8 = (bf16[2,16,8,512]{3,2,1,0:T(8,128)(2,1)S(1)}, bf16[2,16,8,512]{3,2,1,0:T(8,128)(2,1)}, u32[]{:S(2)}, u32[]{:S(2)}) collective-permute-start(bf16[2,16,8,512]{3,2,1,0:T(8,128)(2,1)S(1)} %get-tuple-element.36), channel_id=1, source_target_pairs={{0,6},{1,7},{2,4},{3,5},{4,2},{5,3},{6,0},{7,1},{8,14},{9,15},{10,... | collective-permute-start | bytes 786440 | tf_op jit(solution)/shard_map/ppermute | solution.py:424
  29.2 5.6 %copy-start.2 = (bf16[2,16,8,256]{3,2,1,0:T(8,128)(2,1)}, bf16[2,16,8,256]{3,2,1,0:T(8,128)(2,1)S(1)}, u32[]{:S(2)}) copy-start(bf16[2,16,8,256]{3,2,1,0:T(8,128)(2,1)S(1)} %collective-permute-done.1.refs_4_) | copy-start | bytes 393220
  29.2 13.4 %collective-permute-start.10 = (bf16[2,16,8,256]{3,2,1,0:T(8,128)(2,1)}, bf16[2,16,8,256]{3,2,1,0:T(8,128)(2,1)}, u32[]{:S(2)}, u32[]{:S(2)}) collective-permute-start(bf16[2,16,8,256]{3,2,1,0:T(8,128)(2,1)} %get-tuple-element.41), channel_id=1, source_target_pairs={{0,12},{1,13},{2,14},{3,15},{4,8},{5,9},{6,10},{7,11},{8,4},{9,5},... | collective-permute-start | bytes 393224 | tf_op jit(solution)/shard_map/ppermute | solution.py:424
  32.1 12.7 %collective-permute-start.11 = (bf16[2,16,8,256]{3,2,1,0:T(8,128)(2,1)}, bf16[2,16,8,256]{3,2,1,0:T(8,128)(2,1)}, u32[]{:S(2)}, u32[]{:S(2)}) collective-permute-start(bf16[2,16,8,256]{3,2,1,0:T(8,128)(2,1)} %get-tuple-element.42), channel_id=1, source_target_pairs={{0,14},{1,15},{2,12},{3,13},{4,10},{5,11},{6,8},{7,9},{8,6},{9,7},... | collective-permute-start | bytes 393224 | tf_op jit(solution)/shard_map/ppermute | solution.py:424
  42.6 21.7 %collective-permute-start.2 = (bf16[2,16,8,256]{3,2,1,0:T(8,128)(2,1)}, bf16[2,16,8,256]{3,2,1,0:T(8,128)(2,1)S(1)}, u32[]{:S(2)}, u32[]{:S(2)}) collective-permute-start(bf16[2,16,8,256]{3,2,1,0:T(8,128)(2,1)} %get-tuple-element.29), channel_id=1, source_target_pairs={{0,8},{1,9},{2,10},{3,11},{4,12},{5,13},{6,14},{7,15},{8,0},{9,1},... | collective-permute-start | bytes 393224 | tf_op jit(solution)/shard_map/ppermute | solution.py:424
  44.8 19.5 %collective-permute-start.3 = (bf16[2,16,8,256]{3,2,1,0:T(8,128)(2,1)}, bf16[2,16,8,256]{3,2,1,0:T(8,128)(2,1)S(1)}, u32[]{:S(2)}, u32[]{:S(2)}) collective-permute-start(bf16[2,16,8,256]{3,2,1,0:T(8,128)(2,1)} %get-tuple-element.30), channel_id=1, source_target_pairs={{0,10},{1,11},{2,8},{3,9},{4,14},{5,15},{6,12},{7,13},{8,2},{9,3},... | collective-permute-start | bytes 393224 | tf_op jit(solution)/shard_map/ppermute | solution.py:424
  45.1 19.2 %collective-permute-start.4 = (bf16[2,16,8,256]{3,2,1,0:T(8,128)(2,1)}, bf16[2,16,8,256]{3,2,1,0:T(8,128)(2,1)S(1)}, u32[]{:S(2)}, u32[]{:S(2)}) collective-permute-start(bf16[2,16,8,256]{3,2,1,0:T(8,128)(2,1)} %get-tuple-element.31), channel_id=1, source_target_pairs={{0,12},{1,13},{2,14},{3,15},{4,8},{5,9},{6,10},{7,11},{8,4},{9,5},... | collective-permute-start | bytes 393224 | tf_op jit(solution)/shard_map/ppermute | solution.py:424
  47.1 17.2 %collective-permute-start.5 = (bf16[2,16,8,256]{3,2,1,0:T(8,128)(2,1)}, bf16[2,16,8,256]{3,2,1,0:T(8,128)(2,1)S(1)}, u32[]{:S(2)}, u32[]{:S(2)}) collective-permute-start(bf16[2,16,8,256]{3,2,1,0:T(8,128)(2,1)} %get-tuple-element.32), channel_id=1, source_target_pairs={{0,14},{1,15},{2,12},{3,13},{4,10},{5,11},{6,8},{7,9},{8,6},{9,7},... | collective-permute-start | bytes 393224 | tf_op jit(solution)/shard_map/ppermute | solution.py:424
